TPU v7x, 32 devices: a whole 2x2x4 slice. The times are simulated.
32 devices in a mesh: grp: 2 (over y), band: 8 (over z, x), ch: 2 (over core).
Axes of the slice: x: 2, y: 2, z: 4, core: 2. Of those that a mesh axis runs over, the one named last changes fastest.
Arguments:
- grid_input: bfloat16 [32768, 227], P(('grp', 'band')), parts along dimension 0, may hold values from -6 to 6
- grid_senders: int32 [2048, 32], P(('grp', 'band')), parts along dimension 0, may hold values from 0 to 16383, as said below
- grid_lengths: int32 [2048], P(('grp', 'band')), parts along dimension 0, may hold values from 11 to 32, as said below
- grid_feats: bfloat16 [4, 65536], P(None, ('grp', 'band')), parts along dimension 1, may hold values from -6 to 6
- mesh_latent: bfloat16 [2048, 512], P(('grp', 'band'), 'ch'), parts along dimension 0, may hold values from -6 to 6
- mesh_senders: int32 [128, 16], P(('grp', 'band')), parts along dimension 0, may hold values from 0 to 127, as said below
- mesh_receivers: int32 [128, 16], P(('grp', 'band')), parts along dimension 0, may hold values from 0 to 127, as said below
- mesh_counts: int32 [16, 8], P(('grp', 'band')), parts along dimension 0, may hold values from 0 to 16, as said below
- mesh_feats: bfloat16 [4, 2048], P(None, ('grp', 'band')), parts along dimension 1, may hold values from -6 to 6
- embed_first: bfloat16 [227, 512], P(None, 'ch'), may hold values from -0.375 to 0.375
- embed_second: bfloat16 [512, 512], P('ch'), may hold values from -0.25 to 0.25
- link_sender: bfloat16 [512, 512], P(None, 'ch'), may hold values from -0.25 to 0.25
- link_receiver: bfloat16 [512, 512], P(None, 'ch'), may hold values from -0.25 to 0.25
- link_edge: bfloat16 [4, 512], P(None, 'ch'), may hold values from -3 to 3
- link_out: bfloat16 [512, 512], P('ch'), may hold values from -0.046875 to 0.046875
- proc_sender: bfloat16 [512, 512], P(None, 'ch'), may hold values from -0.25 to 0.25
- proc_receiver: bfloat16 [512, 512], P(None, 'ch'), may hold values from -0.25 to 0.25
- proc_edge: bfloat16 [4, 512], P(None, 'ch'), may hold values from -3 to 3
- proc_out: bfloat16 [512, 512], P('ch'), may hold values from -0.25 to 0.25
- node_first: bfloat16 [1024, 512], P(None, 'ch'), may hold values from -0.1875 to 0.1875
- node_second: bfloat16 [512, 512], P('ch'), may hold values from -0.25 to 0.25
- norm_gain: float32 [512], P('ch'), may hold values from 0.4 to 1.6
Outputs:
- mesh_out: bfloat16 [2048, 512], P(('grp', 'band'), 'ch'), parts along dimension 0
There are 2 independent parts, one for each index of `grp`. A program takes and returns all parts, laid end to end along the dimension named above; an argument that names none is the same for every part. Nothing has to cross between parts.
Inputs may be any that keep to these rules, and one draw needn't show every extreme that they name: `grid_senders`: the senders of the mesh nodes of patch b (rows b * 128 to b * 128 + 127) lie in the latitude slabs b - 1, b, b + 1 (grid rows of slab q: q * 2048 to q * 2048 + 2047), within the grid. `grid_lengths`: each patch has at least one mesh node with all 32 slots used. `mesh_counts`: entry (b, p) is 0 unless p is b - 1, b or b + 1 modulo 8 (neighbouring patches) or p < 2 (patches that hold the coarse mesh levels); Each row has at least one block with all 16 slots used, from a neighbouring patch. `mesh_senders`: in a block from a patch p < 2 that is not a neighbour of b, the senders are coarse-level nodes: at most 4 distinct nodes of patch p, the same for every such block from p. `mesh_receivers`: in a block from a patch p < 2 that is not a neighbour of b, the receivers are coarse-level nodes: at most 4 distinct nodes of patch b, the same for every such block into b.
All inputs are finite; a program needn't handle non-finite values.
Results may differ from a plain program's by a relative error of at most 0.007.
Values may be sent and summed in bfloat16 or wider, within the bound.
No kernel may reach another device: no remote copies, remote signals or barrier semaphores. Data moves between devices by JAX's collectives and lax.ppermute only.
A program may use at most 64 MiB of HBM per device.

v0:
```python
import jax
import jax.numpy as jnp
from jax import lax
from jax.sharding import PartitionSpec as P


def with_halo(shard, sides, width):
    for axis, dim in sides:
        peers, length = (lax.axis_size(axis), shard.shape[dim])
        up = [(i, (i + 1) % peers) for i in range(peers - 1)]
        down = [(j, i) for i, j in up]
        last = lax.slice_in_dim(shard, length - width, length, axis=dim)
        leading = lax.slice_in_dim(shard, 0, width, axis=dim)
        before = lax.ppermute(last, axis, up)
        after = lax.ppermute(leading, axis, down)
        shard = jnp.concatenate([before, shard, after], axis=dim)
    return shard


def per_device(
    grid_input,
    grid_senders,
    grid_lengths,
    grid_feats,
    mesh_latent,
    mesh_senders,
    mesh_receivers,
    mesh_counts,
    mesh_feats,
    embed_first,
    embed_second,
    link_sender,
    link_receiver,
    link_edge,
    link_out,
    proc_sender,
    proc_receiver,
    proc_edge,
    proc_out,
    node_first,
    node_second,
    norm_gain,
):
    band_index = lax.axis_index("band")
    band_size = lax.axis_size("band")
    ch_size = lax.axis_size("ch")
    grid_rows = grid_input.shape[0]
    mesh_rows = mesh_latent.shape[0]
    half_width = link_sender.shape[1]
    full_width = half_width * ch_size
    slot_count = grid_senders.shape[1]
    capacity = mesh_senders.shape[1]
    contract_first = (((0,), (0,)), ((), ()))
    embed_hidden = jax.nn.silu(
        jnp.dot(grid_input, embed_first, preferred_element_type=jnp.float32)
    ).astype(jnp.bfloat16)
    partial_latent = jnp.dot(embed_hidden, embed_second, preferred_element_type=jnp.float32)
    own_latent = lax.psum_scatter(
        partial_latent.astype(jnp.bfloat16), "ch", scatter_dimension=1, tiled=True
    )
    grid_latent = lax.all_gather(own_latent, "ch", axis=1, tiled=True)
    grid_send = jnp.dot(grid_latent, link_sender, preferred_element_type=jnp.float32).astype(
        jnp.bfloat16
    )
    slab_table = with_halo(grid_send, (("band", 0),), grid_rows)
    local_index = (grid_senders - (band_index - 1) * grid_rows).reshape(-1)
    sender_rows = (
        jnp.take(slab_table, local_index, axis=0)
        .astype(jnp.float32)
        .reshape(mesh_rows, slot_count, half_width)
    )
    mesh_full = lax.all_gather(mesh_latent, "ch", axis=1, tiled=True)
    receiver_term = jnp.dot(mesh_full, link_receiver, preferred_element_type=jnp.float32)
    edge_term = lax.dot_general(
        grid_feats, link_edge, contract_first, preferred_element_type=jnp.float32
    ).reshape(mesh_rows, slot_count, half_width)
    activity = jax.nn.silu(sender_rows + receiver_term[:, None, :] + edge_term)
    valid = jnp.arange(slot_count, dtype=jnp.int32)[None, :] < grid_lengths[:, None]
    link_pool = jnp.sum(jnp.where(valid[:, :, None], activity, jnp.float32(0.0)), axis=1).astype(
        jnp.bfloat16
    )
    link_agg = lax.psum_scatter(
        jnp.dot(link_pool, link_out, preferred_element_type=jnp.float32),
        "ch",
        scatter_dimension=1,
        tiled=True,
    )
    mesh_mid = (mesh_latent.astype(jnp.float32) + link_agg).astype(jnp.bfloat16)
    middle_full = lax.all_gather(mesh_mid, "ch", axis=1, tiled=True)
    mesh_send = jnp.dot(middle_full, proc_sender, preferred_element_type=jnp.float32).astype(
        jnp.bfloat16
    )
    mesh_recv = jnp.dot(middle_full, proc_receiver, preferred_element_type=jnp.float32)
    global_senders = (
        jnp.arange(band_size, dtype=jnp.int32)[:, None] * mesh_rows + mesh_senders
    ).reshape(-1)
    empty_rows = jnp.zeros((band_size * capacity, half_width), jnp.bfloat16)
    piece = lax.all_gather(mesh_send, "band", axis=0, tiled=True)
    inside = (global_senders >= 0) & (global_senders < piece.shape[0])
    taken = jnp.take(piece, jnp.clip(global_senders, 0, piece.shape[0] - 1), axis=0)
    fetched = jnp.where(inside[:, None], taken, empty_rows)
    receivers = mesh_receivers.reshape(-1)
    proc_receiver_term = jnp.take(mesh_recv, receivers, axis=0)
    proc_edge_term = lax.dot_general(
        mesh_feats, proc_edge, contract_first, preferred_element_type=jnp.float32
    )
    proc_activity = jax.nn.silu(
        fetched.astype(jnp.float32) + proc_receiver_term + proc_edge_term
    ).astype(jnp.bfloat16)
    used = (jnp.arange(capacity, dtype=jnp.int32)[None, :] < mesh_counts[0][:, None]).reshape(-1)
    one_hot = (
        (jnp.arange(mesh_rows, dtype=jnp.int32)[:, None] == receivers[None, :]) & used[None, :]
    ).astype(jnp.bfloat16)
    proc_pool = jnp.dot(one_hot, proc_activity, preferred_element_type=jnp.float32).astype(
        jnp.bfloat16
    )
    proc_agg = lax.psum_scatter(
        jnp.dot(proc_pool, proc_out, preferred_element_type=jnp.float32).astype(jnp.bfloat16),
        "ch",
        scatter_dimension=1,
        tiled=True,
    )
    agg_full = lax.all_gather(proc_agg, "ch", axis=1, tiled=True)
    joined = jnp.concatenate([middle_full, agg_full], axis=1)
    node_hidden = jax.nn.silu(
        jnp.dot(joined, node_first, preferred_element_type=jnp.float32)
    ).astype(jnp.bfloat16)
    node_update = lax.psum_scatter(
        jnp.dot(node_hidden, node_second, preferred_element_type=jnp.float32),
        "ch",
        scatter_dimension=1,
        tiled=True,
    )
    row_total, row_squares = lax.psum(
        (jnp.sum(node_update, axis=1), jnp.sum(node_update * node_update, axis=1)), "ch"
    )
    row_mean = row_total / full_width
    row_var = row_squares / full_width - row_mean * row_mean
    normed = (
        (node_update - row_mean[:, None]) * lax.rsqrt(row_var + 1e-05)[:, None] * norm_gain[None, :]
    )
    return (mesh_mid.astype(jnp.float32) + normed).astype(jnp.bfloat16)


def solution(mesh):
    in_specs = (
        P(("grp", "band"), None),
        P(("grp", "band"), None),
        P(("grp", "band")),
        P(None, ("grp", "band")),
        P(("grp", "band"), "ch"),
        P(("grp", "band"), None),
        P(("grp", "band"), None),
        P(("grp", "band"), None),
        P(None, ("grp", "band")),
        P(None, "ch"),
        P("ch", None),
        P(None, "ch"),
        P(None, "ch"),
        P(None, "ch"),
        P("ch", None),
        P(None, "ch"),
        P(None, "ch"),
        P(None, "ch"),
        P("ch", None),
        P(None, "ch"),
        P("ch", None),
        P("ch"),
    )
    out_specs = P(("grp", "band"), "ch")
    return jax.shard_map(
        per_device, mesh=mesh, in_specs=in_specs, out_specs=out_specs, check_vma=False
    )
```

profile of v0, /device:TPU:0, one launch (start us, length us, event | category | flops | bytes accessed | tf_op | source)
XLA Modules:
  0.0 191.8 jit_solution(10391703845429549606)
XLA Ops:
  6.5 1.2 copy-done
  7.7 3.7 %convolution_convert_fusion = bf16[2048,512]{1,0:T(8,128)(2,1)} fusion(bf16[256,512]{1,0:T(8,128)(2,1)} %param.32, bf16[2048,227]{0,1:T(8,128)(2,1)S(1)} %copy-done, bf16[227,256]{1,0:T(8,128)(2,1)} %param.31), kind=kOutput, calls=%fused_computation.5 | convolution fusion | flops 778567680 | bytes 3405312 | tf_op jit(solution)/shard_map/dot_general | solution.py:57
  12.2 11.7 %reduce-scatter.5.cloned.1.call-done = bf16[2048,256]{1,0:T(8,128)(2,1)} async-done(((bf16[2048,512]{1,0:T(8,128)(2,1)}), bf16[2048,256]{1,0:T(8,128)(2,1)}) %reduce-scatter.5.cloned.1.call-update) | async-done | bytes 1048592 | tf_op jit(solution)/shard_map/reduce_scatter | solution.py:58
  24.3 0.6 and.45
  25.5 11.5 %all-gather.2.cloned.1.call-done = bf16[2048,512]{1,0:T(8,128)(2,1)} async-done(((bf16[2048,256]{1,0:T(8,128)(2,1)}), bf16[2048,512]{1,0:T(8,128)(2,1)}) %all-gather.2.cloned.1.call-update) | async-done | bytes 2097168 | tf_op jit(solution)/shard_map/all_gather | solution.py:61
  37.0 2.3 %convolution_convert_fusion.1 = bf16[2048,256]{1,0:T(8,128)(2,1)S(1)} fusion(bf16[2048,512]{1,0:T(8,128)(2,1)} %all-gather.2.cloned.1.call-done, bf16[512,256]{1,0:T(8,128)(2,1)S(1)} %copy-done.14), kind=kOutput, calls=%fused_computation.6 | convolution fusion | flops 537395200 | bytes 3407872 | tf_op jit(solution)/shard_map/dot_general | solution.py:62
  39.3 1.3 collective-permute-start.1
  40.6 4.6 %collective-permute-start = (bf16[2048,256]{1,0:T(8,128)(2,1)S(1)}, bf16[2048,256]{1,0:T(8,128)(2,1)S(1)}, u32[]{:S(2)}, u32[]{:S(2)}) collective-permute-start(bf16[2048,256]{1,0:T(8,128)(2,1)S(1)} %convolution_convert_fusion.1), channel_id=1, source_target_pairs={{0,2},{2,4},{4,6},{6,8},{8,10},{10,12},{12,14},{1,3},{3,5},{5,7},{... | collective-permute-start | bytes 3145736 | tf_op jit(solution)/shard_map/ppermute | solution.py:14
  45.3 1.9 all_gather.16
  47.5 2.7 %fusion.28 = f32[4096,256]{1,0:T(8,128)} fusion(bf16[4,4096]{1,0:T(4,128)(2,1)S(1)} %copy-done.6, bf16[4,256]{1,0:T(4,128)(2,1)S(1)} %copy-done.10), kind=kOutput, calls=%fused_computation.57 | convolution fusion | flops 8388608 | bytes 4229120 | tf_op jit(solution)/shard_map/dot_general | solution.py:74
  50.2 16.4 %collective-permute-done.1 = bf16[2048,256]{1,0:T(8,128)(2,1)S(1)} collective-permute-done((bf16[2048,256]{1,0:T(8,128)(2,1)S(1)}, bf16[2048,256]{1,0:T(8,128)(2,1)S(1)}, u32[]{:S(2)}, u32[]{:S(2)}) %collective-permute-start.1) | collective-permute-done | bytes 1048608 | tf_op jit(solution)/shard_map/ppermute | solution.py:15
  66.6 22.6 %collective-permute-done = bf16[2048,256]{1,0:T(8,128)(2,1)S(1)} collective-permute-done((bf16[2048,256]{1,0:T(8,128)(2,1)S(1)}, bf16[2048,256]{1,0:T(8,128)(2,1)S(1)}, u32[]{:S(2)}, u32[]{:S(2)}) %collective-permute-start) | collective-permute-done | bytes 1048608 | tf_op jit(solution)/shard_map/ppermute | solution.py:14
  89.2 1.8 pad_maximum_fusion
  91.0 15.3 %gather_fusion = bf16[4096,256]{1,0:T(8,128)(2,1)S(1)} fusion(bf16[6144,256]{1,0:T(8,128)(2,1)} %pad_maximum_fusion, s32[4096]{0:T(1024)S(1)} %broadcast_clamp_fusion), kind=kCustom, calls=%fused_computation | custom fusion | bytes 4210688 | tf_op jit(solution)/shard_map/jit(_take)/gather | solution.py:68
  106.3 4.3 %select_reduce_fusion = bf16[128,256]{1,0:T(8,128)(2,1)S(1)} fusion(f32[128,256]{1,0:T(8,128)S(1)} %fusion.27, pred[128,32]{1,0:T(8,128)(4,1)S(1)} %copy.24, pred[128,32]{1,0:T(8,128)(4,1)S(1)} %iota_compare_fusion.1, f32[4096,256]{1,0:T(8,128)} %fusion.28, bf16[4096,256]{1,0:T(8,128)(2,1)S(1)} %gather_fusion), kind=kLoop, calls=%fused_computation.3 | loop fusion | flops 10452992 | bytes 6496256 | tf_op jit(solution)/shard_map/reduce_sum | solution.py:79
  110.7 0.9 fusion.30
  111.6 0.7 fusion.21
  112.3 8.1 %reduce-scatter.7.cloned.1.call-done = f32[128,256]{1,0:T(8,128)} async-done(((f32[128,512]{1,0:T(8,128)}), f32[128,256]{1,0:T(8,128)}) %reduce-scatter.7.cloned.1.call-update) | async-done | bytes 131088 | tf_op jit(solution)/shard_map/reduce_scatter | solution.py:82
  120.4 0.9 add_convert_fusion.1
  121.3 1.9 all_gather.17
  123.4 1.1 fusion.29
  124.6 31.8 %all_gather.18 = bf16[1024,256]{1,0:T(8,128)(2,1)S(1)} all-gather(bf16[128,256]{1,0:T(8,128)(2,1)S(1)} %convolution_convert_fusion.4), channel_id=1, replica_groups=mesh['grp'=2,'band'=8,'ch'=2] {'band'}, dimensions={0}, use_global_device_ids=true | all-gather | bytes 589824 | tf_op jit(solution)/shard_map/all_gather | solution.py:98
  156.4 0.8 gather_fusion.2
  157.2 0.8 gather_fusion.1
  158.3 1.0 convolution_convert_fusion.2
  159.3 8.4 %reduce-scatter.9.cloned.1.call-done = bf16[128,256]{1,0:T(8,128)(2,1)} async-done(((bf16[128,512]{1,0:T(8,128)(2,1)}), bf16[128,256]{1,0:T(8,128)(2,1)}) %reduce-scatter.9.cloned.1.call-update) | async-done | bytes 65552 | tf_op jit(solution)/shard_map/reduce_scatter | solution.py:117
  167.7 2.3 %all_gather.19 = bf16[128,512]{1,0:T(8,128)(2,1)S(1)} all-gather(bf16[128,256]{1,0:T(8,128)(2,1)} %reduce-scatter.9.cloned.1.call-done), channel_id=1, replica_groups=mesh['grp'=2,'band'=8,'ch'=2] {'ch'}, dimensions={1}, use_global_device_ids=true | all-gather | bytes 196608 | tf_op jit(solution)/shard_map/all_gather | solution.py:123
  170.0 1.1 fusion.8
  171.1 9.0 %reduce-scatter.11.cloned.1.call-done = f32[128,256]{1,0:T(8,128)} async-done(((f32[128,512]{1,0:T(8,128)}), f32[128,256]{1,0:T(8,128)}) %reduce-scatter.11.cloned.1.call-update) | async-done | bytes 131088 | tf_op jit(solution)/shard_map/reduce_scatter | solution.py:128
  180.1 1.0 fusion.26
  181.1 2.5 %all-reduce = (f32[128]{0:T(128)S(1)}, f32[128]{0:T(128)S(1)}) all-reduce(f32[128]{0:T(128)S(1)} %get-tuple-element.6, f32[128]{0:T(128)S(1)} %get-tuple-element.5), channel_id=1, replica_groups=mesh['grp'=2,'band'=8,'ch'=2] {'ch'}, use_global_device_ids=true, to_apply=%region_8.9 | all-reduce | flops 256 | bytes 2048 | tf_op jit(solution)/shard_map/psum | solution.py:134
  183.6 1.6 add_convert_fusion
  (73 shorter events, 2.6 us)
Async XLA Ops:
  6.5 1.2 copy-start
  6.5 4.9 %copy-start.8 = (s32[8,16]{1,0:T(8,128)S(1)}, s32[8,16]{1,0:T(8,128)}, u32[]{:S(2)}) copy-start(s32[8,16]{1,0:T(8,128)} %param.28) | copy-start | bytes 1540
  6.5 17.4 %reduce-scatter.5.cloned.1.call-start = ((), (), s32[]{:S(2)}) async-start(), calls=%async_computation.4 | async-start | bytes 3145728 | tf_op jit(solution)/shard_map/reduce_scatter | solution.py:58
  11.4 12.6 %copy-start.9 = (s32[8,16]{1,0:T(8,128)S(1)}, s32[8,16]{1,0:T(8,128)}, u32[]{:S(2)}) copy-start(s32[8,16]{1,0:T(8,128)} %param.27) | copy-start | bytes 1540
  11.4 13.5 %copy-start.18 = (s32[1,8]{1,0:T(1,128)S(1)}, s32[1,8]{1,0:T(1,128)}, u32[]{:S(2)}) copy-start(s32[1,8]{1,0:T(1,128)} %param.29) | copy-start | bytes 100
  11.4 13.7 %copy-start.7 = (s32[128,32]{0,1:T(8,128)S(1)}, s32[128,32]{0,1:T(8,128)}, u32[]{:S(2)}) copy-start(s32[128,32]{0,1:T(8,128)} %param.23) | copy-start | bytes 49156
  11.4 25.6 %copy-start.14 = (bf16[512,256]{1,0:T(8,128)(2,1)S(1)}, bf16[512,256]{1,0:T(8,128)(2,1)}, u32[]{:S(2)}) copy-start(bf16[512,256]{1,0:T(8,128)(2,1)} %param.33) | copy-start | bytes 786436
  11.4 25.6 %all-gather.2.cloned.1.call-start = ((), (), s32[]{:S(2)}) async-start(), calls=%async_computation.5 | async-start | bytes 3145728 | tf_op jit(solution)/shard_map/all_gather | solution.py:61
  23.9 21.3 %copy-start.5 = (bf16[128,256]{1,0:T(8,128)(2,1)S(1)}, bf16[128,256]{1,0:T(8,128)(2,1)}, u32[]{:S(2)}) copy-start(bf16[128,256]{1,0:T(8,128)(2,1)} %param.26) | copy-start | bytes 196612
  23.9 23.2 %copy-start.12 = (s32[128]{0:T(128)S(1)}, s32[128]{0:T(128)}, u32[]{:S(2)}) copy-start(s32[128]{0:T(128)} %param.24) | copy-start | bytes 1540
  23.9 96.4 %reduce-scatter.7.cloned.1.call-start = ((), (), s32[]{:S(2)}) async-start(), calls=%async_computation.6 | async-start | bytes 393216 | tf_op jit(solution)/shard_map/reduce_scatter | solution.py:82
  25.0 22.3 %copy-start.3 = (bf16[512,256]{1,0:T(8,128)(2,1)S(1)}, bf16[512,256]{1,0:T(8,128)(2,1)}, u32[]{:S(2)}) copy-start(bf16[512,256]{1,0:T(8,128)(2,1)} %param.34) | copy-start | bytes 786436
  25.5 22.0 %copy-start.6 = (bf16[4,4096]{1,0:T(4,128)(2,1)S(1)}, bf16[4,4096]{1,0:T(4,128)(2,1)}, u32[]{:S(2)}) copy-start(bf16[4,4096]{1,0:T(4,128)(2,1)} %param.25) | copy-start | bytes 98308
  25.5 22.0 %copy-start.10 = (bf16[4,256]{1,0:T(4,128)(2,1)S(1)}, bf16[4,256]{1,0:T(4,128)(2,1)}, u32[]{:S(2)}) copy-start(bf16[4,256]{1,0:T(4,128)(2,1)} %param.35) | copy-start | bytes 6148
  39.3 27.3 %collective-permute-start.1 = (bf16[2048,256]{1,0:T(8,128)(2,1)S(1)}, bf16[2048,256]{1,0:T(8,128)(2,1)S(1)}, u32[]{:S(2)}, u32[]{:S(2)}) collective-permute-start(bf16[2048,256]{1,0:T(8,128)(2,1)S(1)} %convolution_convert_fusion.1), channel_id=1, source_target_pairs={{2,0},{4,2},{6,4},{8,6},{10,8},{12,10},{14,12},{3,1},{5,3},{7,5},{... | collective-permute-start | bytes 3145736 | tf_op jit(solution)/shard_map/ppermute | solution.py:15
  40.6 48.6 %collective-permute-start = (bf16[2048,256]{1,0:T(8,128)(2,1)S(1)}, bf16[2048,256]{1,0:T(8,128)(2,1)S(1)}, u32[]{:S(2)}, u32[]{:S(2)}) collective-permute-start(bf16[2048,256]{1,0:T(8,128)(2,1)S(1)} %convolution_convert_fusion.1), channel_id=1, source_target_pairs={{0,2},{2,4},{4,6},{6,8},{8,10},{10,12},{12,14},{1,3},{3,5},{5,7},{... | collective-permute-start | bytes 3145736 | tf_op jit(solution)/shard_map/ppermute | solution.py:14
  106.3 4.3 %copy-start.4 = (bf16[256,512]{1,0:T(8,128)(2,1)S(1)}, bf16[256,512]{1,0:T(8,128)(2,1)}, u32[]{:S(2)}) copy-start(bf16[256,512]{1,0:T(8,128)(2,1)} %param.36) | copy-start | bytes 786436
  106.3 16.9 %copy-start.1 = (bf16[512,256]{1,0:T(8,128)(2,1)S(1)}, bf16[512,256]{1,0:T(8,128)(2,1)}, u32[]{:S(2)}) copy-start(bf16[512,256]{1,0:T(8,128)(2,1)} %param.37) | copy-start | bytes 786436
  110.6 47.4 %copy-start.16 = (bf16[4,256]{1,0:T(4,128)(2,1)S(1)}, bf16[4,256]{1,0:T(4,128)(2,1)}, u32[]{:S(2)}) copy-start(bf16[4,256]{1,0:T(4,128)(2,1)} %param.39) | copy-start | bytes 6148
  110.6 47.4 %copy-start.17 = (bf16[4,128]{1,0:T(4,128)(2,1)S(1)}, bf16[4,128]{1,0:T(4,128)(2,1)}, u32[]{:S(2)}) copy-start(bf16[4,128]{1,0:T(4,128)(2,1)} %param.30) | copy-start | bytes 3076
  110.6 47.4 %copy-start.19 = (pred[128]{0:T(512)(128)(4,1)S(1)}, pred[128]{0:T(512)(128)(4,1)}, u32[]{:S(2)}) copy-start(pred[128]{0:T(512)(128)(4,1)} %and.45) | copy-start | bytes 388
  110.6 47.7 %copy-start.2 = (bf16[256,512]{1,0:T(8,128)(2,1)S(1)}, bf16[256,512]{1,0:T(8,128)(2,1)}, u32[]{:S(2)}) copy-start(bf16[256,512]{1,0:T(8,128)(2,1)} %param.40) | copy-start | bytes 786436
  110.6 59.3 %copy-start.13 = (bf16[1024,256]{1,0:T(8,128)(2,1)S(1)}, bf16[1024,256]{1,0:T(8,128)(2,1)}, u32[]{:S(2)}) copy-start(bf16[1024,256]{1,0:T(8,128)(2,1)} %param.41) | copy-start | bytes 1572868
  110.7 59.3 %copy-start.15 = (bf16[256,512]{1,0:T(8,128)(2,1)S(1)}, bf16[256,512]{1,0:T(8,128)(2,1)}, u32[]{:S(2)}) copy-start(bf16[256,512]{1,0:T(8,128)(2,1)} %param.42) | copy-start | bytes 786436
  111.6 56.1 %reduce-scatter.9.cloned.1.call-start = ((), (), s32[]{:S(2)}) async-start(), calls=%async_computation.7 | async-start | bytes 196608 | tf_op jit(solution)/shard_map/reduce_scatter | solution.py:117
  124.6 59.1 %copy-start.11 = (f32[256]{0:T(256)S(1)}, f32[256]{0:T(256)}, u32[]{:S(2)}) copy-start(f32[256]{0:T(256)} %param.43) | copy-start | bytes 3076
  159.3 20.8 %reduce-scatter.11.cloned.1.call-start = ((), (), s32[]{:S(2)}) async-start(), calls=%async_computation.8 | async-start | bytes 393216 | tf_op jit(solution)/shard_map/reduce_scatter | solution.py:128
Sparse Core Ops, SparseCore 0:
  11.6 12.2 reduce-scatter.4
  25.5 11.4 all-gather.1
  111.7 8.6 reduce-scatter.6
  159.4 8.2 reduce-scatter.8
  171.3 8.8 reduce-scatter.10
where the time goes:
time: 192 us
  waiting for transfers between devices  87.7 us (46%)
  blocking collectives  40.4 us (21%)
  local copies, waits for them, and re-layouts  20 us (10%)
  between operations  13.5 us (7%)
  matrix products  13.4 us (7%)
  other arithmetic  10.7 us (6%)
  starting transfers between devices  6.07 us (3%)
    all_gather x1, blocking collectives, per_device(): piece = lax.all_gather(mesh_send, 'band', axis=0, tiled=True)  31.8 us
    ppermute x1, waiting for transfers between devices, with_halo(): before = lax.ppermute(last, axis, up)  22.6 us
    ppermute x1, waiting for transfers between devices, with_halo(): after = lax.ppermute(leading, axis, down)  16.4 us
    gather x1, local copies, waits for them, and re-layouts, per_device(): jnp.take(slab_table, local_index, axis=0).astype(jnp.float32)  15.3 us
    reduce_scatter x1, waiting for transfers between devices, per_device(): lax.psum_scatter(partial_latent.astype(jnp.bfloat16), 'ch', scatter_dimen...  11.7 us
    all_gather x1, waiting for transfers between devices, per_device(): grid_latent = lax.all_gather(own_latent, 'ch', axis=1, tiled=True)  11.5 us
    reduce_scatter x1, waiting for transfers between devices, per_device(): lax.psum_scatter(jnp.dot(node_hidden, node_second, preferred_element_type...  8.98 us
    reduce_scatter x1, waiting for transfers between devices, per_device(): lax.psum_scatter(jnp.dot(proc_pool, proc_out, preferred_element_type=jnp....  8.37 us
  transfers between devices with their start and end apart: 7, of which 7 were waited for; matrix products, arithmetic and copies ran while one was open for 3% of the time, Pallas kernels for 0%

commit v1 on v0

v1 whole, which is shorter than its diff:
```python
import functools

import jax
import jax.numpy as jnp
from jax import lax
from jax.experimental import pallas as pl
from jax.experimental.pallas import tpu as pltpu
from jax.sharding import PartitionSpec as P

F32 = jnp.float32
BF16 = jnp.bfloat16
LANES = 128
CHUNK = 256
BLOCKS_PER_GROUP = 8
VMEM_LIMIT = 48 * 1024 * 1024


def dot(a, b):
    return jnp.dot(a, b, preferred_element_type=F32)


def dot_on(a, b, dim_a, dim_b):
    return lax.dot_general(a, b, (((dim_a,), (dim_b,)), ((), ())), preferred_element_type=F32)


def silu(v):
    return 0.5 * v * (1.0 + jnp.tanh(0.5 * v))


def iota(shape, dim):
    return lax.broadcasted_iota(jnp.int32, shape, dim)


def ones_where(mask):
    return jnp.where(mask, 1.0, 0.0).astype(BF16)


def call(body, out_shape, args, grid_spec=None, flops=0, moved=0, scratch=(), **kw):
    whole = pl.BlockSpec(memory_space=pltpu.VMEM)
    if "in_specs" not in kw:
        kw["in_specs"] = [whole] * len(args)
        kw["out_specs"] = jax.tree.map(lambda _: whole, out_shape)
    return pl.pallas_call(
        body,
        out_shape=out_shape,
        scratch_shapes=list(scratch),
        compiler_params=pltpu.CompilerParams(vmem_limit_bytes=VMEM_LIMIT),
        cost_estimate=pl.CostEstimate(flops=flops, bytes_accessed=moved, transcendentals=0),
        **kw,
    )(*args)


def pack_body(slab_rows, senders_ref, lengths_ref, feats_ref, own_ref, other_ref, out_ref):
    band = lax.axis_index("band")
    core = lax.axis_index("ch")
    nodes, slots = senders_ref.shape
    width = out_ref.shape[1]
    own, other = own_ref[...], other_ref[...]
    first = core == 0
    out_ref[0:nodes, :] = jnp.concatenate(
        [jnp.where(first, own, other), jnp.where(first, other, own)], axis=1
    )
    per_row = LANES // slots
    rows = nodes // per_row
    pieces = [senders_ref[pl.ds(j, rows, stride=per_row), :] for j in range(per_row)]
    index = jnp.concatenate(pieces, axis=1) - (band - 1) * slab_rows
    shape = (rows, LANES)
    spread = jnp.where(
        iota((rows, nodes), 1) // per_row == iota((rows, nodes), 0),
        lengths_ref[...].astype(F32),
        0.0,
    ).astype(BF16)
    pick = ones_where(iota((nodes, LANES), 0) % per_row == iota((nodes, LANES), 1) // slots)
    length = dot(spread, pick)
    used = (iota(shape, 1) % slots).astype(F32) < length
    high = jnp.where(used, index // LANES + 1, 0).astype(F32)
    low = jnp.where(used, index % LANES, 0).astype(F32)
    fill = jnp.zeros((rows, width - 2 * LANES), F32)
    feats = feats_ref[...].astype(F32)
    parts = [feats[:, k * width : (k + 1) * width] for k in range(feats.shape[1] // width)]
    tail = jnp.concatenate(parts + [jnp.concatenate([high, low, fill], axis=1)], axis=0)
    out_ref[nodes:, :] = tail.astype(BF16)


def embed_body(x_ref, f_own, f_oth, s_own, s_oth, l_own, l_oth, out_ref):
    x = x_ref[...]
    half = f_own.shape[1]
    hidden_own = silu(dot(x, f_own[...])).astype(BF16)
    hidden_oth = silu(dot(x, f_oth[...])).astype(BF16)
    latent = (dot(hidden_own, s_own[...]) + dot(hidden_oth, s_oth[...])).astype(BF16)
    out_ref[:, :half] = dot(latent, l_own[...]).astype(BF16)
    out_ref[:, half:] = dot(latent, l_oth[...]).astype(BF16)


def pool_part(high, low, feats, latent, kind, slots, table_ref, weights, payload, ranks, right, out_ref):
    lr_own, lr_oth, le_own, le_oth = weights
    blocks = high.shape[0]
    nodes = latent.shape[0]
    groups = blocks // BLOCKS_PER_GROUP
    group_nodes = nodes // groups
    group_slots = BLOCKS_PER_GROUP * LANES
    table_rows, width = table_ref.shape
    per_slab = table_rows // LANES
    recv = jnp.concatenate([dot(latent, lr_own[...]), dot(latent, lr_oth[...])], axis=1)
    recv_high = recv.astype(BF16).astype(F32)
    recv_low = recv - recv_high
    edge = jnp.concatenate([le_own[...], le_oth[...]], axis=1).astype(F32)
    base = (kind * per_slab + 1).astype(F32)
    local = high - base
    valid = (local >= 0.0) & (local < float(per_slab))
    flag = jnp.where(valid, 1.0, 0.0)
    flag16 = flag.astype(BF16)
    inclusive = dot(flag16, ones_where(iota((LANES, LANES), 0) <= iota((LANES, LANES), 1)))
    square = (blocks, blocks)
    ahead = ones_where(
        (iota(square, 1) < iota(square, 0))
        & (iota(square, 1) // BLOCKS_PER_GROUP == iota(square, 0) // BLOCKS_PER_GROUP)
    )
    offset = jnp.sum(dot(ahead, flag16), axis=1, keepdims=True)
    ranks[...] = jnp.where(valid, inclusive - flag + offset, -1.0)
    out_ref[...] = jnp.zeros(out_ref.shape, F32)
    node_rows = jnp.where(
        iota((group_nodes, group_slots), 1) // slots == iota((group_nodes, group_slots), 0), 1.0, 0.0
    )
    for g in range(groups):
        at = g * BLOCKS_PER_GROUP
        row_high = jnp.concatenate(
            [local[at + k : at + k + 1, :] for k in range(BLOCKS_PER_GROUP)], axis=1
        )
        row_low = jnp.concatenate(
            [low[at + k : at + k + 1, :] for k in range(BLOCKS_PER_GROUP)], axis=1
        )
        payload[...] = jnp.concatenate(
            [
                feats[g],
                row_high,
                row_low,
                jnp.zeros((2, group_slots), F32),
                node_rows,
                node_rows,
                jnp.zeros((8, group_slots), F32),
            ],
            axis=0,
        ).astype(BF16)
        n0 = g * group_nodes
        right[...] = jnp.concatenate(
            [
                edge,
                jnp.zeros((4, width), F32),
                recv_high[n0 : n0 + group_nodes],
                recv_low[n0 : n0 + group_nodes],
                jnp.zeros((8, width), F32),
            ],
            axis=0,
        ).astype(BF16)
        count = jnp.sum(flag[at : at + BLOCKS_PER_GROUP]).astype(jnp.int32)

        @pl.loop(0, (count + CHUNK - 1) // CHUNK)
        def _(step):
            wanted = (iota((CHUNK, LANES), 0) + step * CHUNK).astype(F32)
            select = jnp.concatenate(
                [
                    ones_where(ranks[at + k : at + k + 1, :] == wanted)
                    for k in range(BLOCKS_PER_GROUP)
                ],
                axis=1,
            )
            compact = dot_on(select, payload[...], 1, 1)
            row = (compact[:, 4:5] * float(LANES) + compact[:, 5:6]).astype(jnp.int32)
            choose = ones_where(row == iota((CHUNK, table_rows), 1))
            compact = compact.astype(BF16)
            pre = dot(choose, table_ref[...]) + dot(compact, right[...])
            act = silu(pre).astype(BF16)
            out_ref[n0 : n0 + group_nodes, :] += dot_on(
                compact[:, 8 : 8 + group_nodes], act, 0, 0
            )


def unpack(packed_ref, nodes, slots):
    width = packed_ref.shape[1]
    blocks = nodes * slots // LANES
    tail = packed_ref[nodes:, :].astype(F32)
    feat_rows = tail.shape[0] - blocks
    high = tail[feat_rows:, 0:LANES]
    low = tail[feat_rows:, LANES : 2 * LANES]
    per_group = BLOCKS_PER_GROUP * LANES // width
    feats = []
    for g in range(blocks // BLOCKS_PER_GROUP):
        rows = [tail[4 * k : 4 * k + 4] for k in range(g * per_group, (g + 1) * per_group)]
        feats.append(jnp.concatenate(rows, axis=1))
    return high, low, feats


def own_pool_body(nodes, slots, packed_ref, table_ref, lr_own, lr_oth, le_own, le_oth, out_ref, payload, ranks, right):
    first = lax.axis_index("ch") == 0
    high, low, feats = unpack(packed_ref, nodes, slots)
    half_blocks = high.shape[0] // 2
    half_groups = len(feats) // 2
    pick = lambda a, b: jnp.where(first, a, b)
    latent = pick(packed_ref[0 : nodes // 2, :], packed_ref[nodes // 2 : nodes, :])
    pool_part(
        pick(high[:half_blocks], high[half_blocks:]),
        pick(low[:half_blocks], low[half_blocks:]),
        [pick(feats[k], feats[half_groups + k]) for k in range(half_groups)],
        latent,
        jnp.int32(1),
        slots,
        table_ref,
        (lr_own, lr_oth, le_own, le_oth),
        payload,
        ranks,
        right,
        out_ref,
    )


def near_pool_body(nodes, slots, packed_ref, table_ref, lr_own, lr_oth, le_own, le_oth, out_ref, payload, ranks, right, total):
    high, low, feats = unpack(packed_ref, nodes, slots)
    kind = 2 * lax.axis_index("ch")
    pool_part(
        high,
        low,
        feats,
        packed_ref[0:nodes, :],
        kind,
        slots,
        table_ref,
        (lr_own, lr_oth, le_own, le_oth),
        payload,
        ranks,
        right,
        total,
    )
    out_ref[...] = total[...].astype(BF16)


def middle_body(packed_ref, near_ref, near_oth_ref, own_ref, own_oth_ref, lo_own, lo_oth, ps, pr, mid_ref, send_ref, recv_ref):
    first = lax.axis_index("ch") == 0
    half = lo_own.shape[0]
    nodes = near_ref.shape[0]
    mine, theirs = own_ref[...], own_oth_ref[...]
    flip = lambda a: jnp.concatenate([a[:, half:], a[:, :half]], axis=1)
    theirs = flip(theirs)
    total = near_ref[...].astype(F32) + flip(near_oth_ref[...]).astype(F32)
    total = total + jnp.concatenate(
        [jnp.where(first, mine, theirs), jnp.where(first, theirs, mine)], axis=0
    )
    pool = total.astype(BF16)
    agg = dot(pool[:, :half], lo_own[...]) + dot(pool[:, half:], lo_oth[...])
    mid = (packed_ref[0:nodes, :].astype(F32) + agg).astype(BF16)
    mid_ref[...] = mid
    send_ref[...] = dot(mid, ps[...]).astype(BF16)
    recv_ref[...] = dot(mid, pr[...])


def edge_body(patches, piece_ref, recv_ref, senders_ref, receivers_ref, limit_ref, feats_ref, pe, pool_ref):
    nodes = recv_ref.shape[0]
    rows = patches * nodes
    slots = senders_ref.shape[1] * rows // piece_ref.shape[0]
    recv = recv_ref[...]
    recv_high = recv.astype(BF16)
    recv_low = (recv - recv_high.astype(F32)).astype(BF16)
    total = None
    for k in range(piece_ref.shape[0] // rows):
        lanes = slice(k * slots, (k + 1) * slots)
        patch = iota((1, slots), 1) // (slots // patches)
        choose = ones_where(iota((rows, slots), 0) == senders_ref[:, lanes] + patch * nodes)
        into = iota((nodes, slots), 0) == receivers_ref[:, lanes]
        into16 = ones_where(into)
        pre = (
            dot_on(choose, piece_ref[k * rows : (k + 1) * rows, :], 0, 0)
            + dot_on(into16, recv_high, 0, 0)
            + dot_on(into16, recv_low, 0, 0)
            + dot_on(feats_ref[:, lanes], pe[...], 0, 0)
        )
        act = silu(pre).astype(BF16)
        part = dot(ones_where(into & (limit_ref[:, lanes] > 0)), act)
        total = part if total is None else total + part
    pool_ref[...] = total.astype(BF16)


def node_body(mid_ref, pool_ref, pool_oth_ref, po_own, po_oth, nf_own, nf_oth, ns_own, ns_oth, gain_ref, out_ref):
    first = lax.axis_index("ch") == 0
    width = mid_ref.shape[1]
    half = width // 2
    mid = mid_ref[...]
    agg = (dot(pool_ref[...], po_own[...]) + dot(pool_oth_ref[...], po_oth[...])).astype(BF16)
    update = None
    for nf, ns in ((nf_own, ns_own), (nf_oth, ns_oth)):
        hidden = silu(dot(mid, nf[0:width, :]) + dot(agg, nf[width:, :])).astype(BF16)
        term = dot(hidden, ns[...])
        update = term if update is None else update + term
    mean = jnp.sum(update, axis=1, keepdims=True) / width
    square = jnp.sum(update * update, axis=1, keepdims=True) / width
    scale = lax.rsqrt(square - mean * mean + 1e-05)
    pick = lambda a: jnp.where(first, a[:, :half], a[:, half:])
    out_ref[...] = (
        pick(mid).astype(F32) + (pick(update) - mean) * scale * gain_ref[...]
    ).astype(BF16)


def per_device(
    grid_input,
    grid_senders,
    grid_lengths,
    grid_feats,
    mesh_latent,
    mesh_senders,
    mesh_receivers,
    mesh_counts,
    mesh_feats,
    embed_first,
    embed_second,
    link_sender,
    link_receiver,
    link_edge,
    link_out,
    proc_sender,
    proc_receiver,
    proc_edge,
    proc_out,
    node_first,
    node_second,
    norm_gain,
):
    bands = lax.axis_size("band")
    slab_rows = grid_input.shape[0]
    nodes, slots = grid_senders.shape
    half = link_sender.shape[1]
    width = 2 * half
    capacity = mesh_senders.shape[1]
    edges = bands * capacity
    other = lambda a: lax.ppermute(a, "ch", [(0, 1), (1, 0)])
    at = lambda b, c: 2 * b + c
    to_owner = [(at(b + 1, 0), at(b, 0)) for b in range(bands - 1)]
    to_owner += [(at(b, 1), at(b + 1, 1)) for b in range(bands - 1)]
    to_patch = [(d, s) for s, d in to_owner]
    shape = jax.ShapeDtypeStruct

    latent_other = other(mesh_latent)
    packed_rows = nodes + 4 * (nodes * slots // width) + nodes * slots // LANES
    packed = call(
        functools.partial(pack_body, slab_rows),
        shape((packed_rows, width), BF16),
        (grid_senders, grid_lengths.reshape(1, nodes), grid_feats, mesh_latent, latent_other),
    )
    near_packed = lax.ppermute(packed, ("band", "ch"), to_owner)

    tile = slab_rows // 4
    fixed = lambda a: pl.BlockSpec(a.shape, lambda i: (0, 0))
    embed_weights = []
    for w in (embed_first, embed_second, link_sender):
        embed_weights += [w, other(w)]
    table = call(
        embed_body,
        shape((slab_rows, width), BF16),
        (grid_input, *embed_weights),
        grid=(slab_rows // tile,),
        in_specs=[pl.BlockSpec((tile, grid_input.shape[1]), lambda i: (i, 0))]
        + [fixed(w) for w in embed_weights],
        out_specs=pl.BlockSpec((tile, width), lambda i: (i, 0)),
        flops=2 * slab_rows * width * (256 + 2 * width),
        moved=4 * 1024 * 1024,
    )

    link_weights = (link_receiver, other(link_receiver), link_edge, other(link_edge))
    group_slots = BLOCKS_PER_GROUP * LANES
    group_nodes = group_slots // slots
    blocks = nodes * slots // LANES
    scratch = lambda count: [
        pltpu.VMEM((16 + 2 * group_nodes, group_slots), BF16),
        pltpu.VMEM((count, LANES), F32),
        pltpu.VMEM((16 + 2 * group_nodes, width), BF16),
    ]
    own = call(
        functools.partial(own_pool_body, nodes, slots),
        shape((nodes // 2, width), F32),
        (packed, table, *link_weights),
        scratch=scratch(blocks // 2),
        flops=4 * 10**9,
        moved=4 * 1024 * 1024,
    )
    own_other = other(own)
    near = call(
        functools.partial(near_pool_body, nodes, slots),
        shape((nodes, width), BF16),
        (near_packed, table, *link_weights),
        scratch=scratch(blocks) + [pltpu.VMEM((nodes, width), F32)],
        flops=4 * 10**9,
        moved=4 * 1024 * 1024,
    )
    near_back = lax.ppermute(near, ("band", "ch"), to_patch)
    near_back_other = other(near_back)

    mid, send, recv = call(
        middle_body,
        (shape((nodes, width), BF16), shape((nodes, half), BF16), shape((nodes, half), F32)),
        (packed, near_back, near_back_other, own, own_other, link_out, other(link_out), proc_sender, proc_receiver),
    )
    spread = jnp.broadcast_to(send[None], (bands, nodes, half)).reshape(bands * nodes, half)
    piece = lax.all_to_all(spread, "band", 0, 0, tiled=True)

    limit = (
        mesh_counts.reshape(bands, 1) - jnp.arange(capacity, dtype=jnp.int32)[None, :]
    ).reshape(1, edges)
    pool = call(
        functools.partial(edge_body, LANES // capacity),
        shape((nodes, half), BF16),
        (piece, recv, mesh_senders.reshape(1, edges), mesh_receivers.reshape(1, edges), limit, mesh_feats, proc_edge),
    )
    return call(
        node_body,
        shape((nodes, half), BF16),
        (
            mid,
            pool,
            other(pool),
            proc_out,
            other(proc_out),
            node_first,
            other(node_first),
            node_second,
            other(node_second),
            norm_gain.reshape(1, half),
        ),
    )


def solution(mesh):
    rows = P(("grp", "band"), None)
    columns = P(None, ("grp", "band"))
    split = P(("grp", "band"), "ch")
    by_column = P(None, "ch")
    by_row = P("ch", None)
    in_specs = (
        rows,
        rows,
        P(("grp", "band")),
        columns,
        split,
        rows,
        rows,
        rows,
        columns,
        by_column,
        by_row,
        by_column,
        by_column,
        by_column,
        by_row,
        by_column,
        by_column,
        by_column,
        by_row,
        by_column,
        by_row,
        P("ch"),
    )
    return jax.shard_map(
        per_device, mesh=mesh, in_specs=in_specs, out_specs=split, check_vma=False
    )
```

time: 192 us -> 60.4 us (0.31)
  waiting for transfers between devices: 87.7 us -> 19.3 us
  blocking collectives: 40.4 us -> 0 us
  Pallas kernels: 0 us -> 20.6 us
  local copies, waits for them, and re-layouts: 20 us -> 4.09 us
  matrix products: 13.4 us -> 0 us
  between operations: 13.5 us -> 0.3 us
  other arithmetic: 10.7 us -> 0.07 us
  starting transfers between devices: 6.07 us -> 15.2 us
    all_gather x4 -> x0, blocking collectives: 37.9 us -> none  [the longest x1 31.8 us: per_device(): piece = lax.all_gather(mesh_send, 'band', axis=0, tiled=True)]
    reduce_scatter x4 -> x0, waiting for transfers between devices: 37.1 us -> none  [the longest x1 11.7 us: per_device(): lax.psum_scatter(partial_latent.astype(jnp.bfloat16), 'ch', scatter_dimen...]
    ppermute x2 -> x15, waiting for transfers between devices: 39 us -> 5.42 us  [the longest x1 3.16 us: per_device(): near_packed = lax.ppermute(packed, ('band', 'ch'), to_owner)]
    pallas_call x0 -> x7, Pallas kernels: none -> 20.6 us  [call(): pl.pallas_call(body, out_shape=out_shape, scratch_shapes=list(scratch), c...]
    gather x3 -> x0, local copies, waits for them, and re-layouts: 16.9 us -> none  [the longest x1 15.3 us: per_device(): jnp.take(slab_table, local_index, axis=0).astype(jnp.float32)]
    all_to_all x0 -> x1, waiting for transfers between devices: none -> 13.8 us  [per_device(): piece = lax.all_to_all(spread, 'band', 0, 0, tiled=True)]
    dot_general x10 -> x0, matrix products: 13.4 us -> none  [the longest x1 3.67 us: per_device(): jnp.dot(embed_hidden, embed_second, preferred_element_type=jnp.float32)]
    all_gather x1 -> x0, waiting for transfers between devices: 11.5 us -> none  [per_device(): grid_latent = lax.all_gather(own_latent, 'ch', axis=1, tiled=True)]
  transfers between devices with their start and end apart: 7 -> 16, of which waited for: 7 -> 5; matrix products, arithmetic and copies ran while one was open for 3% -> 4% of each run, Pallas kernels for 0% -> 32%
where the time goes in v1:
time: 60.4 us; the launch traced here: 59.4 us
  Pallas kernels  20.6 us (34%)
  waiting for transfers between devices  19.3 us (32%)
  starting transfers between devices  15.2 us (25%)
  local copies, waits for them, and re-layouts  4.09 us (7%)
    pallas_call x7, Pallas kernels, call(): pl.pallas_call(body, out_shape=out_shape, scratch_shapes=list(scratch), c...  20.6 us
    all_to_all x1, waiting for transfers between devices, per_device(): piece = lax.all_to_all(spread, 'band', 0, 0, tiled=True)  13.8 us
    all_to_all x1, starting transfers between devices, per_device(): piece = lax.all_to_all(spread, 'band', 0, 0, tiled=True)  5.35 us
    ppermute x1, starting transfers between devices, per_device(): near_back = lax.ppermute(near, ('band', 'ch'), to_patch)  5.06 us
    ppermute x13, starting transfers between devices, per_device(): other = lambda a: lax.ppermute(a, 'ch', [(0, 1), (1, 0)])  3.47 us
    ppermute x1, waiting for transfers between devices, per_device(): near_packed = lax.ppermute(packed, ('band', 'ch'), to_owner)  3.16 us
    unnamed x42, local copies, waits for them, and re-layouts  3.03 us
    ppermute x13, waiting for transfers between devices, per_device(): other = lambda a: lax.ppermute(a, 'ch', [(0, 1), (1, 0)])  2.25 us
  transfers between devices with their start and end apart: 16, of which 5 were waited for; matrix products, arithmetic and copies ran while one was open for 4% of the time, Pallas kernels for 32%

profile of v1, /device:TPU:0, one launch (start us, length us, event | category | flops | bytes accessed | tf_op | source)
XLA Modules:
  0.0 59.4 jit_solution(2920668421566548444)
XLA Ops:
  0.0 0.5 collective-permute-start.3
  0.6 0.1 collective-permute-start.4
  0.6 0.4 collective-permute-start.2
  1.1 0.1 collective-permute-start
  1.1 0.4 collective-permute-start.5
  1.6 0.8 %copy.23.senders_ref = s32[128,32]{1,0:T(8,128)S(1)} copy(s32[128,32]{0,1:T(8,128)} %param.23) | data formatting | bytes 32768 | tf_op args[1]
  2.4 1.5 %copy.24.x_ref = bf16[2048,227]{1,0:T(8,128)(2,1)S(1)} copy(bf16[2048,227]{0,1:T(8,128)(2,1)} %param.22) | data formatting | bytes 1859584 | tf_op args[0]
  3.9 0.1 collective-permute-start.6
  4.0 0.7 %copy-done.11 = s32[128]{0:T(128)S(1)} copy-done((s32[128]{0:T(128)S(1)}, s32[128]{0:T(128)}, u32[]{:S(2)}) %copy-start.11) | copy-done | bytes 536
  4.7 0.1 shard_map.208.packed_ref
  4.8 0.5 collective-permute-start.10
  5.3 1.3 %collective-permute-start.1 = (bf16[192,512]{1,0:T(8,128)(2,1)S(1)}, bf16[192,512]{1,0:T(8,128)(2,1)S(1)}, u32[]{:S(2)}, u32[]{:S(2)}) collective-permute-start(bf16[192,512]{1,0:T(8,128)(2,1)S(1)} %shard_map.208.packed_ref), channel_id=1, source_target_pairs={{2,0},{4,2},{6,4},{8,6},{10,8},{12,10},{14,12},{1,3},{3,5},{5,7},{... | collective-permute-start | bytes 589832 | tf_op jit(solution)/shard_map/ppermute | solution.py:347
  6.7 3.6 %shard_map.209.table_ref = bf16[2048,512]{1,0:T(8,128)(2,1)S(1)} custom-call(bf16[2048,227]{1,0:T(8,128)(2,1)S(1)} %copy.24.x_ref, bf16[227,256]{1,0:T(8,128)(2,1)S(1)} %copy-done.15, bf16[227,256]{1,0:T(8,128)(2,1)S(1)} %collective-permute-done.2.f_oth, bf16[256,512]{1,0:T(8,128)(2,1)S(1)} %copy-done.12, bf16[256,512]{1,0:T(8,128)(2,1)S(1)} %collective-permute-done.3.s_oth, ...), custom_call_target="tpu_custom_call" | custom-call | flops 2684354560 | bytes 4194304 | tf_op jit(solution)/shard_map/pallas_call | solution.py:43
  10.3 3.2 %collective-permute-done.1.packed_ref = bf16[192,512]{1,0:T(8,128)(2,1)S(1)} collective-permute-done((bf16[192,512]{1,0:T(8,128)(2,1)S(1)}, bf16[192,512]{1,0:T(8,128)(2,1)S(1)}, u32[]{:S(2)}, u32[]{:S(2)}) %collective-permute-start.1) | collective-permute-done | bytes 196640 | tf_op jit(solution)/shard_map/ppermute | solution.py:347
  13.5 7.4 %shard_map.210 = bf16[128,512]{1,0:T(8,128)(2,1)S(1)} custom-call(bf16[192,512]{1,0:T(8,128)(2,1)S(1)} %collective-permute-done.1.packed_ref, bf16[2048,512]{1,0:T(8,128)(2,1)S(1)} %shard_map.209.table_ref, bf16[512,256]{1,0:T(8,128)(2,1)S(1)} %copy-done.14, bf16[512,256]{1,0:T(8,128)(2,1)S(1)} %collective-permute-done.5.lr_oth, ...), custom_call_target="tpu_custom_call" | custom-call | flops 4000000000 | bytes 4194304 | tf_op jit(solution)/shard_map/pallas_call | solution.py:43
  20.9 5.1 %collective-permute-start.7 = (bf16[128,512]{1,0:T(8,128)(2,1)S(1)}, bf16[128,512]{1,0:T(8,128)(2,1)S(1)}, u32[]{:S(2)}, u32[]{:S(2)}) collective-permute-start(bf16[128,512]{1,0:T(8,128)(2,1)S(1)} %shard_map.210), channel_id=1, source_target_pairs={{0,2},{2,4},{4,6},{6,8},{8,10},{10,12},{12,14},{3,1},{5,3},{7,5},{... | collective-permute-start | bytes 393224 | tf_op jit(solution)/shard_map/ppermute | solution.py:392
  26.0 7.1 %shard_map.211.own_ref = f32[64,512]{1,0:T(8,128)S(1)} custom-call(bf16[192,512]{1,0:T(8,128)(2,1)S(1)} %shard_map.208.packed_ref, bf16[2048,512]{1,0:T(8,128)(2,1)S(1)} %shard_map.209.table_ref, bf16[512,256]{1,0:T(8,128)(2,1)S(1)} %copy-done.14, bf16[512,256]{1,0:T(8,128)(2,1)S(1)} %collective-permute-done.5.lr_oth, bf16[4,256]{1,0:T(4,128)(2,1)S(1)} %copy-done.16, ...), custom_call_target="tpu_custom_call" | custom-call | flops 4000000000 | bytes 4194304 | tf_op jit(solution)/shard_map/pallas_call | solution.py:43
  33.3 0.5 collective-permute-start.8
  33.8 0.8 %collective-permute-done.9.own_oth_ref = f32[64,512]{1,0:T(8,128)S(1)} collective-permute-done((f32[64,512]{1,0:T(8,128)S(1)}, f32[64,512]{1,0:T(8,128)S(1)}, u32[]{:S(2)}, u32[]{:S(2)}) %collective-permute-start.9) | collective-permute-done | bytes 131104 | tf_op jit(solution)/shard_map/ppermute | solution.py:333
  34.6 0.2 collective-permute-done.8.near_oth_ref
  34.8 0.4 shard_map.212
  35.2 0.8 %broadcast_in_dim.2 = bf16[8,128,256]{2,1,0:T(8,128)(2,1)} broadcast(bf16[128,256]{1,0:T(8,128)(2,1)S(1)} %get-tuple-element.9), dimensions={1,2} | broadcast | bytes 589824 | tf_op jit(solution)/shard_map/broadcast_in_dim | solution.py:400
  36.0 5.4 %all-to-all-start = ((bf16[8,128,256]{2,1,0:T(8,128)(2,1)}), bf16[8,128,256]{2,1,0:T(8,128)(2,1)S(1)}, u32[]{:S(2)}, u32[]{:S(2)}) async-start(bf16[8,128,256]{2,1,0:T(8,128)(2,1)} %broadcast_in_dim.2), calls=%async_computation | async-start | bytes 1048576 | tf_op jit(solution)/shard_map/all_to_all | solution.py:401
  41.5 0.5 collective-permute-start.12
  42.0 0.1 collective-permute-start.14
  42.1 0.1 sub.29.limit_ref
  42.2 0.1 reshape.43.senders_ref
  42.3 0.1 reshape.44.receivers_ref
  42.4 13.8 %all-to-all-done = bf16[8,128,256]{2,1,0:T(8,128)(2,1)S(1)} async-done(((bf16[8,128,256]{2,1,0:T(8,128)(2,1)}), bf16[8,128,256]{2,1,0:T(8,128)(2,1)S(1)}, u32[]{:S(2)}, u32[]{:S(2)}) %all-to-all-start) | async-done | bytes 524320 | tf_op jit(solution)/shard_map/all_to_all | solution.py:401
  56.2 0.5 shard_map.213.pool_ref
  56.8 1.2 %collective-permute-done.11.pool_oth_ref = bf16[128,256]{1,0:T(8,128)(2,1)S(1)} collective-permute-done((bf16[128,256]{1,0:T(8,128)(2,1)S(1)}, bf16[128,256]{1,0:T(8,128)(2,1)S(1)}, u32[]{:S(2)}, u32[]{:S(2)}) %collective-permute-start.11) | collective-permute-done | bytes 65568 | tf_op jit(solution)/shard_map/ppermute | solution.py:333
  58.0 1.4 %shard_map.214 = bf16[128,256]{1,0:T(8,128)(2,1)} custom-call(bf16[128,512]{1,0:T(8,128)(2,1)S(1)} %get-tuple-element.8.mid_ref, bf16[128,256]{1,0:T(8,128)(2,1)S(1)} %shard_map.213.pool_ref, bf16[128,256]{1,0:T(8,128)(2,1)S(1)} %collective-permute-done.11.pool_oth_ref, bf16[256,512]{1,0:T(8,128)(2,1)S(1)} %copy-done.4, ...), custom_call_target="tpu_custom_call" | custom-call | tf_op jit(solution)/shard_map/pallas_call | solution.py:43
  (54 shorter events, 0.4 us)
Async XLA Ops:
  0.0 6.6 %copy-start.12 = (bf16[256,512]{1,0:T(8,128)(2,1)S(1)}, bf16[256,512]{1,0:T(8,128)(2,1)}, u32[]{:S(2)}) copy-start(bf16[256,512]{1,0:T(8,128)(2,1)} %s_own.1) | copy-start | bytes 786436
  0.0 6.7 %copy-start.13 = (bf16[512,256]{1,0:T(8,128)(2,1)S(1)}, bf16[512,256]{1,0:T(8,128)(2,1)}, u32[]{:S(2)}) copy-start(bf16[512,256]{1,0:T(8,128)(2,1)} %l_own.1) | copy-start | bytes 786436
  0.0 6.7 %copy-start.15 = (bf16[227,256]{1,0:T(8,128)(2,1)S(1)}, bf16[227,256]{1,0:T(8,128)(2,1)}, u32[]{:S(2)}) copy-start(bf16[227,256]{1,0:T(8,128)(2,1)} %f_own.1) | copy-start | bytes 348676
  0.0 5.3 %collective-permute-start.3 = (bf16[256,512]{1,0:T(8,128)(2,1)}, bf16[256,512]{1,0:T(8,128)(2,1)S(1)}, u32[]{:S(2)}, u32[]{:S(2)}) collective-permute-start(bf16[256,512]{1,0:T(8,128)(2,1)} %s_own.1), channel_id=1, source_target_pairs={{0,1},{1,0},{2,3},{3,2},{4,5},{5,4},{6,7},{7,6},{8,9},{9,8},{10,11... | collective-permute-start | bytes 786440 | tf_op jit(solution)/shard_map/ppermute | solution.py:333
  0.6 6.1 %collective-permute-start.4 = (bf16[512,256]{1,0:T(8,128)(2,1)}, bf16[512,256]{1,0:T(8,128)(2,1)S(1)}, u32[]{:S(2)}, u32[]{:S(2)}) collective-permute-start(bf16[512,256]{1,0:T(8,128)(2,1)} %l_own.1), channel_id=1, source_target_pairs={{0,1},{1,0},{2,3},{3,2},{4,5},{5,4},{6,7},{7,6},{8,9},{9,8},{10,11... | collective-permute-start | bytes 786440 | tf_op jit(solution)/shard_map/ppermute | solution.py:333
  0.6 4.2 %collective-permute-start.2 = (bf16[227,256]{1,0:T(8,128)(2,1)}, bf16[227,256]{1,0:T(8,128)(2,1)S(1)}, u32[]{:S(2)}, u32[]{:S(2)}) collective-permute-start(bf16[227,256]{1,0:T(8,128)(2,1)} %f_own.1), channel_id=1, source_target_pairs={{0,1},{1,0},{2,3},{3,2},{4,5},{5,4},{6,7},{7,6},{8,9},{9,8},{10,11... | collective-permute-start | bytes 348680 | tf_op jit(solution)/shard_map/ppermute | solution.py:333
  1.1 2.8 %collective-permute-start = (bf16[128,256]{1,0:T(8,128)(2,1)}, bf16[128,256]{1,0:T(8,128)(2,1)S(1)}, u32[]{:S(2)}, u32[]{:S(2)}) collective-permute-start(bf16[128,256]{1,0:T(8,128)(2,1)} %own_ref.1), channel_id=1, source_target_pairs={{0,1},{1,0},{2,3},{3,2},{4,5},{5,4},{6,7},{7,6},{8,9},{9,8},{10,11... | collective-permute-start | bytes 196616 | tf_op jit(solution)/shard_map/ppermute | solution.py:333
  1.1 12.3 %collective-permute-start.5 = (bf16[512,256]{1,0:T(8,128)(2,1)}, bf16[512,256]{1,0:T(8,128)(2,1)S(1)}, u32[]{:S(2)}, u32[]{:S(2)}) collective-permute-start(bf16[512,256]{1,0:T(8,128)(2,1)} %lr_own.3), channel_id=1, source_target_pairs={{0,1},{1,0},{2,3},{3,2},{4,5},{5,4},{6,7},{7,6},{8,9},{9,8},{10,11... | collective-permute-start | bytes 786440 | tf_op jit(solution)/shard_map/ppermute | solution.py:333
  3.9 6.4 %collective-permute-start.6 = (bf16[4,256]{1,0:T(4,128)(2,1)}, bf16[4,256]{1,0:T(4,128)(2,1)S(1)}, u32[]{:S(2)}, u32[]{:S(2)}) collective-permute-start(bf16[4,256]{1,0:T(4,128)(2,1)} %le_own.3), channel_id=1, source_target_pairs={{0,1},{1,0},{2,3},{3,2},{4,5},{5,4},{6,7},{7,6},{8,9},{9,8},{10,11... | collective-permute-start | bytes 6152 | tf_op jit(solution)/shard_map/ppermute | solution.py:333
  4.8 8.6 %copy-start.14 = (bf16[512,256]{1,0:T(8,128)(2,1)S(1)}, bf16[512,256]{1,0:T(8,128)(2,1)}, u32[]{:S(2)}) copy-start(bf16[512,256]{1,0:T(8,128)(2,1)} %lr_own.3) | copy-start | bytes 786436
  4.8 8.6 %copy-start.16 = (bf16[4,256]{1,0:T(4,128)(2,1)S(1)}, bf16[4,256]{1,0:T(4,128)(2,1)}, u32[]{:S(2)}) copy-start(bf16[4,256]{1,0:T(4,128)(2,1)} %le_own.3) | copy-start | bytes 6148
  4.8 28.9 %collective-permute-start.10 = (bf16[256,512]{1,0:T(8,128)(2,1)S(1)}, bf16[256,512]{1,0:T(8,128)(2,1)S(1)}, u32[]{:S(2)}, u32[]{:S(2)}) collective-permute-start(bf16[256,512]{1,0:T(8,128)(2,1)S(1)} %copy-done.1), channel_id=1, source_target_pairs={{0,1},{1,0},{2,3},{3,2},{4,5},{5,4},{6,7},{7,6},{8,9},{9,8},{10,11... | collective-permute-start | bytes 786440 | tf_op jit(solution)/shard_map/ppermute | solution.py:333
  5.3 8.1 %collective-permute-start.1 = (bf16[192,512]{1,0:T(8,128)(2,1)S(1)}, bf16[192,512]{1,0:T(8,128)(2,1)S(1)}, u32[]{:S(2)}, u32[]{:S(2)}) collective-permute-start(bf16[192,512]{1,0:T(8,128)(2,1)S(1)} %shard_map.208.packed_ref), channel_id=1, source_target_pairs={{2,0},{4,2},{6,4},{8,6},{10,8},{12,10},{14,12},{1,3},{3,5},{5,7},{... | collective-permute-start | bytes 589832 | tf_op jit(solution)/shard_map/ppermute | solution.py:347
  20.9 13.9 %copy-start.2 = (bf16[512,256]{1,0:T(8,128)(2,1)S(1)}, bf16[512,256]{1,0:T(8,128)(2,1)}, u32[]{:S(2)}) copy-start(bf16[512,256]{1,0:T(8,128)(2,1)} %ps.1) | copy-start | bytes 786436
  20.9 13.9 %copy-start.3 = (bf16[512,256]{1,0:T(8,128)(2,1)S(1)}, bf16[512,256]{1,0:T(8,128)(2,1)}, u32[]{:S(2)}) copy-start(bf16[512,256]{1,0:T(8,128)(2,1)} %pr.1) | copy-start | bytes 786436
  20.9 12.4 %collective-permute-start.7 = (bf16[128,512]{1,0:T(8,128)(2,1)S(1)}, bf16[128,512]{1,0:T(8,128)(2,1)S(1)}, u32[]{:S(2)}, u32[]{:S(2)}) collective-permute-start(bf16[128,512]{1,0:T(8,128)(2,1)S(1)} %shard_map.210), channel_id=1, source_target_pairs={{0,2},{2,4},{4,6},{6,8},{8,10},{10,12},{12,14},{3,1},{5,3},{7,5},{... | collective-permute-start | bytes 393224 | tf_op jit(solution)/shard_map/ppermute | solution.py:392
  33.1 8.3 %copy-start = (bf16[1024,256]{1,0:T(8,128)(2,1)S(1)}, bf16[1024,256]{1,0:T(8,128)(2,1)}, u32[]{:S(2)}) copy-start(bf16[1024,256]{1,0:T(8,128)(2,1)} %nf_own.1) | copy-start | bytes 1572868
  33.1 8.4 %copy-start.4 = (bf16[256,512]{1,0:T(8,128)(2,1)S(1)}, bf16[256,512]{1,0:T(8,128)(2,1)}, u32[]{:S(2)}) copy-start(bf16[256,512]{1,0:T(8,128)(2,1)} %po_own.1) | copy-start | bytes 786436
  33.1 8.9 %copy-start.5 = (bf16[256,512]{1,0:T(8,128)(2,1)S(1)}, bf16[256,512]{1,0:T(8,128)(2,1)}, u32[]{:S(2)}) copy-start(bf16[256,512]{1,0:T(8,128)(2,1)} %ns_own.1) | copy-start | bytes 786436
  33.1 9.0 %copy-start.19 = (s32[1,8]{1,0:T(1,128)S(1)}, s32[1,8]{1,0:T(1,128)}, u32[]{:S(2)}) copy-start(s32[1,8]{1,0:T(1,128)} %param.29) | copy-start | bytes 100
  33.1 9.1 %copy-start.17 = (s32[8,16]{1,0:T(8,128)S(1)}, s32[8,16]{1,0:T(8,128)}, u32[]{:S(2)}) copy-start(s32[8,16]{1,0:T(8,128)} %param.27) | copy-start | bytes 1540
  33.1 9.2 %copy-start.18 = (s32[8,16]{1,0:T(8,128)S(1)}, s32[8,16]{1,0:T(8,128)}, u32[]{:S(2)}) copy-start(s32[8,16]{1,0:T(8,128)} %param.28) | copy-start | bytes 1540
  33.1 23.1 %copy-start.8 = (bf16[4,256]{1,0:T(4,128)(2,1)S(1)}, bf16[4,256]{1,0:T(4,128)(2,1)}, u32[]{:S(2)}) copy-start(bf16[4,256]{1,0:T(4,128)(2,1)} %pe.1) | copy-start | bytes 6148
  33.2 23.1 %copy-start.9 = (bf16[4,128]{1,0:T(4,128)(2,1)S(1)}, bf16[4,128]{1,0:T(4,128)(2,1)}, u32[]{:S(2)}) copy-start(bf16[4,128]{1,0:T(4,128)(2,1)} %feats_ref.3) | copy-start | bytes 3076
  33.2 24.9 %copy-start.10 = (f32[256]{0:T(256)S(1)}, f32[256]{0:T(256)}, u32[]{:S(2)}) copy-start(f32[256]{0:T(256)} %param.43) | copy-start | bytes 3076
  33.2 1.4 %collective-permute-start.9 = (f32[64,512]{1,0:T(8,128)S(1)}, f32[64,512]{1,0:T(8,128)S(1)}, u32[]{:S(2)}, u32[]{:S(2)}) collective-permute-start(f32[64,512]{1,0:T(8,128)S(1)} %shard_map.211.own_ref), channel_id=1, source_target_pairs={{0,1},{1,0},{2,3},{3,2},{4,5},{5,4},{6,7},{7,6},{8,9},{9,8},{10,11... | collective-permute-start | bytes 393224 | tf_op jit(solution)/shard_map/ppermute | solution.py:333
  33.3 1.5 %collective-permute-start.8 = (bf16[128,512]{1,0:T(8,128)(2,1)S(1)}, bf16[128,512]{1,0:T(8,128)(2,1)S(1)}, u32[]{:S(2)}, u32[]{:S(2)}) collective-permute-start(bf16[128,512]{1,0:T(8,128)(2,1)S(1)} %collective-permute-done.7.near_ref), channel_id=1, source_target_pairs={{0,1},{1,0},{2,3},{3,2},{4,5},{5,4},{6,7},{7,6},{8,9},{9,8},{10,11... | collective-permute-start | bytes 393224 | tf_op jit(solution)/shard_map/ppermute | solution.py:333
  36.0 20.2 %all-to-all-start = ((bf16[8,128,256]{2,1,0:T(8,128)(2,1)}), bf16[8,128,256]{2,1,0:T(8,128)(2,1)S(1)}, u32[]{:S(2)}, u32[]{:S(2)}) async-start(bf16[8,128,256]{2,1,0:T(8,128)(2,1)} %broadcast_in_dim.2), calls=%async_computation | async-start | bytes 1048576 | tf_op jit(solution)/shard_map/all_to_all | solution.py:401
  41.4 15.4 %collective-permute-start.13 = (bf16[1024,256]{1,0:T(8,128)(2,1)S(1)}, bf16[1024,256]{1,0:T(8,128)(2,1)S(1)}, u32[]{:S(2)}, u32[]{:S(2)}) collective-permute-start(bf16[1024,256]{1,0:T(8,128)(2,1)S(1)} %copy-done), channel_id=1, source_target_pairs={{0,1},{1,0},{2,3},{3,2},{4,5},{5,4},{6,7},{7,6},{8,9},{9,8},{10,11... | collective-permute-start | bytes 1572872 | tf_op jit(solution)/shard_map/ppermute | solution.py:333
  41.5 15.3 %collective-permute-start.12 = (bf16[256,512]{1,0:T(8,128)(2,1)S(1)}, bf16[256,512]{1,0:T(8,128)(2,1)S(1)}, u32[]{:S(2)}, u32[]{:S(2)}) collective-permute-start(bf16[256,512]{1,0:T(8,128)(2,1)S(1)} %copy-done.4), channel_id=1, source_target_pairs={{0,1},{1,0},{2,3},{3,2},{4,5},{5,4},{6,7},{7,6},{8,9},{9,8},{10,11... | collective-permute-start | bytes 786440 | tf_op jit(solution)/shard_map/ppermute | solution.py:333
  42.0 14.8 %collective-permute-start.14 = (bf16[256,512]{1,0:T(8,128)(2,1)S(1)}, bf16[256,512]{1,0:T(8,128)(2,1)S(1)}, u32[]{:S(2)}, u32[]{:S(2)}) collective-permute-start(bf16[256,512]{1,0:T(8,128)(2,1)S(1)} %copy-done.5), channel_id=1, source_target_pairs={{0,1},{1,0},{2,3},{3,2},{4,5},{5,4},{6,7},{7,6},{8,9},{9,8},{10,11... | collective-permute-start | bytes 786440 | tf_op jit(solution)/shard_map/ppermute | solution.py:333
  56.7 1.3 %collective-permute-start.11 = (bf16[128,256]{1,0:T(8,128)(2,1)S(1)}, bf16[128,256]{1,0:T(8,128)(2,1)S(1)}, u32[]{:S(2)}, u32[]{:S(2)}) collective-permute-start(bf16[128,256]{1,0:T(8,128)(2,1)S(1)} %shard_map.213.pool_ref), channel_id=1, source_target_pairs={{0,1},{1,0},{2,3},{3,2},{4,5},{5,4},{6,7},{7,6},{8,9},{9,8},{10,11... | collective-permute-start | bytes 196616 | tf_op jit(solution)/shard_map/ppermute | solution.py:333
  (4 other events, 13.5 us)

commit v2 on v1

--- a/solution.py
+++ b/solution.py
@@ -10,7 +10,7 @@
 F32 = jnp.float32
 BF16 = jnp.bfloat16
 LANES = 128
-CHUNK = 256
+CHUNK = 288
 BLOCKS_PER_GROUP = 8
 VMEM_LIMIT = 48 * 1024 * 1024
 
@@ -50,11 +50,12 @@
     )(*args)
 
 
-def pack_body(slab_rows, senders_ref, lengths_ref, feats_ref, own_ref, other_ref, out_ref):
+def pack_body(slab_rows, senders_ref, lengths_ref, feats_ref, own_ref, other_ref, out_ref, turned):
     band = lax.axis_index("band")
     core = lax.axis_index("ch")
-    nodes, slots = senders_ref.shape
+    slots, nodes = senders_ref.shape
     width = out_ref.shape[1]
+    turned[...] = (senders_ref[...] - (band - 1) * slab_rows).astype(F32).T
     own, other = own_ref[...], other_ref[...]
     first = core == 0
     out_ref[0:nodes, :] = jnp.concatenate(
@@ -62,8 +63,8 @@
     )
     per_row = LANES // slots
     rows = nodes // per_row
-    pieces = [senders_ref[pl.ds(j, rows, stride=per_row), :] for j in range(per_row)]
-    index = jnp.concatenate(pieces, axis=1) - (band - 1) * slab_rows
+    pieces = [turned[pl.ds(j, rows, stride=per_row), :] for j in range(per_row)]
+    index = jnp.concatenate(pieces, axis=1).astype(jnp.int32)
     shape = (rows, LANES)
     spread = jnp.where(
         iota((rows, nodes), 1) // per_row == iota((rows, nodes), 0),
@@ -85,8 +86,8 @@
 def embed_body(x_ref, f_own, f_oth, s_own, s_oth, l_own, l_oth, out_ref):
     x = x_ref[...]
     half = f_own.shape[1]
-    hidden_own = silu(dot(x, f_own[...])).astype(BF16)
-    hidden_oth = silu(dot(x, f_oth[...])).astype(BF16)
+    hidden_own = silu(dot_on(x, f_own[...], 0, 0)).astype(BF16)
+    hidden_oth = silu(dot_on(x, f_oth[...], 0, 0)).astype(BF16)
     latent = (dot(hidden_own, s_own[...]) + dot(hidden_oth, s_oth[...])).astype(BF16)
     out_ref[:, :half] = dot(latent, l_own[...]).astype(BF16)
     out_ref[:, half:] = dot(latent, l_oth[...]).astype(BF16)
@@ -117,24 +118,33 @@
         & (iota(square, 1) // BLOCKS_PER_GROUP == iota(square, 0) // BLOCKS_PER_GROUP)
     )
     offset = jnp.sum(dot(ahead, flag16), axis=1, keepdims=True)
-    ranks[...] = jnp.where(valid, inclusive - flag + offset, -1.0)
-    out_ref[...] = jnp.zeros(out_ref.shape, F32)
+    rank = jnp.where(valid, inclusive - flag + offset, -1.0)
+    ranks[...] = rank
     node_rows = jnp.where(
         iota((group_nodes, group_slots), 1) // slots == iota((group_nodes, group_slots), 0), 1.0, 0.0
     )
+
+    def pooled(rank_rows, start, columns, terms):
+        wanted = iota((CHUNK, LANES), 0).astype(F32) + start
+        select = jnp.concatenate([ones_where(r == wanted) for r in rank_rows], axis=1)
+        compact = dot_on(select, columns, 1, 1)
+        row = (compact[:, 4:5] * float(LANES) + compact[:, 5:6]).astype(jnp.int32)
+        choose = ones_where(row == iota((CHUNK, table_rows), 1))
+        compact = compact.astype(BF16)
+        pre = dot(choose, table_ref[...]) + dot(compact, terms)
+        return dot_on(compact[:, 8 : 8 + group_nodes], silu(pre).astype(BF16), 0, 0)
+
     for g in range(groups):
         at = g * BLOCKS_PER_GROUP
-        row_high = jnp.concatenate(
-            [local[at + k : at + k + 1, :] for k in range(BLOCKS_PER_GROUP)], axis=1
+        n0 = g * group_nodes
+        line = lambda a: jnp.concatenate(
+            [a[at + k : at + k + 1, :] for k in range(BLOCKS_PER_GROUP)], axis=1
         )
-        row_low = jnp.concatenate(
-            [low[at + k : at + k + 1, :] for k in range(BLOCKS_PER_GROUP)], axis=1
-        )
-        payload[...] = jnp.concatenate(
+        columns = jnp.concatenate(
             [
                 feats[g],
-                row_high,
-                row_low,
+                line(local),
+                line(low),
                 jnp.zeros((2, group_slots), F32),
                 node_rows,
                 node_rows,
@@ -142,8 +152,7 @@
             ],
             axis=0,
         ).astype(BF16)
-        n0 = g * group_nodes
-        right[...] = jnp.concatenate(
+        terms = jnp.concatenate(
             [
                 edge,
                 jnp.zeros((4, width), F32),
@@ -153,26 +162,20 @@
             ],
             axis=0,
         ).astype(BF16)
+        payload[g] = columns
+        right[g] = terms
+        rows = [rank[at + k : at + k + 1, :] for k in range(BLOCKS_PER_GROUP)]
+        out_ref[n0 : n0 + group_nodes, :] = pooled(rows, 0.0, columns, terms)
+    for g in range(groups):
+        at = g * BLOCKS_PER_GROUP
+        n0 = g * group_nodes
         count = jnp.sum(flag[at : at + BLOCKS_PER_GROUP]).astype(jnp.int32)
 
-        @pl.loop(0, (count + CHUNK - 1) // CHUNK)
+        @pl.loop(1, (count + CHUNK - 1) // CHUNK)
         def _(step):
-            wanted = (iota((CHUNK, LANES), 0) + step * CHUNK).astype(F32)
-            select = jnp.concatenate(
-                [
-                    ones_where(ranks[at + k : at + k + 1, :] == wanted)
-                    for k in range(BLOCKS_PER_GROUP)
-                ],
-                axis=1,
-            )
-            compact = dot_on(select, payload[...], 1, 1)
-            row = (compact[:, 4:5] * float(LANES) + compact[:, 5:6]).astype(jnp.int32)
-            choose = ones_where(row == iota((CHUNK, table_rows), 1))
-            compact = compact.astype(BF16)
-            pre = dot(choose, table_ref[...]) + dot(compact, right[...])
-            act = silu(pre).astype(BF16)
-            out_ref[n0 : n0 + group_nodes, :] += dot_on(
-                compact[:, 8 : 8 + group_nodes], act, 0, 0
+            rows = [ranks[at + k : at + k + 1, :] for k in range(BLOCKS_PER_GROUP)]
+            out_ref[n0 : n0 + group_nodes, :] += pooled(
+                rows, (step * CHUNK).astype(F32), payload[g], right[g]
             )
 
 
@@ -342,7 +345,8 @@
     packed = call(
         functools.partial(pack_body, slab_rows),
         shape((packed_rows, width), BF16),
-        (grid_senders, grid_lengths.reshape(1, nodes), grid_feats, mesh_latent, latent_other),
+        (grid_senders.T, grid_lengths.reshape(1, nodes), grid_feats, mesh_latent, latent_other),
+        scratch=[pltpu.VMEM((nodes, slots), F32)],
     )
     near_packed = lax.ppermute(packed, ("band", "ch"), to_owner)
 
@@ -354,9 +358,9 @@
     table = call(
         embed_body,
         shape((slab_rows, width), BF16),
-        (grid_input, *embed_weights),
+        (grid_input.T, *embed_weights),
         grid=(slab_rows // tile,),
-        in_specs=[pl.BlockSpec((tile, grid_input.shape[1]), lambda i: (i, 0))]
+        in_specs=[pl.BlockSpec((grid_input.shape[1], tile), lambda i: (0, i))]
         + [fixed(w) for w in embed_weights],
         out_specs=pl.BlockSpec((tile, width), lambda i: (i, 0)),
         flops=2 * slab_rows * width * (256 + 2 * width),
@@ -368,9 +372,9 @@
     group_nodes = group_slots // slots
     blocks = nodes * slots // LANES
     scratch = lambda count: [
-        pltpu.VMEM((16 + 2 * group_nodes, group_slots), BF16),
+        pltpu.VMEM((count // BLOCKS_PER_GROUP, 16 + 2 * group_nodes, group_slots), BF16),
         pltpu.VMEM((count, LANES), F32),
-        pltpu.VMEM((16 + 2 * group_nodes, width), BF16),
+        pltpu.VMEM((count // BLOCKS_PER_GROUP, 16 + 2 * group_nodes, width), BF16),
     ]
     own = call(
         functools.partial(own_pool_body, nodes, slots),

time: 60.4 us -> 64.1 us (1.061)
  local copies, waits for them, and re-layouts: 4.09 us -> 8.1 us
  waiting for transfers between devices: 19.3 us -> 17.1 us
  Pallas kernels: 20.6 us -> 22 us
  starting transfers between devices: 15.2 us -> 16 us
    unnamed x42 -> x44, local copies, waits for them, and re-layouts: 3.03 us -> 7.03 us
    ppermute x1, waiting for transfers between devices: 3.16 us -> 0.01 us  [per_device(): near_packed = lax.ppermute(packed, ('band', 'ch'), to_owner)]
    pallas_call x7, Pallas kernels: 20.6 us -> 22 us  [call(): pl.pallas_call(body, out_shape=out_shape, scratch_shapes=list(scratch), c...]
    ppermute x13, waiting for transfers between devices: 2.25 us -> 3.24 us  [per_device(): other = lambda a: lax.ppermute(a, 'ch', [(0, 1), (1, 0)])]
    ppermute x1, starting transfers between devices: 5.06 us -> 5.71 us  [per_device(): near_back = lax.ppermute(near, ('band', 'ch'), to_patch)]
  transfers between devices with their start and end apart: 16 -> 16, of which waited for: 5 -> 5; matrix products, arithmetic and copies ran while one was open for 4% -> 0% of each run, Pallas kernels for 32% -> 32%
where the time goes in v2:
time: 64.1 us; the launch traced here: 63.6 us
  Pallas kernels  22 us (34%)
  waiting for transfers between devices  17.1 us (27%)
  starting transfers between devices  16 us (25%)
  local copies, waits for them, and re-layouts  8.1 us (13%)
    pallas_call x7, Pallas kernels, call(): pl.pallas_call(body, out_shape=out_shape, scratch_shapes=list(scratch), c...  22 us
    all_to_all x1, waiting for transfers between devices, per_device(): piece = lax.all_to_all(spread, 'band', 0, 0, tiled=True)  13.8 us
    unnamed x44, local copies, waits for them, and re-layouts  7.03 us
    all_to_all x1, starting transfers between devices, per_device(): piece = lax.all_to_all(spread, 'band', 0, 0, tiled=True)  5.72 us
    ppermute x1, starting transfers between devices, per_device(): near_back = lax.ppermute(near, ('band', 'ch'), to_patch)  5.71 us
    ppermute x13, starting transfers between devices, per_device(): other = lambda a: lax.ppermute(a, 'ch', [(0, 1), (1, 0)])  3.33 us
    ppermute x13, waiting for transfers between devices, per_device(): other = lambda a: lax.ppermute(a, 'ch', [(0, 1), (1, 0)])  3.24 us
  transfers between devices with their start and end apart: 16, of which 5 were waited for; matrix products, arithmetic and copies ran while one was open for 0% of the time, Pallas kernels for 32%

profile of v2, /device:TPU:0, one launch (start us, length us, event | category | flops | bytes accessed | tf_op | source)
XLA Modules:
  0.0 63.6 jit_solution(5467448266979586006)
XLA Ops:
  0.0 0.5 collective-permute-start.3
  0.5 0.5 collective-permute-start.2
  1.0 0.5 collective-permute-start.5
  1.5 1.0 %collective-permute-done.other_ref = bf16[128,256]{1,0:T(8,128)(2,1)S(1)} collective-permute-done((bf16[128,256]{1,0:T(8,128)(2,1)}, bf16[128,256]{1,0:T(8,128)(2,1)S(1)}, u32[]{:S(2)}, u32[]{:S(2)}) %collective-permute-start) | collective-permute-done | bytes 65568 | tf_op jit(solution)/shard_map/ppermute | solution.py:336
  2.5 0.4 collective-permute-start.6
  2.8 0.8 %copy-done.6 = bf16[128,256]{1,0:T(8,128)(2,1)S(1)} copy-done((bf16[128,256]{1,0:T(8,128)(2,1)S(1)}, bf16[128,256]{1,0:T(8,128)(2,1)}, u32[]{:S(2)}) %copy-start.6) | copy-done | bytes 65560
  3.7 0.8 %copy-done.7 = bf16[4,4096]{1,0:T(4,128)(2,1)S(1)} copy-done((bf16[4,4096]{1,0:T(4,128)(2,1)S(1)}, bf16[4,4096]{1,0:T(4,128)(2,1)}, u32[]{:S(2)}) %copy-start.7) | copy-done | bytes 32792
  4.4 0.7 %copy-done.8 = s32[128,32]{0,1:T(8,128)S(1)} copy-done((s32[128,32]{0,1:T(8,128)S(1)}, s32[128,32]{0,1:T(8,128)}, u32[]{:S(2)}) %copy-start.8) | copy-done | bytes 16408
  5.2 0.7 %copy-done.12 = s32[128]{0:T(128)S(1)} copy-done((s32[128]{0:T(128)S(1)}, s32[128]{0:T(128)}, u32[]{:S(2)}) %copy-start.12) | copy-done | bytes 536
  5.8 0.2 shard_map.208.packed_ref
  6.0 0.2 collective-permute-start.10
  6.2 1.3 %collective-permute-start.1 = (bf16[192,512]{1,0:T(8,128)(2,1)S(1)}, bf16[192,512]{1,0:T(8,128)(2,1)S(1)}, u32[]{:S(2)}, u32[]{:S(2)}) collective-permute-start(bf16[192,512]{1,0:T(8,128)(2,1)S(1)} %shard_map.208.packed_ref), channel_id=1, source_target_pairs={{2,0},{4,2},{6,4},{8,6},{10,8},{12,10},{14,12},{1,3},{3,5},{5,7},{... | collective-permute-start | bytes 589832 | tf_op jit(solution)/shard_map/ppermute | solution.py:351
  7.6 1.2 %copy-done.13 = bf16[2048,227]{0,1:T(8,128)(2,1)S(1)} copy-done((bf16[2048,227]{0,1:T(8,128)(2,1)S(1)}, bf16[2048,227]{0,1:T(8,128)(2,1)}, u32[]{:S(2)}) %copy-start.13) | copy-done | bytes 929816
  8.7 0.9 %copy-done.14 = bf16[256,512]{1,0:T(8,128)(2,1)S(1)} copy-done((bf16[256,512]{1,0:T(8,128)(2,1)S(1)}, bf16[256,512]{1,0:T(8,128)(2,1)}, u32[]{:S(2)}) %copy-start.14) | copy-done | bytes 262168
  9.7 0.9 %copy-done.15 = bf16[512,256]{1,0:T(8,128)(2,1)S(1)} copy-done((bf16[512,256]{1,0:T(8,128)(2,1)S(1)}, bf16[512,256]{1,0:T(8,128)(2,1)}, u32[]{:S(2)}) %copy-start.15) | copy-done | bytes 262168
  10.6 0.9 %copy-done.17 = bf16[227,256]{1,0:T(8,128)(2,1)S(1)} copy-done((bf16[227,256]{1,0:T(8,128)(2,1)S(1)}, bf16[227,256]{1,0:T(8,128)(2,1)}, u32[]{:S(2)}) %copy-start.17) | copy-done | bytes 116248
  11.5 3.8 %shard_map.209.table_ref = bf16[2048,512]{1,0:T(8,128)(2,1)S(1)} custom-call(bf16[227,2048]{1,0:T(8,128)(2,1)S(1)} %bitcast.10, bf16[227,256]{1,0:T(8,128)(2,1)S(1)} %copy-done.17, bf16[227,256]{1,0:T(8,128)(2,1)S(1)} %collective-permute-done.2.f_oth, bf16[256,512]{1,0:T(8,128)(2,1)S(1)} %copy-done.14, bf16[256,512]{1,0:T(8,128)(2,1)S(1)} %collective-permute-done.3.s_oth, ...), custom_call_target="tpu_custom_call" | custom-call | flops 2684354560 | bytes 4194304 | tf_op jit(solution)/shard_map/pallas_call | solution.py:43
  15.4 8.1 %shard_map.210 = bf16[128,512]{1,0:T(8,128)(2,1)S(1)} custom-call(bf16[192,512]{1,0:T(8,128)(2,1)S(1)} %collective-permute-done.1.packed_ref, bf16[2048,512]{1,0:T(8,128)(2,1)S(1)} %shard_map.209.table_ref, bf16[512,256]{1,0:T(8,128)(2,1)S(1)} %copy-done.16, bf16[512,256]{1,0:T(8,128)(2,1)S(1)} %collective-permute-done.5.lr_oth, ...), custom_call_target="tpu_custom_call" | custom-call | flops 4000000000 | bytes 4194304 | tf_op jit(solution)/shard_map/pallas_call | solution.py:43
  23.6 5.7 %collective-permute-start.7 = (bf16[128,512]{1,0:T(8,128)(2,1)S(1)}, bf16[128,512]{1,0:T(8,128)(2,1)S(1)}, u32[]{:S(2)}, u32[]{:S(2)}) collective-permute-start(bf16[128,512]{1,0:T(8,128)(2,1)S(1)} %shard_map.210), channel_id=1, source_target_pairs={{0,2},{2,4},{4,6},{6,8},{8,10},{10,12},{12,14},{3,1},{5,3},{7,5},{... | collective-permute-start | bytes 393224 | tf_op jit(solution)/shard_map/ppermute | solution.py:396
  29.3 7.6 %shard_map.211.own_ref = f32[64,512]{1,0:T(8,128)S(1)} custom-call(bf16[192,512]{1,0:T(8,128)(2,1)S(1)} %shard_map.208.packed_ref, bf16[2048,512]{1,0:T(8,128)(2,1)S(1)} %shard_map.209.table_ref, bf16[512,256]{1,0:T(8,128)(2,1)S(1)} %copy-done.16, bf16[512,256]{1,0:T(8,128)(2,1)S(1)} %collective-permute-done.5.lr_oth, bf16[4,256]{1,0:T(4,128)(2,1)S(1)} %copy-done.18, ...), custom_call_target="tpu_custom_call" | custom-call | flops 4000000000 | bytes 4194304 | tf_op jit(solution)/shard_map/pallas_call | solution.py:43
  37.1 0.5 collective-permute-start.8
  37.6 0.8 %collective-permute-done.9.own_oth_ref = f32[64,512]{1,0:T(8,128)S(1)} collective-permute-done((f32[64,512]{1,0:T(8,128)S(1)}, f32[64,512]{1,0:T(8,128)S(1)}, u32[]{:S(2)}, u32[]{:S(2)}) %collective-permute-start.9) | collective-permute-done | bytes 131104 | tf_op jit(solution)/shard_map/ppermute | solution.py:336
  38.4 0.2 collective-permute-done.8.near_oth_ref
  38.6 0.4 shard_map.212
  39.0 0.8 %broadcast_in_dim.2 = bf16[8,128,256]{2,1,0:T(8,128)(2,1)} broadcast(bf16[128,256]{1,0:T(8,128)(2,1)S(1)} %get-tuple-element.9), dimensions={1,2} | broadcast | bytes 589824 | tf_op jit(solution)/shard_map/broadcast_in_dim | solution.py:404
  39.8 5.7 %all-to-all-start = ((bf16[8,128,256]{2,1,0:T(8,128)(2,1)}), bf16[8,128,256]{2,1,0:T(8,128)(2,1)S(1)}, u32[]{:S(2)}, u32[]{:S(2)}) async-start(bf16[8,128,256]{2,1,0:T(8,128)(2,1)} %broadcast_in_dim.2), calls=%async_computation | async-start | bytes 1048576 | tf_op jit(solution)/shard_map/all_to_all | solution.py:405
  45.7 0.5 collective-permute-start.12
  46.1 0.1 collective-permute-start.14
  46.6 13.8 %all-to-all-done = bf16[8,128,256]{2,1,0:T(8,128)(2,1)S(1)} async-done(((bf16[8,128,256]{2,1,0:T(8,128)(2,1)}), bf16[8,128,256]{2,1,0:T(8,128)(2,1)S(1)}, u32[]{:S(2)}, u32[]{:S(2)}) %all-to-all-start) | async-done | bytes 524320 | tf_op jit(solution)/shard_map/all_to_all | solution.py:405
  60.4 0.5 shard_map.213.pool_ref
  61.0 1.2 %collective-permute-done.11.pool_oth_ref = bf16[128,256]{1,0:T(8,128)(2,1)S(1)} collective-permute-done((bf16[128,256]{1,0:T(8,128)(2,1)S(1)}, bf16[128,256]{1,0:T(8,128)(2,1)S(1)}, u32[]{:S(2)}, u32[]{:S(2)}) %collective-permute-start.11) | collective-permute-done | bytes 65568 | tf_op jit(solution)/shard_map/ppermute | solution.py:336
  62.2 1.4 %shard_map.214 = bf16[128,256]{1,0:T(8,128)(2,1)} custom-call(bf16[128,512]{1,0:T(8,128)(2,1)S(1)} %get-tuple-element.8.mid_ref, bf16[128,256]{1,0:T(8,128)(2,1)S(1)} %shard_map.213.pool_ref, bf16[128,256]{1,0:T(8,128)(2,1)S(1)} %collective-permute-done.11.pool_oth_ref, bf16[256,512]{1,0:T(8,128)(2,1)S(1)} %copy-done.4, ...), custom_call_target="tpu_custom_call" | custom-call | tf_op jit(solution)/shard_map/pallas_call | solution.py:43
  (56 shorter events, 0.8 us)
Async XLA Ops:
  0.0 6.2 %collective-permute-start.3 = (bf16[256,512]{1,0:T(8,128)(2,1)}, bf16[256,512]{1,0:T(8,128)(2,1)S(1)}, u32[]{:S(2)}, u32[]{:S(2)}) collective-permute-start(bf16[256,512]{1,0:T(8,128)(2,1)} %s_own.1), channel_id=1, source_target_pairs={{0,1},{1,0},{2,3},{3,2},{4,5},{5,4},{6,7},{7,6},{8,9},{9,8},{10,11... | collective-permute-start | bytes 786440 | tf_op jit(solution)/shard_map/ppermute | solution.py:336
  0.5 7.1 %collective-permute-start.4 = (bf16[512,256]{1,0:T(8,128)(2,1)}, bf16[512,256]{1,0:T(8,128)(2,1)S(1)}, u32[]{:S(2)}, u32[]{:S(2)}) collective-permute-start(bf16[512,256]{1,0:T(8,128)(2,1)} %l_own.1), channel_id=1, source_target_pairs={{0,1},{1,0},{2,3},{3,2},{4,5},{5,4},{6,7},{7,6},{8,9},{9,8},{10,11... | collective-permute-start | bytes 786440 | tf_op jit(solution)/shard_map/ppermute | solution.py:336
  0.5 5.5 %collective-permute-start.2 = (bf16[227,256]{1,0:T(8,128)(2,1)}, bf16[227,256]{1,0:T(8,128)(2,1)S(1)}, u32[]{:S(2)}, u32[]{:S(2)}) collective-permute-start(bf16[227,256]{1,0:T(8,128)(2,1)} %f_own.1), channel_id=1, source_target_pairs={{0,1},{1,0},{2,3},{3,2},{4,5},{5,4},{6,7},{7,6},{8,9},{9,8},{10,11... | collective-permute-start | bytes 348680 | tf_op jit(solution)/shard_map/ppermute | solution.py:336
  1.0 1.5 %collective-permute-start = (bf16[128,256]{1,0:T(8,128)(2,1)}, bf16[128,256]{1,0:T(8,128)(2,1)S(1)}, u32[]{:S(2)}, u32[]{:S(2)}) collective-permute-start(bf16[128,256]{1,0:T(8,128)(2,1)} %own_ref.1), channel_id=1, source_target_pairs={{0,1},{1,0},{2,3},{3,2},{4,5},{5,4},{6,7},{7,6},{8,9},{9,8},{10,11... | collective-permute-start | bytes 196616 | tf_op jit(solution)/shard_map/ppermute | solution.py:336
  1.0 14.4 %collective-permute-start.5 = (bf16[512,256]{1,0:T(8,128)(2,1)}, bf16[512,256]{1,0:T(8,128)(2,1)S(1)}, u32[]{:S(2)}, u32[]{:S(2)}) collective-permute-start(bf16[512,256]{1,0:T(8,128)(2,1)} %lr_own.3), channel_id=1, source_target_pairs={{0,1},{1,0},{2,3},{3,2},{4,5},{5,4},{6,7},{7,6},{8,9},{9,8},{10,11... | collective-permute-start | bytes 786440 | tf_op jit(solution)/shard_map/ppermute | solution.py:336
  2.5 12.9 %collective-permute-start.6 = (bf16[4,256]{1,0:T(4,128)(2,1)}, bf16[4,256]{1,0:T(4,128)(2,1)S(1)}, u32[]{:S(2)}, u32[]{:S(2)}) collective-permute-start(bf16[4,256]{1,0:T(4,128)(2,1)} %le_own.3), channel_id=1, source_target_pairs={{0,1},{1,0},{2,3},{3,2},{4,5},{5,4},{6,7},{7,6},{8,9},{9,8},{10,11... | collective-permute-start | bytes 6152 | tf_op jit(solution)/shard_map/ppermute | solution.py:336
  6.0 31.5 %collective-permute-start.10 = (bf16[256,512]{1,0:T(8,128)(2,1)}, bf16[256,512]{1,0:T(8,128)(2,1)S(1)}, u32[]{:S(2)}, u32[]{:S(2)}) collective-permute-start(bf16[256,512]{1,0:T(8,128)(2,1)} %lo_own.1), channel_id=1, source_target_pairs={{0,1},{1,0},{2,3},{3,2},{4,5},{5,4},{6,7},{7,6},{8,9},{9,8},{10,11... | collective-permute-start | bytes 786440 | tf_op jit(solution)/shard_map/ppermute | solution.py:336
  6.2 9.1 %collective-permute-start.1 = (bf16[192,512]{1,0:T(8,128)(2,1)S(1)}, bf16[192,512]{1,0:T(8,128)(2,1)S(1)}, u32[]{:S(2)}, u32[]{:S(2)}) collective-permute-start(bf16[192,512]{1,0:T(8,128)(2,1)S(1)} %shard_map.208.packed_ref), channel_id=1, source_target_pairs={{2,0},{4,2},{6,4},{8,6},{10,8},{12,10},{14,12},{1,3},{3,5},{5,7},{... | collective-permute-start | bytes 589832 | tf_op jit(solution)/shard_map/ppermute | solution.py:351
  7.5 1.2 %copy-start.13 = (bf16[2048,227]{0,1:T(8,128)(2,1)S(1)}, bf16[2048,227]{0,1:T(8,128)(2,1)}, u32[]{:S(2)}) copy-start(bf16[2048,227]{0,1:T(8,128)(2,1)} %param.22) | copy-start | bytes 2789380
  8.7 0.9 %copy-start.14 = (bf16[256,512]{1,0:T(8,128)(2,1)S(1)}, bf16[256,512]{1,0:T(8,128)(2,1)}, u32[]{:S(2)}) copy-start(bf16[256,512]{1,0:T(8,128)(2,1)} %s_own.1) | copy-start | bytes 786436
  11.5 3.9 %copy-start.16 = (bf16[512,256]{1,0:T(8,128)(2,1)S(1)}, bf16[512,256]{1,0:T(8,128)(2,1)}, u32[]{:S(2)}) copy-start(bf16[512,256]{1,0:T(8,128)(2,1)} %lr_own.3) | copy-start | bytes 786436
  11.5 3.9 %copy-start.18 = (bf16[4,256]{1,0:T(4,128)(2,1)S(1)}, bf16[4,256]{1,0:T(4,128)(2,1)}, u32[]{:S(2)}) copy-start(bf16[4,256]{1,0:T(4,128)(2,1)} %le_own.3) | copy-start | bytes 6148
  23.5 15.0 %copy-start.1 = (bf16[256,512]{1,0:T(8,128)(2,1)S(1)}, bf16[256,512]{1,0:T(8,128)(2,1)}, u32[]{:S(2)}) copy-start(bf16[256,512]{1,0:T(8,128)(2,1)} %lo_own.1) | copy-start | bytes 786436
  23.6 15.0 %copy-start.2 = (bf16[512,256]{1,0:T(8,128)(2,1)S(1)}, bf16[512,256]{1,0:T(8,128)(2,1)}, u32[]{:S(2)}) copy-start(bf16[512,256]{1,0:T(8,128)(2,1)} %ps.1) | copy-start | bytes 786436
  23.6 15.0 %copy-start.3 = (bf16[512,256]{1,0:T(8,128)(2,1)S(1)}, bf16[512,256]{1,0:T(8,128)(2,1)}, u32[]{:S(2)}) copy-start(bf16[512,256]{1,0:T(8,128)(2,1)} %pr.1) | copy-start | bytes 786436
  23.6 13.5 %collective-permute-start.7 = (bf16[128,512]{1,0:T(8,128)(2,1)S(1)}, bf16[128,512]{1,0:T(8,128)(2,1)S(1)}, u32[]{:S(2)}, u32[]{:S(2)}) collective-permute-start(bf16[128,512]{1,0:T(8,128)(2,1)S(1)} %shard_map.210), channel_id=1, source_target_pairs={{0,2},{2,4},{4,6},{6,8},{8,10},{10,12},{12,14},{3,1},{5,3},{7,5},{... | collective-permute-start | bytes 393224 | tf_op jit(solution)/shard_map/ppermute | solution.py:396
  36.9 8.7 %copy-start = (bf16[1024,256]{1,0:T(8,128)(2,1)S(1)}, bf16[1024,256]{1,0:T(8,128)(2,1)}, u32[]{:S(2)}) copy-start(bf16[1024,256]{1,0:T(8,128)(2,1)} %nf_own.1) | copy-start | bytes 1572868
  36.9 8.8 %copy-start.4 = (bf16[256,512]{1,0:T(8,128)(2,1)S(1)}, bf16[256,512]{1,0:T(8,128)(2,1)}, u32[]{:S(2)}) copy-start(bf16[256,512]{1,0:T(8,128)(2,1)} %po_own.1) | copy-start | bytes 786436
  36.9 9.2 %copy-start.5 = (bf16[256,512]{1,0:T(8,128)(2,1)S(1)}, bf16[256,512]{1,0:T(8,128)(2,1)}, u32[]{:S(2)}) copy-start(bf16[256,512]{1,0:T(8,128)(2,1)} %ns_own.1) | copy-start | bytes 786436
  36.9 9.3 %copy-start.21 = (s32[1,8]{1,0:T(1,128)S(1)}, s32[1,8]{1,0:T(1,128)}, u32[]{:S(2)}) copy-start(s32[1,8]{1,0:T(1,128)} %param.29) | copy-start | bytes 100
  36.9 9.5 %copy-start.19 = (s32[8,16]{1,0:T(8,128)S(1)}, s32[8,16]{1,0:T(8,128)}, u32[]{:S(2)}) copy-start(s32[8,16]{1,0:T(8,128)} %param.27) | copy-start | bytes 1540
  36.9 9.5 %copy-start.20 = (s32[8,16]{1,0:T(8,128)S(1)}, s32[8,16]{1,0:T(8,128)}, u32[]{:S(2)}) copy-start(s32[8,16]{1,0:T(8,128)} %param.28) | copy-start | bytes 1540
  36.9 23.5 %copy-start.9 = (bf16[4,256]{1,0:T(4,128)(2,1)S(1)}, bf16[4,256]{1,0:T(4,128)(2,1)}, u32[]{:S(2)}) copy-start(bf16[4,256]{1,0:T(4,128)(2,1)} %pe.1) | copy-start | bytes 6148
  37.0 23.4 %copy-start.10 = (bf16[4,128]{1,0:T(4,128)(2,1)S(1)}, bf16[4,128]{1,0:T(4,128)(2,1)}, u32[]{:S(2)}) copy-start(bf16[4,128]{1,0:T(4,128)(2,1)} %feats_ref.3) | copy-start | bytes 3076
  37.0 25.2 %copy-start.11 = (f32[256]{0:T(256)S(1)}, f32[256]{0:T(256)}, u32[]{:S(2)}) copy-start(f32[256]{0:T(256)} %param.43) | copy-start | bytes 3076
  37.0 1.4 %collective-permute-start.9 = (f32[64,512]{1,0:T(8,128)S(1)}, f32[64,512]{1,0:T(8,128)S(1)}, u32[]{:S(2)}, u32[]{:S(2)}) collective-permute-start(f32[64,512]{1,0:T(8,128)S(1)} %shard_map.211.own_ref), channel_id=1, source_target_pairs={{0,1},{1,0},{2,3},{3,2},{4,5},{5,4},{6,7},{7,6},{8,9},{9,8},{10,11... | collective-permute-start | bytes 393224 | tf_op jit(solution)/shard_map/ppermute | solution.py:336
  37.1 1.5 %collective-permute-start.8 = (bf16[128,512]{1,0:T(8,128)(2,1)S(1)}, bf16[128,512]{1,0:T(8,128)(2,1)S(1)}, u32[]{:S(2)}, u32[]{:S(2)}) collective-permute-start(bf16[128,512]{1,0:T(8,128)(2,1)S(1)} %collective-permute-done.7.near_ref), channel_id=1, source_target_pairs={{0,1},{1,0},{2,3},{3,2},{4,5},{5,4},{6,7},{7,6},{8,9},{9,8},{10,11... | collective-permute-start | bytes 393224 | tf_op jit(solution)/shard_map/ppermute | solution.py:336
  39.8 20.6 %all-to-all-start = ((bf16[8,128,256]{2,1,0:T(8,128)(2,1)}), bf16[8,128,256]{2,1,0:T(8,128)(2,1)S(1)}, u32[]{:S(2)}, u32[]{:S(2)}) async-start(bf16[8,128,256]{2,1,0:T(8,128)(2,1)} %broadcast_in_dim.2), calls=%async_computation | async-start | bytes 1048576 | tf_op jit(solution)/shard_map/all_to_all | solution.py:405
  45.6 15.4 %collective-permute-start.13 = (bf16[1024,256]{1,0:T(8,128)(2,1)S(1)}, bf16[1024,256]{1,0:T(8,128)(2,1)S(1)}, u32[]{:S(2)}, u32[]{:S(2)}) collective-permute-start(bf16[1024,256]{1,0:T(8,128)(2,1)S(1)} %copy-done), channel_id=1, source_target_pairs={{0,1},{1,0},{2,3},{3,2},{4,5},{5,4},{6,7},{7,6},{8,9},{9,8},{10,11... | collective-permute-start | bytes 1572872 | tf_op jit(solution)/shard_map/ppermute | solution.py:336
  45.7 15.3 %collective-permute-start.12 = (bf16[256,512]{1,0:T(8,128)(2,1)S(1)}, bf16[256,512]{1,0:T(8,128)(2,1)S(1)}, u32[]{:S(2)}, u32[]{:S(2)}) collective-permute-start(bf16[256,512]{1,0:T(8,128)(2,1)S(1)} %copy-done.4), channel_id=1, source_target_pairs={{0,1},{1,0},{2,3},{3,2},{4,5},{5,4},{6,7},{7,6},{8,9},{9,8},{10,11... | collective-permute-start | bytes 786440 | tf_op jit(solution)/shard_map/ppermute | solution.py:336
  46.1 14.8 %collective-permute-start.14 = (bf16[256,512]{1,0:T(8,128)(2,1)S(1)}, bf16[256,512]{1,0:T(8,128)(2,1)S(1)}, u32[]{:S(2)}, u32[]{:S(2)}) collective-permute-start(bf16[256,512]{1,0:T(8,128)(2,1)S(1)} %copy-done.5), channel_id=1, source_target_pairs={{0,1},{1,0},{2,3},{3,2},{4,5},{5,4},{6,7},{7,6},{8,9},{9,8},{10,11... | collective-permute-start | bytes 786440 | tf_op jit(solution)/shard_map/ppermute | solution.py:336
  60.9 1.3 %collective-permute-start.11 = (bf16[128,256]{1,0:T(8,128)(2,1)S(1)}, bf16[128,256]{1,0:T(8,128)(2,1)S(1)}, u32[]{:S(2)}, u32[]{:S(2)}) collective-permute-start(bf16[128,256]{1,0:T(8,128)(2,1)S(1)} %shard_map.213.pool_ref), channel_id=1, source_target_pairs={{0,1},{1,0},{2,3},{3,2},{4,5},{5,4},{6,7},{7,6},{8,9},{9,8},{10,11... | collective-permute-start | bytes 196616 | tf_op jit(solution)/shard_map/ppermute | solution.py:336
  (6 other events, 4.8 us)

commit v3 on v2

--- a/solution.py
+++ b/solution.py
@@ -10,7 +10,8 @@
 F32 = jnp.float32
 BF16 = jnp.bfloat16
 LANES = 128
-CHUNK = 288
+CHUNK = 256
+PAYLOAD_ROWS = 16
 BLOCKS_PER_GROUP = 8
 VMEM_LIMIT = 48 * 1024 * 1024
 
@@ -50,7 +51,13 @@
     )(*args)
 
 
-def pack_body(slab_rows, senders_ref, lengths_ref, feats_ref, own_ref, other_ref, out_ref, turned):
+def pack_body(slab_rows, senders_hbm, lengths_hbm, feats_hbm, own_hbm, other_ref, out_ref, senders_ref, lengths_ref, feats_ref, own_ref, turned, sems):
+    copies = fetch(
+        [(senders_hbm, senders_ref), (lengths_hbm, lengths_ref), (feats_hbm, feats_ref), (own_hbm, own_ref)],
+        sems,
+    )
+    for c in copies:
+        c.wait()
     band = lax.axis_index("band")
     core = lax.axis_index("ch")
     slots, nodes = senders_ref.shape
@@ -83,60 +90,95 @@
     out_ref[nodes:, :] = tail.astype(BF16)
 
 
-def embed_body(x_ref, f_own, f_oth, s_own, s_oth, l_own, l_oth, out_ref):
-    x = x_ref[...]
-    half = f_own.shape[1]
-    hidden_own = silu(dot_on(x, f_own[...], 0, 0)).astype(BF16)
-    hidden_oth = silu(dot_on(x, f_oth[...], 0, 0)).astype(BF16)
-    latent = (dot(hidden_own, s_own[...]) + dot(hidden_oth, s_oth[...])).astype(BF16)
-    out_ref[:, :half] = dot(latent, l_own[...]).astype(BF16)
-    out_ref[:, half:] = dot(latent, l_oth[...]).astype(BF16)
-
-
-def pool_part(high, low, feats, latent, kind, slots, table_ref, weights, payload, ranks, right, out_ref):
+def fetch(moves, sems):
+    copies = [pltpu.make_async_copy(src, dst, sems.at[k]) for k, (src, dst) in enumerate(moves)]
+    for c in copies:
+        c.start()
+    return copies
+
+
+def embed_body(tile, x_hbm, f_hbm, s_hbm, l_hbm, f_oth, s_oth, l_oth, out_ref, x_ref, f_own, s_own, l_own, first_t, second_t, third_t, sems):
+    half = f_oth.shape[1]
+    tiles = x_ref.shape[1] // tile
+    moves = [(f_hbm, f_own), (s_hbm, s_own), (l_hbm, l_own)]
+    moves += [
+        (x_hbm.at[:, pl.ds(k * tile, tile)], x_ref.at[:, pl.ds(k * tile, tile)]) for k in range(tiles)
+    ]
+    copies = fetch(moves, sems)
+    first_t[half:, :] = f_oth[...].T
+    second_t[:, half:] = s_oth[...].T
+    third_t[half:, :] = l_oth[...].T
+    for c in copies[:3]:
+        c.wait()
+    first_t[:half, :] = f_own[...].T
+    second_t[:, :half] = s_own[...].T
+    third_t[:half, :] = l_own[...].T
+    for c in copies[3:]:
+        c.wait()
+
+    @pl.loop(0, tiles)
+    def _(k):
+        at = pl.ds(pl.multiple_of(k * tile, tile), tile)
+        hidden = silu(dot(first_t[...], x_ref[:, at])).astype(BF16)
+        latent = dot(second_t[...], hidden).astype(BF16)
+        out_ref[:, at] = dot(third_t[...], latent).astype(BF16)
+
+
+def running(flag16, together):
+    blocks = flag16.shape[0]
+    inclusive = dot(flag16, ones_where(iota((LANES, LANES), 0) <= iota((LANES, LANES), 1)))
+    square = (blocks, blocks)
+    earlier = iota(square, 1) < iota(square, 0)
+    earlier &= iota(square, 1) // together == iota(square, 0) // together
+    return inclusive + jnp.sum(dot(ones_where(earlier), flag16), axis=1, keepdims=True)
+
+
+def pool_part(high, low, feats, latent, kind, slots, table_ref, weights, payload, late, right, out_ref):
     lr_own, lr_oth, le_own, le_oth = weights
     blocks = high.shape[0]
     nodes = latent.shape[0]
     groups = blocks // BLOCKS_PER_GROUP
     group_nodes = nodes // groups
     group_slots = BLOCKS_PER_GROUP * LANES
-    table_rows, width = table_ref.shape
+    width, table_rows = table_ref.shape
     per_slab = table_rows // LANES
     recv = jnp.concatenate([dot(latent, lr_own[...]), dot(latent, lr_oth[...])], axis=1)
-    recv_high = recv.astype(BF16).astype(F32)
-    recv_low = recv - recv_high
     edge = jnp.concatenate([le_own[...], le_oth[...]], axis=1).astype(F32)
+    right[0:nodes, :] = recv.astype(BF16)
+    right[nodes:, :] = jnp.concatenate(
+        [edge, jnp.zeros((PAYLOAD_ROWS - edge.shape[0], width), F32)], axis=0
+    ).astype(BF16)
     base = (kind * per_slab + 1).astype(F32)
     local = high - base
     valid = (local >= 0.0) & (local < float(per_slab))
     flag = jnp.where(valid, 1.0, 0.0)
-    flag16 = flag.astype(BF16)
-    inclusive = dot(flag16, ones_where(iota((LANES, LANES), 0) <= iota((LANES, LANES), 1)))
-    square = (blocks, blocks)
-    ahead = ones_where(
-        (iota(square, 1) < iota(square, 0))
-        & (iota(square, 1) // BLOCKS_PER_GROUP == iota(square, 0) // BLOCKS_PER_GROUP)
-    )
-    offset = jnp.sum(dot(ahead, flag16), axis=1, keepdims=True)
-    rank = jnp.where(valid, inclusive - flag + offset, -1.0)
-    ranks[...] = rank
-    node_rows = jnp.where(
-        iota((group_nodes, group_slots), 1) // slots == iota((group_nodes, group_slots), 0), 1.0, 0.0
-    )
-
-    def pooled(rank_rows, start, columns, terms):
-        wanted = iota((CHUNK, LANES), 0).astype(F32) + start
-        select = jnp.concatenate([ones_where(r == wanted) for r in rank_rows], axis=1)
-        compact = dot_on(select, columns, 1, 1)
-        row = (compact[:, 4:5] * float(LANES) + compact[:, 5:6]).astype(jnp.int32)
-        choose = ones_where(row == iota((CHUNK, table_rows), 1))
-        compact = compact.astype(BF16)
-        pre = dot(choose, table_ref[...]) + dot(compact, terms)
-        return dot_on(compact[:, 8 : 8 + group_nodes], silu(pre).astype(BF16), 0, 0)
-
+    rank = running(flag.astype(BF16), BLOCKS_PER_GROUP) - 1.0
+    over = valid & (rank >= float(CHUNK))
+    over_flag = jnp.where(over, 1.0, 0.0)
+    late[...] = jnp.where(over, running(over_flag.astype(BF16), blocks) - 1.0, -1.0)
+    rank = jnp.where(valid, rank, -1.0)
+    spot = iota((1, group_slots), 1) // slots
+    place = iota((CHUNK, LANES), 0).astype(F32)
+
+    def picked(rows, start, columns):
+        select = jnp.concatenate([ones_where(r == place + start) for r in rows], axis=1)
+        return dot_on(columns, select, 1, 1)
+
+    def pooled(compact):
+        count = compact.shape[1]
+        own_node = ones_where(iota((nodes, count), 0).astype(F32) + 1.0 == compact[6:7, :])
+        one_low = ones_where(iota((LANES, count), 0).astype(F32) == compact[5:6, :])
+        row_high = compact[4:5, :]
+        choose = jnp.concatenate(
+            [one_low * ones_where(row_high == float(k)) for k in range(per_slab)], axis=0
+        )
+        terms = jnp.concatenate([own_node, compact.astype(BF16)], axis=0)
+        pre = dot(table_ref[...], choose) + dot_on(right[...], terms, 0, 0)
+        return dot_on(silu(pre).astype(BF16), own_node, 1, 1)
+
+    parts = []
     for g in range(groups):
         at = g * BLOCKS_PER_GROUP
-        n0 = g * group_nodes
         line = lambda a: jnp.concatenate(
             [a[at + k : at + k + 1, :] for k in range(BLOCKS_PER_GROUP)], axis=1
         )
@@ -145,38 +187,27 @@
                 feats[g],
                 line(local),
                 line(low),
-                jnp.zeros((2, group_slots), F32),
-                node_rows,
-                node_rows,
-                jnp.zeros((8, group_slots), F32),
-            ],
-            axis=0,
-        ).astype(BF16)
-        terms = jnp.concatenate(
-            [
-                edge,
-                jnp.zeros((4, width), F32),
-                recv_high[n0 : n0 + group_nodes],
-                recv_low[n0 : n0 + group_nodes],
-                jnp.zeros((8, width), F32),
+                (spot + g * group_nodes + 1).astype(F32),
+                jnp.zeros((PAYLOAD_ROWS - 7, group_slots), F32),
             ],
             axis=0,
         ).astype(BF16)
         payload[g] = columns
-        right[g] = terms
         rows = [rank[at + k : at + k + 1, :] for k in range(BLOCKS_PER_GROUP)]
-        out_ref[n0 : n0 + group_nodes, :] = pooled(rows, 0.0, columns, terms)
-    for g in range(groups):
-        at = g * BLOCKS_PER_GROUP
-        n0 = g * group_nodes
-        count = jnp.sum(flag[at : at + BLOCKS_PER_GROUP]).astype(jnp.int32)
-
-        @pl.loop(1, (count + CHUNK - 1) // CHUNK)
-        def _(step):
-            rows = [ranks[at + k : at + k + 1, :] for k in range(BLOCKS_PER_GROUP)]
-            out_ref[n0 : n0 + group_nodes, :] += pooled(
-                rows, (step * CHUNK).astype(F32), payload[g], right[g]
-            )
+        parts.append(picked(rows, 0.0, columns))
+    out_ref[...] = pooled(jnp.concatenate(parts, axis=1))
+    count = jnp.sum(over_flag).astype(jnp.int32)
+
+    @pl.loop(0, (count + CHUNK - 1) // CHUNK)
+    def _(step):
+        start = (step * CHUNK).astype(F32)
+        total = None
+        for g in range(groups):
+            at = g * BLOCKS_PER_GROUP
+            rows = [late[at + k : at + k + 1, :] for k in range(BLOCKS_PER_GROUP)]
+            term = picked(rows, start, payload[g])
+            total = term if total is None else total + term
+        out_ref[...] += pooled(total)
 
 
 def unpack(packed_ref, nodes, slots):
@@ -194,7 +225,7 @@
     return high, low, feats
 
 
-def own_pool_body(nodes, slots, packed_ref, table_ref, lr_own, lr_oth, le_own, le_oth, out_ref, payload, ranks, right):
+def own_pool_body(nodes, slots, packed_ref, table_ref, lr_own, lr_oth, le_own, le_oth, out_ref, payload, late, right):
     first = lax.axis_index("ch") == 0
     high, low, feats = unpack(packed_ref, nodes, slots)
     half_blocks = high.shape[0] // 2
@@ -211,13 +242,13 @@
         table_ref,
         (lr_own, lr_oth, le_own, le_oth),
         payload,
-        ranks,
+        late,
         right,
         out_ref,
     )
 
 
-def near_pool_body(nodes, slots, packed_ref, table_ref, lr_own, lr_oth, le_own, le_oth, out_ref, payload, ranks, right, total):
+def near_pool_body(nodes, slots, packed_ref, table_ref, lr_own, lr_oth, le_own, le_oth, out_ref, payload, late, right, total):
     high, low, feats = unpack(packed_ref, nodes, slots)
     kind = 2 * lax.axis_index("ch")
     pool_part(
@@ -230,7 +261,7 @@
         table_ref,
         (lr_own, lr_oth, le_own, le_oth),
         payload,
-        ranks,
+        late,
         right,
         total,
     )
@@ -240,15 +271,15 @@
 def middle_body(packed_ref, near_ref, near_oth_ref, own_ref, own_oth_ref, lo_own, lo_oth, ps, pr, mid_ref, send_ref, recv_ref):
     first = lax.axis_index("ch") == 0
     half = lo_own.shape[0]
-    nodes = near_ref.shape[0]
+    nodes = near_ref.shape[1]
     mine, theirs = own_ref[...], own_oth_ref[...]
-    flip = lambda a: jnp.concatenate([a[:, half:], a[:, :half]], axis=1)
+    flip = lambda a: jnp.concatenate([a[half:, :], a[:half, :]], axis=0)
     theirs = flip(theirs)
     total = near_ref[...].astype(F32) + flip(near_oth_ref[...]).astype(F32)
     total = total + jnp.concatenate(
-        [jnp.where(first, mine, theirs), jnp.where(first, theirs, mine)], axis=0
-    )
-    pool = total.astype(BF16)
+        [jnp.where(first, mine, theirs), jnp.where(first, theirs, mine)], axis=1
+    )
+    pool = total.astype(BF16).T
     agg = dot(pool[:, :half], lo_own[...]) + dot(pool[:, half:], lo_oth[...])
     mid = (packed_ref[0:nodes, :].astype(F32) + agg).astype(BF16)
     mid_ref[...] = mid
@@ -340,45 +371,50 @@
     to_patch = [(d, s) for s, d in to_owner]
     shape = jax.ShapeDtypeStruct
 
+    hbm = pl.BlockSpec(memory_space=pltpu.HBM)
+    vmem = pl.BlockSpec(memory_space=pltpu.VMEM)
     latent_other = other(mesh_latent)
     packed_rows = nodes + 4 * (nodes * slots // width) + nodes * slots // LANES
+    pack_inputs = (grid_senders.T, grid_lengths.reshape(1, nodes), grid_feats, mesh_latent)
     packed = call(
         functools.partial(pack_body, slab_rows),
         shape((packed_rows, width), BF16),
-        (grid_senders.T, grid_lengths.reshape(1, nodes), grid_feats, mesh_latent, latent_other),
-        scratch=[pltpu.VMEM((nodes, slots), F32)],
+        (*pack_inputs, latent_other),
+        in_specs=[hbm] * 4 + [vmem],
+        out_specs=vmem,
+        scratch=[pltpu.VMEM(a.shape, a.dtype) for a in pack_inputs]
+        + [pltpu.VMEM((nodes, slots), F32), pltpu.SemaphoreType.DMA((4,))],
     )
     near_packed = lax.ppermute(packed, ("band", "ch"), to_owner)
 
     tile = slab_rows // 4
-    fixed = lambda a: pl.BlockSpec(a.shape, lambda i: (0, 0))
-    embed_weights = []
-    for w in (embed_first, embed_second, link_sender):
-        embed_weights += [w, other(w)]
+    embed_weights = (embed_first, embed_second, link_sender)
+    inputs = grid_input.shape[1]
     table = call(
-        embed_body,
-        shape((slab_rows, width), BF16),
-        (grid_input.T, *embed_weights),
-        grid=(slab_rows // tile,),
-        in_specs=[pl.BlockSpec((grid_input.shape[1], tile), lambda i: (0, i))]
-        + [fixed(w) for w in embed_weights],
-        out_specs=pl.BlockSpec((tile, width), lambda i: (i, 0)),
+        functools.partial(embed_body, tile),
+        shape((width, slab_rows), BF16),
+        (grid_input.T, *embed_weights, *[other(w) for w in embed_weights]),
+        in_specs=[hbm] * 4 + [vmem] * 3,
+        out_specs=vmem,
+        scratch=[pltpu.VMEM((inputs, slab_rows), BF16)]
+        + [pltpu.VMEM(w.shape, BF16) for w in embed_weights]
+        + [pltpu.VMEM((width, n), BF16) for n in (inputs, width, width)]
+        + [pltpu.SemaphoreType.DMA((3 + slab_rows // tile,))],
         flops=2 * slab_rows * width * (256 + 2 * width),
         moved=4 * 1024 * 1024,
     )
 
     link_weights = (link_receiver, other(link_receiver), link_edge, other(link_edge))
     group_slots = BLOCKS_PER_GROUP * LANES
-    group_nodes = group_slots // slots
     blocks = nodes * slots // LANES
     scratch = lambda count: [
-        pltpu.VMEM((count // BLOCKS_PER_GROUP, 16 + 2 * group_nodes, group_slots), BF16),
+        pltpu.VMEM((count // BLOCKS_PER_GROUP, PAYLOAD_ROWS, group_slots), BF16),
         pltpu.VMEM((count, LANES), F32),
-        pltpu.VMEM((count // BLOCKS_PER_GROUP, 16 + 2 * group_nodes, width), BF16),
+        pltpu.VMEM((PAYLOAD_ROWS + count * LANES // slots, width), BF16),
     ]
     own = call(
         functools.partial(own_pool_body, nodes, slots),
-        shape((nodes // 2, width), F32),
+        shape((width, nodes // 2), F32),
         (packed, table, *link_weights),
         scratch=scratch(blocks // 2),
         flops=4 * 10**9,
@@ -387,9 +423,9 @@
     own_other = other(own)
     near = call(
         functools.partial(near_pool_body, nodes, slots),
-        shape((nodes, width), BF16),
+        shape((width, nodes), BF16),
         (near_packed, table, *link_weights),
-        scratch=scratch(blocks) + [pltpu.VMEM((nodes, width), F32)],
+        scratch=scratch(blocks) + [pltpu.VMEM((width, nodes), F32)],
         flops=4 * 10**9,
         moved=4 * 1024 * 1024,
     )

time: 64.1 us -> 61 us (0.952); the launches traced: 63.6 us -> 59.9 us
  starting transfers between devices: 16 us -> 13.7 us
  Pallas kernels: 22 us -> 20.3 us
    all_to_all x1, starting transfers between devices: 5.72 us -> 3.49 us  [per_device(): piece = lax.all_to_all(spread, 'band', 0, 0, tiled=True)]
    pallas_call x7, Pallas kernels: 22 us -> 20.3 us  [call(): pl.pallas_call(body, out_shape=out_shape, scratch_shapes=list(scratch), c...]
  transfers between devices with their start and end apart: 16 -> 16, of which waited for: 5 -> 5; matrix products, arithmetic and copies ran while one was open for 0% -> 1% of each run, Pallas kernels for 32% -> 31%
where the time goes in v3:
time: 61 us; the launch traced here: 59.9 us
  Pallas kernels  20.3 us (33%)
  waiting for transfers between devices  17.4 us (29%)
  starting transfers between devices  13.7 us (22%)
  local copies, waits for them, and re-layouts  8.1 us (13%)
    pallas_call x7, Pallas kernels, call(): pl.pallas_call(body, out_shape=out_shape, scratch_shapes=list(scratch), c...  20.3 us
    all_to_all x1, waiting for transfers between devices, per_device(): piece = lax.all_to_all(spread, 'band', 0, 0, tiled=True)  13.9 us
    unnamed x44, local copies, waits for them, and re-layouts  7.03 us
    ppermute x1, starting transfers between devices, per_device(): near_back = lax.ppermute(near, ('band', 'ch'), to_patch)  5.54 us
    all_to_all x1, starting transfers between devices, per_device(): piece = lax.all_to_all(spread, 'band', 0, 0, tiled=True)  3.49 us
    ppermute x13, waiting for transfers between devices, per_device(): other = lambda a: lax.ppermute(a, 'ch', [(0, 1), (1, 0)])  3.43 us
    ppermute x13, starting transfers between devices, per_device(): other = lambda a: lax.ppermute(a, 'ch', [(0, 1), (1, 0)])  3.39 us
    ppermute x1, starting transfers between devices, per_device(): near_packed = lax.ppermute(packed, ('band', 'ch'), to_owner)  1.28 us
  transfers between devices with their start and end apart: 16, of which 5 were waited for; matrix products, arithmetic and copies ran while one was open for 1% of the time, Pallas kernels for 31%

profile of v3, /device:TPU:0, one launch (start us, length us, event | category | flops | bytes accessed | tf_op | source)
XLA Modules:
  0.0 59.9 jit_solution(1752059366705587942)
XLA Ops:
  0.0 0.5 collective-permute-start.3
  0.5 0.5 collective-permute-start.2
  1.0 0.5 collective-permute-start.5
  1.5 1.0 %collective-permute-done.other_ref = bf16[128,256]{1,0:T(8,128)(2,1)S(1)} collective-permute-done((bf16[128,256]{1,0:T(8,128)(2,1)}, bf16[128,256]{1,0:T(8,128)(2,1)S(1)}, u32[]{:S(2)}, u32[]{:S(2)}) %collective-permute-start) | collective-permute-done | bytes 65568 | tf_op jit(solution)/shard_map/ppermute | solution.py:367
  2.5 0.4 collective-permute-start.6
  2.8 0.8 %copy-done.6 = bf16[128,256]{1,0:T(8,128)(2,1)S(1)} copy-done((bf16[128,256]{1,0:T(8,128)(2,1)S(1)}, bf16[128,256]{1,0:T(8,128)(2,1)}, u32[]{:S(2)}) %copy-start.6) | copy-done | bytes 65560
  3.7 0.8 %copy-done.7 = bf16[4,4096]{1,0:T(4,128)(2,1)S(1)} copy-done((bf16[4,4096]{1,0:T(4,128)(2,1)S(1)}, bf16[4,4096]{1,0:T(4,128)(2,1)}, u32[]{:S(2)}) %copy-start.7) | copy-done | bytes 32792
  4.4 0.7 %copy-done.8 = s32[128,32]{0,1:T(8,128)S(1)} copy-done((s32[128,32]{0,1:T(8,128)S(1)}, s32[128,32]{0,1:T(8,128)}, u32[]{:S(2)}) %copy-start.8) | copy-done | bytes 16408
  5.2 0.7 %copy-done.12 = s32[128]{0:T(128)S(1)} copy-done((s32[128]{0:T(128)S(1)}, s32[128]{0:T(128)}, u32[]{:S(2)}) %copy-start.12) | copy-done | bytes 536
  5.8 0.4 shard_map.208.packed_ref
  6.2 0.2 collective-permute-start.10
  6.4 1.3 %collective-permute-start.1 = (bf16[192,512]{1,0:T(8,128)(2,1)S(1)}, bf16[192,512]{1,0:T(8,128)(2,1)S(1)}, u32[]{:S(2)}, u32[]{:S(2)}) collective-permute-start(bf16[192,512]{1,0:T(8,128)(2,1)S(1)} %shard_map.208.packed_ref), channel_id=1, source_target_pairs={{2,0},{4,2},{6,4},{8,6},{10,8},{12,10},{14,12},{1,3},{3,5},{5,7},{... | collective-permute-start | bytes 589832 | tf_op jit(solution)/shard_map/ppermute | solution.py:388
  7.7 1.2 %copy-done.13 = bf16[2048,227]{0,1:T(8,128)(2,1)S(1)} copy-done((bf16[2048,227]{0,1:T(8,128)(2,1)S(1)}, bf16[2048,227]{0,1:T(8,128)(2,1)}, u32[]{:S(2)}) %copy-start.13) | copy-done | bytes 929816
  8.9 0.9 %copy-done.14 = bf16[256,512]{1,0:T(8,128)(2,1)S(1)} copy-done((bf16[256,512]{1,0:T(8,128)(2,1)S(1)}, bf16[256,512]{1,0:T(8,128)(2,1)}, u32[]{:S(2)}) %copy-start.14) | copy-done | bytes 262168
  9.9 0.9 %copy-done.15 = bf16[512,256]{1,0:T(8,128)(2,1)S(1)} copy-done((bf16[512,256]{1,0:T(8,128)(2,1)S(1)}, bf16[512,256]{1,0:T(8,128)(2,1)}, u32[]{:S(2)}) %copy-start.15) | copy-done | bytes 262168
  10.8 0.9 %copy-done.17 = bf16[227,256]{1,0:T(8,128)(2,1)S(1)} copy-done((bf16[227,256]{1,0:T(8,128)(2,1)S(1)}, bf16[227,256]{1,0:T(8,128)(2,1)}, u32[]{:S(2)}) %copy-start.17) | copy-done | bytes 116248
  11.7 5.0 %shard_map.209.table_ref = bf16[512,2048]{1,0:T(8,128)(2,1)S(1)} custom-call(bf16[227,2048]{1,0:T(8,128)(2,1)S(1)} %bitcast.10, bf16[227,256]{1,0:T(8,128)(2,1)S(1)} %copy-done.17, bf16[256,512]{1,0:T(8,128)(2,1)S(1)} %copy-done.14, bf16[512,256]{1,0:T(8,128)(2,1)S(1)} %copy-done.15, bf16[227,256]{1,0:T(8,128)(2,1)S(1)} %collective-permute-done.2.f_oth, ...), custom_call_target="tpu_custom_call" | custom-call | flops 2684354560 | bytes 4194304 | tf_op jit(solution)/shard_map/pallas_call | solution.py:44
  16.7 6.5 %shard_map.210 = bf16[512,128]{1,0:T(8,128)(2,1)S(1)} custom-call(bf16[192,512]{1,0:T(8,128)(2,1)S(1)} %collective-permute-done.1.packed_ref, bf16[512,2048]{1,0:T(8,128)(2,1)S(1)} %shard_map.209.table_ref, bf16[512,256]{1,0:T(8,128)(2,1)S(1)} %copy-done.16, bf16[512,256]{1,0:T(8,128)(2,1)S(1)} %collective-permute-done.5.lr_oth, ...), custom_call_target="tpu_custom_call" | custom-call | flops 4000000000 | bytes 4194304 | tf_op jit(solution)/shard_map/pallas_call | solution.py:44
  23.3 5.5 %collective-permute-start.7 = (bf16[512,128]{1,0:T(8,128)(2,1)S(1)}, bf16[512,128]{1,0:T(8,128)(2,1)S(1)}, u32[]{:S(2)}, u32[]{:S(2)}) collective-permute-start(bf16[512,128]{1,0:T(8,128)(2,1)S(1)} %shard_map.210), channel_id=1, source_target_pairs={{0,2},{2,4},{4,6},{6,8},{8,10},{10,12},{12,14},{3,1},{5,3},{7,5},{... | collective-permute-start | bytes 393224 | tf_op jit(solution)/shard_map/ppermute | solution.py:432
  28.9 6.0 %shard_map.211.own_ref = f32[512,64]{1,0:T(8,128)S(1)} custom-call(bf16[192,512]{1,0:T(8,128)(2,1)S(1)} %shard_map.208.packed_ref, bf16[512,2048]{1,0:T(8,128)(2,1)S(1)} %shard_map.209.table_ref, bf16[512,256]{1,0:T(8,128)(2,1)S(1)} %copy-done.16, bf16[512,256]{1,0:T(8,128)(2,1)S(1)} %collective-permute-done.5.lr_oth, bf16[4,256]{1,0:T(4,128)(2,1)S(1)} %copy-done.18, ...), custom_call_target="tpu_custom_call" | custom-call | flops 4000000000 | bytes 4194304 | tf_op jit(solution)/shard_map/pallas_call | solution.py:44
  35.1 0.5 collective-permute-start.8
  35.6 1.0 %collective-permute-done.9.own_oth_ref = f32[512,64]{1,0:T(8,128)S(1)} collective-permute-done((f32[512,64]{1,0:T(8,128)S(1)}, f32[512,64]{1,0:T(8,128)S(1)}, u32[]{:S(2)}, u32[]{:S(2)}) %collective-permute-start.9) | collective-permute-done | bytes 131104 | tf_op jit(solution)/shard_map/ppermute | solution.py:367
  36.6 0.2 collective-permute-done.8.near_oth_ref
  36.8 0.5 shard_map.212
  37.3 0.8 %broadcast_in_dim.2 = bf16[8,128,256]{2,1,0:T(8,128)(2,1)} broadcast(bf16[128,256]{1,0:T(8,128)(2,1)S(1)} %get-tuple-element.9), dimensions={1,2} | broadcast | bytes 589824 | tf_op jit(solution)/shard_map/broadcast_in_dim | solution.py:440
  38.2 3.5 %all-to-all-start = ((bf16[8,128,256]{2,1,0:T(8,128)(2,1)}), bf16[8,128,256]{2,1,0:T(8,128)(2,1)S(1)}, u32[]{:S(2)}, u32[]{:S(2)}) async-start(bf16[8,128,256]{2,1,0:T(8,128)(2,1)} %broadcast_in_dim.2), calls=%async_computation | async-start | bytes 1048576 | tf_op jit(solution)/shard_map/all_to_all | solution.py:441
  41.7 0.2 collective-permute-start.13
  41.9 0.4 collective-permute-start.12
  42.7 13.9 %all-to-all-done = bf16[8,128,256]{2,1,0:T(8,128)(2,1)S(1)} async-done(((bf16[8,128,256]{2,1,0:T(8,128)(2,1)}), bf16[8,128,256]{2,1,0:T(8,128)(2,1)S(1)}, u32[]{:S(2)}, u32[]{:S(2)}) %all-to-all-start) | async-done | bytes 524320 | tf_op jit(solution)/shard_map/all_to_all | solution.py:441
  56.7 0.5 shard_map.213.pool_ref
  57.3 1.2 %collective-permute-done.11.pool_oth_ref = bf16[128,256]{1,0:T(8,128)(2,1)S(1)} collective-permute-done((bf16[128,256]{1,0:T(8,128)(2,1)S(1)}, bf16[128,256]{1,0:T(8,128)(2,1)S(1)}, u32[]{:S(2)}, u32[]{:S(2)}) %collective-permute-start.11) | collective-permute-done | bytes 65568 | tf_op jit(solution)/shard_map/ppermute | solution.py:367
  58.5 1.4 %shard_map.214 = bf16[128,256]{1,0:T(8,128)(2,1)} custom-call(bf16[128,512]{1,0:T(8,128)(2,1)S(1)} %get-tuple-element.8.mid_ref, bf16[128,256]{1,0:T(8,128)(2,1)S(1)} %shard_map.213.pool_ref, bf16[128,256]{1,0:T(8,128)(2,1)S(1)} %collective-permute-done.11.pool_oth_ref, bf16[256,512]{1,0:T(8,128)(2,1)S(1)} %copy-done.1, ...), custom_call_target="tpu_custom_call" | custom-call | tf_op jit(solution)/shard_map/pallas_call | solution.py:44
  (56 shorter events, 0.8 us)
Async XLA Ops:
  0.0 6.4 %collective-permute-start.3 = (bf16[256,512]{1,0:T(8,128)(2,1)}, bf16[256,512]{1,0:T(8,128)(2,1)S(1)}, u32[]{:S(2)}, u32[]{:S(2)}) collective-permute-start(bf16[256,512]{1,0:T(8,128)(2,1)} %s_hbm.1), channel_id=1, source_target_pairs={{0,1},{1,0},{2,3},{3,2},{4,5},{5,4},{6,7},{7,6},{8,9},{9,8},{10,11... | collective-permute-start | bytes 786440 | tf_op jit(solution)/shard_map/ppermute | solution.py:367
  0.5 7.3 %collective-permute-start.4 = (bf16[512,256]{1,0:T(8,128)(2,1)}, bf16[512,256]{1,0:T(8,128)(2,1)S(1)}, u32[]{:S(2)}, u32[]{:S(2)}) collective-permute-start(bf16[512,256]{1,0:T(8,128)(2,1)} %l_hbm.1), channel_id=1, source_target_pairs={{0,1},{1,0},{2,3},{3,2},{4,5},{5,4},{6,7},{7,6},{8,9},{9,8},{10,11... | collective-permute-start | bytes 786440 | tf_op jit(solution)/shard_map/ppermute | solution.py:367
  0.5 5.7 %collective-permute-start.2 = (bf16[227,256]{1,0:T(8,128)(2,1)}, bf16[227,256]{1,0:T(8,128)(2,1)S(1)}, u32[]{:S(2)}, u32[]{:S(2)}) collective-permute-start(bf16[227,256]{1,0:T(8,128)(2,1)} %f_hbm.1), channel_id=1, source_target_pairs={{0,1},{1,0},{2,3},{3,2},{4,5},{5,4},{6,7},{7,6},{8,9},{9,8},{10,11... | collective-permute-start | bytes 348680 | tf_op jit(solution)/shard_map/ppermute | solution.py:367
  1.0 1.5 %collective-permute-start = (bf16[128,256]{1,0:T(8,128)(2,1)}, bf16[128,256]{1,0:T(8,128)(2,1)S(1)}, u32[]{:S(2)}, u32[]{:S(2)}) collective-permute-start(bf16[128,256]{1,0:T(8,128)(2,1)} %own_hbm.1), channel_id=1, source_target_pairs={{0,1},{1,0},{2,3},{3,2},{4,5},{5,4},{6,7},{7,6},{8,9},{9,8},{10,11... | collective-permute-start | bytes 196616 | tf_op jit(solution)/shard_map/ppermute | solution.py:367
  1.0 15.7 %collective-permute-start.5 = (bf16[512,256]{1,0:T(8,128)(2,1)}, bf16[512,256]{1,0:T(8,128)(2,1)S(1)}, u32[]{:S(2)}, u32[]{:S(2)}) collective-permute-start(bf16[512,256]{1,0:T(8,128)(2,1)} %lr_own.3), channel_id=1, source_target_pairs={{0,1},{1,0},{2,3},{3,2},{4,5},{5,4},{6,7},{7,6},{8,9},{9,8},{10,11... | collective-permute-start | bytes 786440 | tf_op jit(solution)/shard_map/ppermute | solution.py:367
  2.5 14.2 %collective-permute-start.6 = (bf16[4,256]{1,0:T(4,128)(2,1)}, bf16[4,256]{1,0:T(4,128)(2,1)S(1)}, u32[]{:S(2)}, u32[]{:S(2)}) collective-permute-start(bf16[4,256]{1,0:T(4,128)(2,1)} %le_own.3), channel_id=1, source_target_pairs={{0,1},{1,0},{2,3},{3,2},{4,5},{5,4},{6,7},{7,6},{8,9},{9,8},{10,11... | collective-permute-start | bytes 6152 | tf_op jit(solution)/shard_map/ppermute | solution.py:367
  6.2 29.4 %collective-permute-start.10 = (bf16[256,512]{1,0:T(8,128)(2,1)}, bf16[256,512]{1,0:T(8,128)(2,1)S(1)}, u32[]{:S(2)}, u32[]{:S(2)}) collective-permute-start(bf16[256,512]{1,0:T(8,128)(2,1)} %lo_own.1), channel_id=1, source_target_pairs={{0,1},{1,0},{2,3},{3,2},{4,5},{5,4},{6,7},{7,6},{8,9},{9,8},{10,11... | collective-permute-start | bytes 786440 | tf_op jit(solution)/shard_map/ppermute | solution.py:367
  6.4 10.3 %collective-permute-start.1 = (bf16[192,512]{1,0:T(8,128)(2,1)S(1)}, bf16[192,512]{1,0:T(8,128)(2,1)S(1)}, u32[]{:S(2)}, u32[]{:S(2)}) collective-permute-start(bf16[192,512]{1,0:T(8,128)(2,1)S(1)} %shard_map.208.packed_ref), channel_id=1, source_target_pairs={{2,0},{4,2},{6,4},{8,6},{10,8},{12,10},{14,12},{1,3},{3,5},{5,7},{... | collective-permute-start | bytes 589832 | tf_op jit(solution)/shard_map/ppermute | solution.py:388
  7.7 1.2 %copy-start.13 = (bf16[2048,227]{0,1:T(8,128)(2,1)S(1)}, bf16[2048,227]{0,1:T(8,128)(2,1)}, u32[]{:S(2)}) copy-start(bf16[2048,227]{0,1:T(8,128)(2,1)} %param.22) | copy-start | bytes 2789380
  8.9 0.9 %copy-start.14 = (bf16[256,512]{1,0:T(8,128)(2,1)S(1)}, bf16[256,512]{1,0:T(8,128)(2,1)}, u32[]{:S(2)}) copy-start(bf16[256,512]{1,0:T(8,128)(2,1)} %s_hbm.1) | copy-start | bytes 786436
  11.7 5.0 %copy-start.16 = (bf16[512,256]{1,0:T(8,128)(2,1)S(1)}, bf16[512,256]{1,0:T(8,128)(2,1)}, u32[]{:S(2)}) copy-start(bf16[512,256]{1,0:T(8,128)(2,1)} %lr_own.3) | copy-start | bytes 786436
  11.7 5.0 %copy-start.18 = (bf16[4,256]{1,0:T(4,128)(2,1)S(1)}, bf16[4,256]{1,0:T(4,128)(2,1)}, u32[]{:S(2)}) copy-start(bf16[4,256]{1,0:T(4,128)(2,1)} %le_own.3) | copy-start | bytes 6148
  23.3 13.5 %copy-start.3 = (bf16[256,512]{1,0:T(8,128)(2,1)S(1)}, bf16[256,512]{1,0:T(8,128)(2,1)}, u32[]{:S(2)}) copy-start(bf16[256,512]{1,0:T(8,128)(2,1)} %lo_own.1) | copy-start | bytes 786436
  23.3 13.5 %copy-start.4 = (bf16[512,256]{1,0:T(8,128)(2,1)S(1)}, bf16[512,256]{1,0:T(8,128)(2,1)}, u32[]{:S(2)}) copy-start(bf16[512,256]{1,0:T(8,128)(2,1)} %ps.1) | copy-start | bytes 786436
  23.3 13.5 %copy-start.5 = (bf16[512,256]{1,0:T(8,128)(2,1)S(1)}, bf16[512,256]{1,0:T(8,128)(2,1)}, u32[]{:S(2)}) copy-start(bf16[512,256]{1,0:T(8,128)(2,1)} %pr.1) | copy-start | bytes 786436
  23.3 11.8 %collective-permute-start.7 = (bf16[512,128]{1,0:T(8,128)(2,1)S(1)}, bf16[512,128]{1,0:T(8,128)(2,1)S(1)}, u32[]{:S(2)}, u32[]{:S(2)}) collective-permute-start(bf16[512,128]{1,0:T(8,128)(2,1)S(1)} %shard_map.210), channel_id=1, source_target_pairs={{0,2},{2,4},{4,6},{6,8},{8,10},{10,12},{12,14},{3,1},{5,3},{7,5},{... | collective-permute-start | bytes 393224 | tf_op jit(solution)/shard_map/ppermute | solution.py:432
  34.9 6.8 %copy-start = (bf16[1024,256]{1,0:T(8,128)(2,1)S(1)}, bf16[1024,256]{1,0:T(8,128)(2,1)}, u32[]{:S(2)}) copy-start(bf16[1024,256]{1,0:T(8,128)(2,1)} %nf_own.1) | copy-start | bytes 1572868
  34.9 7.0 %copy-start.1 = (bf16[256,512]{1,0:T(8,128)(2,1)S(1)}, bf16[256,512]{1,0:T(8,128)(2,1)}, u32[]{:S(2)}) copy-start(bf16[256,512]{1,0:T(8,128)(2,1)} %po_own.1) | copy-start | bytes 786436
  34.9 7.3 %copy-start.2 = (bf16[256,512]{1,0:T(8,128)(2,1)S(1)}, bf16[256,512]{1,0:T(8,128)(2,1)}, u32[]{:S(2)}) copy-start(bf16[256,512]{1,0:T(8,128)(2,1)} %ns_own.1) | copy-start | bytes 786436
  34.9 7.5 %copy-start.21 = (s32[1,8]{1,0:T(1,128)S(1)}, s32[1,8]{1,0:T(1,128)}, u32[]{:S(2)}) copy-start(s32[1,8]{1,0:T(1,128)} %param.29) | copy-start | bytes 100
  34.9 7.6 %copy-start.19 = (s32[8,16]{1,0:T(8,128)S(1)}, s32[8,16]{1,0:T(8,128)}, u32[]{:S(2)}) copy-start(s32[8,16]{1,0:T(8,128)} %param.27) | copy-start | bytes 1540
  34.9 7.7 %copy-start.20 = (s32[8,16]{1,0:T(8,128)S(1)}, s32[8,16]{1,0:T(8,128)}, u32[]{:S(2)}) copy-start(s32[8,16]{1,0:T(8,128)} %param.28) | copy-start | bytes 1540
  35.0 21.7 %copy-start.9 = (bf16[4,256]{1,0:T(4,128)(2,1)S(1)}, bf16[4,256]{1,0:T(4,128)(2,1)}, u32[]{:S(2)}) copy-start(bf16[4,256]{1,0:T(4,128)(2,1)} %pe.1) | copy-start | bytes 6148
  35.0 21.7 %copy-start.10 = (bf16[4,128]{1,0:T(4,128)(2,1)S(1)}, bf16[4,128]{1,0:T(4,128)(2,1)}, u32[]{:S(2)}) copy-start(bf16[4,128]{1,0:T(4,128)(2,1)} %feats_ref.1) | copy-start | bytes 3076
  35.0 23.5 %copy-start.11 = (f32[256]{0:T(256)S(1)}, f32[256]{0:T(256)}, u32[]{:S(2)}) copy-start(f32[256]{0:T(256)} %param.43) | copy-start | bytes 3076
  35.0 1.6 %collective-permute-start.9 = (f32[512,64]{1,0:T(8,128)S(1)}, f32[512,64]{1,0:T(8,128)S(1)}, u32[]{:S(2)}, u32[]{:S(2)}) collective-permute-start(f32[512,64]{1,0:T(8,128)S(1)} %shard_map.211.own_ref), channel_id=1, source_target_pairs={{0,1},{1,0},{2,3},{3,2},{4,5},{5,4},{6,7},{7,6},{8,9},{9,8},{10,11... | collective-permute-start | bytes 393224 | tf_op jit(solution)/shard_map/ppermute | solution.py:367
  35.1 1.7 %collective-permute-start.8 = (bf16[512,128]{1,0:T(8,128)(2,1)S(1)}, bf16[512,128]{1,0:T(8,128)(2,1)S(1)}, u32[]{:S(2)}, u32[]{:S(2)}) collective-permute-start(bf16[512,128]{1,0:T(8,128)(2,1)S(1)} %collective-permute-done.7.near_ref), channel_id=1, source_target_pairs={{0,1},{1,0},{2,3},{3,2},{4,5},{5,4},{6,7},{7,6},{8,9},{9,8},{10,11... | collective-permute-start | bytes 393224 | tf_op jit(solution)/shard_map/ppermute | solution.py:367
  38.2 18.5 %all-to-all-start = ((bf16[8,128,256]{2,1,0:T(8,128)(2,1)}), bf16[8,128,256]{2,1,0:T(8,128)(2,1)S(1)}, u32[]{:S(2)}, u32[]{:S(2)}) async-start(bf16[8,128,256]{2,1,0:T(8,128)(2,1)} %broadcast_in_dim.2), calls=%async_computation | async-start | bytes 1048576 | tf_op jit(solution)/shard_map/all_to_all | solution.py:441
  41.7 15.6 %collective-permute-start.13 = (bf16[1024,256]{1,0:T(8,128)(2,1)S(1)}, bf16[1024,256]{1,0:T(8,128)(2,1)S(1)}, u32[]{:S(2)}, u32[]{:S(2)}) collective-permute-start(bf16[1024,256]{1,0:T(8,128)(2,1)S(1)} %copy-done), channel_id=1, source_target_pairs={{0,1},{1,0},{2,3},{3,2},{4,5},{5,4},{6,7},{7,6},{8,9},{9,8},{10,11... | collective-permute-start | bytes 1572872 | tf_op jit(solution)/shard_map/ppermute | solution.py:367
  41.9 15.3 %collective-permute-start.12 = (bf16[256,512]{1,0:T(8,128)(2,1)S(1)}, bf16[256,512]{1,0:T(8,128)(2,1)S(1)}, u32[]{:S(2)}, u32[]{:S(2)}) collective-permute-start(bf16[256,512]{1,0:T(8,128)(2,1)S(1)} %copy-done.1), channel_id=1, source_target_pairs={{0,1},{1,0},{2,3},{3,2},{4,5},{5,4},{6,7},{7,6},{8,9},{9,8},{10,11... | collective-permute-start | bytes 786440 | tf_op jit(solution)/shard_map/ppermute | solution.py:367
  42.3 15.0 %collective-permute-start.14 = (bf16[256,512]{1,0:T(8,128)(2,1)S(1)}, bf16[256,512]{1,0:T(8,128)(2,1)S(1)}, u32[]{:S(2)}, u32[]{:S(2)}) collective-permute-start(bf16[256,512]{1,0:T(8,128)(2,1)S(1)} %copy-done.2), channel_id=1, source_target_pairs={{0,1},{1,0},{2,3},{3,2},{4,5},{5,4},{6,7},{7,6},{8,9},{9,8},{10,11... | collective-permute-start | bytes 786440 | tf_op jit(solution)/shard_map/ppermute | solution.py:367
  57.1 1.3 %collective-permute-start.11 = (bf16[128,256]{1,0:T(8,128)(2,1)S(1)}, bf16[128,256]{1,0:T(8,128)(2,1)S(1)}, u32[]{:S(2)}, u32[]{:S(2)}) collective-permute-start(bf16[128,256]{1,0:T(8,128)(2,1)S(1)} %shard_map.213.pool_ref), channel_id=1, source_target_pairs={{0,1},{1,0},{2,3},{3,2},{4,5},{5,4},{6,7},{7,6},{8,9},{9,8},{10,11... | collective-permute-start | bytes 196616 | tf_op jit(solution)/shard_map/ppermute | solution.py:367
  (6 other events, 4.8 us)

commit v4 on v3

--- a/solution.py
+++ b/solution.py
@@ -11,6 +11,7 @@
 BF16 = jnp.bfloat16
 LANES = 128
 CHUNK = 256
+SPARE = 128
 PAYLOAD_ROWS = 16
 BLOCKS_PER_GROUP = 8
 VMEM_LIMIT = 48 * 1024 * 1024
@@ -51,23 +52,15 @@
     )(*args)
 
 
-def pack_body(slab_rows, senders_hbm, lengths_hbm, feats_hbm, own_hbm, other_ref, out_ref, senders_ref, lengths_ref, feats_ref, own_ref, turned, sems):
+def tail_body(slab_rows, width, senders_hbm, lengths_hbm, feats_hbm, mesh_hbm, out_ref, request_ref, senders_ref, lengths_ref, feats_ref, mesh_ref, turned, sems):
+    band = lax.axis_index("band")
     copies = fetch(
-        [(senders_hbm, senders_ref), (lengths_hbm, lengths_ref), (feats_hbm, feats_ref), (own_hbm, own_ref)],
-        sems,
+        [(senders_hbm, senders_ref), (lengths_hbm, lengths_ref), (feats_hbm, feats_ref), (mesh_hbm, mesh_ref)], sems
     )
     for c in copies:
         c.wait()
-    band = lax.axis_index("band")
-    core = lax.axis_index("ch")
     slots, nodes = senders_ref.shape
-    width = out_ref.shape[1]
     turned[...] = (senders_ref[...] - (band - 1) * slab_rows).astype(F32).T
-    own, other = own_ref[...], other_ref[...]
-    first = core == 0
-    out_ref[0:nodes, :] = jnp.concatenate(
-        [jnp.where(first, own, other), jnp.where(first, other, own)], axis=1
-    )
     per_row = LANES // slots
     rows = nodes // per_row
     pieces = [turned[pl.ds(j, rows, stride=per_row), :] for j in range(per_row)]
@@ -79,15 +72,32 @@
         0.0,
     ).astype(BF16)
     pick = ones_where(iota((nodes, LANES), 0) % per_row == iota((nodes, LANES), 1) // slots)
-    length = dot(spread, pick)
-    used = (iota(shape, 1) % slots).astype(F32) < length
+    used = (iota(shape, 1) % slots).astype(F32) < dot(spread, pick)
     high = jnp.where(used, index // LANES + 1, 0).astype(F32)
     low = jnp.where(used, index % LANES, 0).astype(F32)
-    fill = jnp.zeros((rows, width - 2 * LANES), F32)
+    half = rows // 2
     feats = feats_ref[...].astype(F32)
     parts = [feats[:, k * width : (k + 1) * width] for k in range(feats.shape[1] // width)]
-    tail = jnp.concatenate(parts + [jnp.concatenate([high, low, fill], axis=1)], axis=0)
-    out_ref[nodes:, :] = tail.astype(BF16)
+    places = [high[:half], low[:half], high[half:], low[half:]]
+    tail = jnp.concatenate(parts + [jnp.concatenate(places, axis=1)], axis=0)
+    out_ref[...] = tail.astype(BF16)
+    peers, capacity = mesh_ref.shape
+    edges = peers * capacity
+    peer = ones_where(iota((edges, peers), 0) // capacity == iota((edges, peers), 1))
+    lists = dot(peer, mesh_ref[...].astype(F32).astype(BF16))
+    own_slot = iota((edges, capacity), 0) % capacity == iota((edges, capacity), 1)
+    single = jnp.where(own_slot, lists, 0.0).astype(BF16)
+    request_ref[...] = dot(single, jnp.ones((capacity, width), BF16)).astype(BF16)
+
+
+def pack_body(own_ref, other_ref, tail_ref, out_ref):
+    first = lax.axis_index("ch") == 0
+    nodes = own_ref.shape[0]
+    own, other = own_ref[...], other_ref[...]
+    out_ref[0:nodes, :] = jnp.concatenate(
+        [jnp.where(first, own, other), jnp.where(first, other, own)], axis=1
+    )
+    out_ref[nodes:, :] = tail_ref[...]
 
 
 def fetch(moves, sems):
@@ -97,22 +107,23 @@
     return copies
 
 
-def embed_body(tile, x_hbm, f_hbm, s_hbm, l_hbm, f_oth, s_oth, l_oth, out_ref, x_ref, f_own, s_own, l_own, first_t, second_t, third_t, sems):
+def embed_body(tile, x_hbm, f_hbm, s_hbm, l_hbm, f_oth, s_oth, l_oth, out_ref, x_ref, f_own, s_own, l_own, first_t, joint_t, sems):
     half = f_oth.shape[1]
     tiles = x_ref.shape[1] // tile
-    moves = [(f_hbm, f_own), (s_hbm, s_own), (l_hbm, l_own)]
+    moves = [(s_hbm, s_own), (l_hbm, l_own), (f_hbm, f_own)]
     moves += [
         (x_hbm.at[:, pl.ds(k * tile, tile)], x_ref.at[:, pl.ds(k * tile, tile)]) for k in range(tiles)
     ]
     copies = fetch(moves, sems)
     first_t[half:, :] = f_oth[...].T
-    second_t[:, half:] = s_oth[...].T
-    third_t[half:, :] = l_oth[...].T
-    for c in copies[:3]:
-        c.wait()
+    copies[0].wait()
+    copies[1].wait()
+    for k, s in ((0, s_own), (1, s_oth)):
+        for j, l in ((0, l_own), (1, l_oth)):
+            joint = dot(s[...], l[...]).astype(BF16)
+            joint_t[j * half : (j + 1) * half, k * half : (k + 1) * half] = joint.T
+    copies[2].wait()
     first_t[:half, :] = f_own[...].T
-    second_t[:, :half] = s_own[...].T
-    third_t[:half, :] = l_own[...].T
     for c in copies[3:]:
         c.wait()
 
@@ -120,8 +131,7 @@
     def _(k):
         at = pl.ds(pl.multiple_of(k * tile, tile), tile)
         hidden = silu(dot(first_t[...], x_ref[:, at])).astype(BF16)
-        latent = dot(second_t[...], hidden).astype(BF16)
-        out_ref[:, at] = dot(third_t[...], latent).astype(BF16)
+        out_ref[:, at] = dot(joint_t[...], hidden).astype(BF16)
 
 
 def running(flag16, together):
@@ -133,7 +143,7 @@
     return inclusive + jnp.sum(dot(ones_where(earlier), flag16), axis=1, keepdims=True)
 
 
-def pool_part(high, low, feats, latent, kind, slots, table_ref, weights, payload, late, right, out_ref):
+def pool_part(high, low, feats, latent, kind, slots, room, spare, table_ref, weights, payload, late, right, out_ref):
     lr_own, lr_oth, le_own, le_oth = weights
     blocks = high.shape[0]
     nodes = latent.shape[0]
@@ -153,16 +163,25 @@
     valid = (local >= 0.0) & (local < float(per_slab))
     flag = jnp.where(valid, 1.0, 0.0)
     rank = running(flag.astype(BF16), BLOCKS_PER_GROUP) - 1.0
-    over = valid & (rank >= float(CHUNK))
+    over = valid & (rank >= float(room))
     over_flag = jnp.where(over, 1.0, 0.0)
     late[...] = jnp.where(over, running(over_flag.astype(BF16), blocks) - 1.0, -1.0)
     rank = jnp.where(valid, rank, -1.0)
     spot = iota((1, group_slots), 1) // slots
-    place = iota((CHUNK, LANES), 0).astype(F32)
-
-    def picked(rows, start, columns):
-        select = jnp.concatenate([ones_where(r == place + start) for r in rows], axis=1)
+
+    def picked(rows, start, count, columns):
+        place = iota((count, LANES), 0).astype(F32) + start
+        select = jnp.concatenate([ones_where(r == place) for r in rows], axis=1)
         return dot_on(columns, select, 1, 1)
+
+    def picked_late(start, count):
+        total = None
+        for g in range(groups):
+            at = g * BLOCKS_PER_GROUP
+            rows = [late[at + k : at + k + 1, :] for k in range(BLOCKS_PER_GROUP)]
+            term = picked(rows, start, count, payload[g])
+            total = term if total is None else total + term
+        return total
 
     def pooled(compact):
         count = compact.shape[1]
@@ -194,29 +213,25 @@
         ).astype(BF16)
         payload[g] = columns
         rows = [rank[at + k : at + k + 1, :] for k in range(BLOCKS_PER_GROUP)]
-        parts.append(picked(rows, 0.0, columns))
+        parts.append(picked(rows, 0.0, room, columns))
+    if spare:
+        parts.append(picked_late(0.0, spare))
     out_ref[...] = pooled(jnp.concatenate(parts, axis=1))
     count = jnp.sum(over_flag).astype(jnp.int32)
 
-    @pl.loop(0, (count + CHUNK - 1) // CHUNK)
+    @pl.loop(0, jnp.maximum(count - spare + CHUNK - 1, 0) // CHUNK)
     def _(step):
-        start = (step * CHUNK).astype(F32)
-        total = None
-        for g in range(groups):
-            at = g * BLOCKS_PER_GROUP
-            rows = [late[at + k : at + k + 1, :] for k in range(BLOCKS_PER_GROUP)]
-            term = picked(rows, start, payload[g])
-            total = term if total is None else total + term
-        out_ref[...] += pooled(total)
+        out_ref[...] += pooled(picked_late((step * CHUNK + spare).astype(F32), CHUNK))
 
 
 def unpack(packed_ref, nodes, slots):
     width = packed_ref.shape[1]
     blocks = nodes * slots // LANES
     tail = packed_ref[nodes:, :].astype(F32)
-    feat_rows = tail.shape[0] - blocks
-    high = tail[feat_rows:, 0:LANES]
-    low = tail[feat_rows:, LANES : 2 * LANES]
+    feat_rows = tail.shape[0] - blocks // 2
+    place = lambda k: tail[feat_rows:, k * LANES : (k + 1) * LANES]
+    high = jnp.concatenate([place(0), place(2)], axis=0)
+    low = jnp.concatenate([place(1), place(3)], axis=0)
     per_group = BLOCKS_PER_GROUP * LANES // width
     feats = []
     for g in range(blocks // BLOCKS_PER_GROUP):
@@ -239,6 +254,8 @@
         latent,
         jnp.int32(1),
         slots,
+        2 * CHUNK,
+        0,
         table_ref,
         (lr_own, lr_oth, le_own, le_oth),
         payload,
@@ -258,6 +275,8 @@
         packed_ref[0:nodes, :],
         kind,
         slots,
+        CHUNK,
+        SPARE,
         table_ref,
         (lr_own, lr_oth, le_own, le_oth),
         payload,
@@ -268,7 +287,7 @@
     out_ref[...] = total[...].astype(BF16)
 
 
-def middle_body(packed_ref, near_ref, near_oth_ref, own_ref, own_oth_ref, lo_own, lo_oth, ps, pr, mid_ref, send_ref, recv_ref):
+def middle_body(packed_ref, near_ref, near_oth_ref, own_ref, own_oth_ref, lo_own, lo_oth, request_ref, mid_ref, rows_ref):
     first = lax.axis_index("ch") == 0
     half = lo_own.shape[0]
     nodes = near_ref.shape[1]
@@ -283,45 +302,49 @@
     agg = dot(pool[:, :half], lo_own[...]) + dot(pool[:, half:], lo_oth[...])
     mid = (packed_ref[0:nodes, :].astype(F32) + agg).astype(BF16)
     mid_ref[...] = mid
-    send_ref[...] = dot(mid, ps[...]).astype(BF16)
-    recv_ref[...] = dot(mid, pr[...])
-
-
-def edge_body(patches, piece_ref, recv_ref, senders_ref, receivers_ref, limit_ref, feats_ref, pe, pool_ref):
-    nodes = recv_ref.shape[0]
-    rows = patches * nodes
-    slots = senders_ref.shape[1] * rows // piece_ref.shape[0]
-    recv = recv_ref[...]
-    recv_high = recv.astype(BF16)
-    recv_low = (recv - recv_high.astype(F32)).astype(BF16)
-    total = None
-    for k in range(piece_ref.shape[0] // rows):
-        lanes = slice(k * slots, (k + 1) * slots)
-        patch = iota((1, slots), 1) // (slots // patches)
-        choose = ones_where(iota((rows, slots), 0) == senders_ref[:, lanes] + patch * nodes)
-        into = iota((nodes, slots), 0) == receivers_ref[:, lanes]
-        into16 = ones_where(into)
-        pre = (
-            dot_on(choose, piece_ref[k * rows : (k + 1) * rows, :], 0, 0)
-            + dot_on(into16, recv_high, 0, 0)
-            + dot_on(into16, recv_low, 0, 0)
-            + dot_on(feats_ref[:, lanes], pe[...], 0, 0)
+    request = request_ref[...].astype(F32)
+    wanted = ones_where(iota((request.shape[0], nodes), 1).astype(F32) == request[:, 0:1])
+    rows_ref[...] = dot(wanted, mid).astype(BF16)
+
+
+def base_body(mid_ref, receivers_ref, feats_ref, pr_own, pr_oth, pe_own, pe_oth, nf_own, nf_oth, base_ref, upper_ref):
+    nodes, width = mid_ref.shape
+    mid = mid_ref[...]
+    edges = receivers_ref.shape[1]
+    into = ones_where(iota((nodes, edges), 0) == receivers_ref[...])
+    half = width // 2
+    for k, (pr, pe, nf) in enumerate(((pr_own, pe_own, nf_own), (pr_oth, pe_oth, nf_oth))):
+        at = slice(k * half, (k + 1) * half)
+        recv = dot(mid, pr[...])
+        high = recv.astype(BF16)
+        low = (recv - high.astype(F32)).astype(BF16)
+        base_ref[:, at] = (
+            dot_on(into, high, 0, 0) + dot_on(into, low, 0, 0) + dot_on(feats_ref[...], pe[...], 0, 0)
         )
-        act = silu(pre).astype(BF16)
-        part = dot(ones_where(into & (limit_ref[:, lanes] > 0)), act)
-        total = part if total is None else total + part
-    pool_ref[...] = total.astype(BF16)
-
-
-def node_body(mid_ref, pool_ref, pool_oth_ref, po_own, po_oth, nf_own, nf_oth, ns_own, ns_oth, gain_ref, out_ref):
+        upper_ref[:, at] = dot(mid, nf[0:width, :])
+
+
+def node_body(rows_ref, base_ref, upper_ref, mid_ref, receivers_ref, limit_ref, gain_ref, ps_own, ps_oth, po_own, po_oth, nf_own, nf_oth, ns_own, ns_oth, out_ref):
     first = lax.axis_index("ch") == 0
-    width = mid_ref.shape[1]
+    nodes, width = mid_ref.shape
     half = width // 2
-    mid = mid_ref[...]
-    agg = (dot(pool_ref[...], po_own[...]) + dot(pool_oth_ref[...], po_oth[...])).astype(BF16)
+    rows = rows_ref[...]
+    edges = rows.shape[0]
+    into = ones_where(
+        (iota((nodes, edges), 0) == receivers_ref[...]) & (limit_ref[...] > 0)
+    )
+    agg = None
+    for k, (ps, po) in enumerate(((ps_own, po_own), (ps_oth, po_oth))):
+        at = slice(k * half, (k + 1) * half)
+        sent = dot(rows, ps[...]).astype(BF16).astype(F32)
+        act = silu(sent + base_ref[:, at]).astype(BF16)
+        term = dot(dot(into, act).astype(BF16), po[...])
+        agg = term if agg is None else agg + term
+    agg = agg.astype(BF16)
     update = None
-    for nf, ns in ((nf_own, ns_own), (nf_oth, ns_oth)):
-        hidden = silu(dot(mid, nf[0:width, :]) + dot(agg, nf[width:, :])).astype(BF16)
+    for k, (nf, ns) in enumerate(((nf_own, ns_own), (nf_oth, ns_oth))):
+        at = slice(k * half, (k + 1) * half)
+        hidden = silu(upper_ref[:, at] + dot(agg, nf[width:, :])).astype(BF16)
         term = dot(hidden, ns[...])
         update = term if update is None else update + term
     mean = jnp.sum(update, axis=1, keepdims=True) / width
@@ -329,7 +352,7 @@
     scale = lax.rsqrt(square - mean * mean + 1e-05)
     pick = lambda a: jnp.where(first, a[:, :half], a[:, half:])
     out_ref[...] = (
-        pick(mid).astype(F32) + (pick(update) - mean) * scale * gain_ref[...]
+        pick(mid_ref[...]).astype(F32) + (pick(update) - mean) * scale * gain_ref[...]
     ).astype(BF16)
 
 
@@ -373,40 +396,52 @@
 
     hbm = pl.BlockSpec(memory_space=pltpu.HBM)
     vmem = pl.BlockSpec(memory_space=pltpu.VMEM)
+    pin = lambda a: pltpu.with_memory_space_constraint(a, pltpu.HBM)
     latent_other = other(mesh_latent)
-    packed_rows = nodes + 4 * (nodes * slots // width) + nodes * slots // LANES
-    pack_inputs = (grid_senders.T, grid_lengths.reshape(1, nodes), grid_feats, mesh_latent)
+    blocks = nodes * slots // LANES
+    tail_rows = 4 * (nodes * slots // width) + blocks // 2
+    tail_inputs = [pin(a) for a in (grid_senders.T, grid_lengths.reshape(1, nodes), grid_feats, mesh_senders)]
+    tail, request = call(
+        functools.partial(tail_body, slab_rows, width),
+        (shape((tail_rows, width), BF16), shape((edges, width), BF16)),
+        tail_inputs,
+        in_specs=[hbm] * 4,
+        out_specs=(vmem, vmem),
+        scratch=[pltpu.VMEM(a.shape, a.dtype) for a in tail_inputs]
+        + [pltpu.VMEM((nodes, slots), F32), pltpu.SemaphoreType.DMA((4,))],
+    )
     packed = call(
-        functools.partial(pack_body, slab_rows),
-        shape((packed_rows, width), BF16),
-        (*pack_inputs, latent_other),
-        in_specs=[hbm] * 4 + [vmem],
-        out_specs=vmem,
-        scratch=[pltpu.VMEM(a.shape, a.dtype) for a in pack_inputs]
-        + [pltpu.VMEM((nodes, slots), F32), pltpu.SemaphoreType.DMA((4,))],
+        pack_body, shape((nodes + tail_rows, width), BF16), (mesh_latent, latent_other, tail)
     )
     near_packed = lax.ppermute(packed, ("band", "ch"), to_owner)
+    after = lambda token, *arrays: lax.optimization_barrier((token, *arrays))[1:]
+    embed_weights = after(packed, embed_first, embed_second, link_sender)
+    link_receiver, link_edge, link_out, request = after(
+        packed, link_receiver, link_edge, link_out, request
+    )
+    request = lax.all_to_all(request, "band", 0, 0, tiled=True)
 
     tile = slab_rows // 4
-    embed_weights = (embed_first, embed_second, link_sender)
     inputs = grid_input.shape[1]
     table = call(
         functools.partial(embed_body, tile),
         shape((width, slab_rows), BF16),
-        (grid_input.T, *embed_weights, *[other(w) for w in embed_weights]),
+        (
+            *[pin(a) for a in (grid_input.T, embed_first, embed_second, link_sender)],
+            *[other(w) for w in embed_weights],
+        ),
         in_specs=[hbm] * 4 + [vmem] * 3,
         out_specs=vmem,
         scratch=[pltpu.VMEM((inputs, slab_rows), BF16)]
         + [pltpu.VMEM(w.shape, BF16) for w in embed_weights]
-        + [pltpu.VMEM((width, n), BF16) for n in (inputs, width, width)]
+        + [pltpu.VMEM((width, n), BF16) for n in (inputs, width)]
         + [pltpu.SemaphoreType.DMA((3 + slab_rows // tile,))],
-        flops=2 * slab_rows * width * (256 + 2 * width),
+        flops=2 * slab_rows * width * (256 + width),
         moved=4 * 1024 * 1024,
     )
 
     link_weights = (link_receiver, other(link_receiver), link_edge, other(link_edge))
     group_slots = BLOCKS_PER_GROUP * LANES
-    blocks = nodes * slots // LANES
     scratch = lambda count: [
         pltpu.VMEM((count // BLOCKS_PER_GROUP, PAYLOAD_ROWS, group_slots), BF16),
         pltpu.VMEM((count, LANES), F32),
@@ -432,37 +467,30 @@
     near_back = lax.ppermute(near, ("band", "ch"), to_patch)
     near_back_other = other(near_back)
 
-    mid, send, recv = call(
+    lanes = lambda a: a.reshape(1, edges)
+    mid, rows = call(
         middle_body,
-        (shape((nodes, width), BF16), shape((nodes, half), BF16), shape((nodes, half), F32)),
-        (packed, near_back, near_back_other, own, own_other, link_out, other(link_out), proc_sender, proc_receiver),
-    )
-    spread = jnp.broadcast_to(send[None], (bands, nodes, half)).reshape(bands * nodes, half)
-    piece = lax.all_to_all(spread, "band", 0, 0, tiled=True)
-
-    limit = (
+        (shape((nodes, width), BF16), shape((edges, width), BF16)),
+        (packed, near_back, near_back_other, own, own_other, link_out, other(link_out), request),
+    )
+    rows = lax.all_to_all(rows, "band", 0, 0, tiled=True)
+    pairs = []
+    for w in after(mid, proc_receiver, proc_edge, node_first, proc_sender, proc_out, node_second):
+        pairs.append((w, other(w)))
+    pr, pe, nf, ps, po, ns = pairs
+    receivers = lanes(mesh_receivers)
+    limit = lanes(
         mesh_counts.reshape(bands, 1) - jnp.arange(capacity, dtype=jnp.int32)[None, :]
-    ).reshape(1, edges)
-    pool = call(
-        functools.partial(edge_body, LANES // capacity),
-        shape((nodes, half), BF16),
-        (piece, recv, mesh_senders.reshape(1, edges), mesh_receivers.reshape(1, edges), limit, mesh_feats, proc_edge),
+    )
+    base, upper = call(
+        base_body,
+        (shape((edges, width), F32), shape((nodes, width), F32)),
+        (mid, receivers, mesh_feats, *pr, *pe, *nf),
     )
     return call(
         node_body,
         shape((nodes, half), BF16),
-        (
-            mid,
-            pool,
-            other(pool),
-            proc_out,
-            other(proc_out),
-            node_first,
-            other(node_first),
-            node_second,
-            other(node_second),
-            norm_gain.reshape(1, half),
-        ),
+        (rows, base, upper, mid, receivers, limit, norm_gain.reshape(1, half), *ps, *po, *nf, *ns),
     )
 
 

time: 61 us -> 52.1 us (0.85)
  waiting for transfers between devices: 17.4 us -> 5.9 us
  starting transfers between devices: 13.7 us -> 21.8 us
  local copies, waits for them, and re-layouts: 8.1 us -> 4.6 us
  Pallas kernels: 20.3 us -> 18.8 us
    all_to_all x1 -> x2, waiting for transfers between devices: 13.9 us -> 3.92 us  [the longest x1 3.92 us: per_device(): rows = lax.all_to_all(rows, 'band', 0, 0, tiled=True)]
    all_to_all x1 -> x2, starting transfers between devices: 3.49 us -> 12.6 us  [the longest x1 8.05 us: per_device(): request = lax.all_to_all(request, 'band', 0, 0, tiled=True)]
    unnamed x44 -> x38, local copies, waits for them, and re-layouts: 7.03 us -> 4.44 us
    ppermute x1, starting transfers between devices: 5.54 us -> 4 us  [per_device(): near_back = lax.ppermute(near, ('band', 'ch'), to_patch)]
    pallas_call x7 -> x8, Pallas kernels: 20.3 us -> 18.8 us  [call(): pl.pallas_call(body, out_shape=out_shape, scratch_shapes=list(scratch), c...]
    ppermute x13 -> x15, waiting for transfers between devices: 3.43 us -> 1.97 us  [per_device(): other = lambda a: lax.ppermute(a, 'ch', [(0, 1), (1, 0)])]
    broadcast_in_dim x1 -> x0, local copies, waits for them, and re-layouts: 0.83 us -> none  [per_device(): jnp.broadcast_to(send[None], (bands, nodes, half))]
    ppermute x13 -> x15, starting transfers between devices: 3.39 us -> 3.96 us  [per_device(): other = lambda a: lax.ppermute(a, 'ch', [(0, 1), (1, 0)])]
  transfers between devices with their start and end apart: 16 -> 19, of which waited for: 5 -> 4; matrix products, arithmetic and copies ran while one was open for 1% -> 0% of each run, Pallas kernels for 31% -> 31%
where the time goes in v4:
time: 52.1 us; the launch traced here: 51.5 us
  starting transfers between devices  21.8 us (42%)
  Pallas kernels  18.8 us (36%)
  waiting for transfers between devices  5.9 us (11%)
  local copies, waits for them, and re-layouts  4.6 us (9%)
    pallas_call x8, Pallas kernels, call(): pl.pallas_call(body, out_shape=out_shape, scratch_shapes=list(scratch), c...  18.8 us
    all_to_all x1, starting transfers between devices, per_device(): request = lax.all_to_all(request, 'band', 0, 0, tiled=True)  8.05 us
    all_to_all x1, starting transfers between devices, per_device(): rows = lax.all_to_all(rows, 'band', 0, 0, tiled=True)  4.55 us
    unnamed x38, local copies, waits for them, and re-layouts  4.44 us
    ppermute x1, starting transfers between devices, per_device(): near_back = lax.ppermute(near, ('band', 'ch'), to_patch)  4 us
    ppermute x15, starting transfers between devices, per_device(): other = lambda a: lax.ppermute(a, 'ch', [(0, 1), (1, 0)])  3.96 us
    all_to_all x1, waiting for transfers between devices, per_device(): rows = lax.all_to_all(rows, 'band', 0, 0, tiled=True)  3.92 us
    ppermute x15, waiting for transfers between devices, per_device(): other = lambda a: lax.ppermute(a, 'ch', [(0, 1), (1, 0)])  1.97 us
  transfers between devices with their start and end apart: 19, of which 4 were waited for; matrix products, arithmetic and copies ran while one was open for 0% of the time, Pallas kernels for 31%

profile of v4, /device:TPU:0, one launch (start us, length us, event | category | flops | bytes accessed | tf_op | source)
XLA Modules:
  0.0 51.5 jit_solution(13258568201557510069)
XLA Ops:
  0.0 0.5 collective-permute-start
  0.5 1.8 %shard_map.208 = (bf16[48,512]{1,0:T(8,128)(2,1)S(1)}, bf16[128,512]{1,0:T(8,128)(2,1)}) custom-call(s32[32,128]{1,0:T(8,128)} %bitcast.12, s32[1,128]{1,0:T(1,128)} %bitcast.13, bf16[4,4096]{1,0:T(4,128)(2,1)} %feats_hbm.1, s32[8,16]{1,0:T(8,128)} %mesh_hbm.1), custom_call_target="tpu_custom_call" | custom-call | tf_op jit(solution)/shard_map/pallas_call | solution.py:45
  2.3 0.8 %copy-done.9 = bf16[128,256]{1,0:T(8,128)(2,1)S(1)} copy-done((bf16[128,256]{1,0:T(8,128)(2,1)S(1)}, bf16[128,256]{1,0:T(8,128)(2,1)}, u32[]{:S(2)}) %copy-start.9) | copy-done | bytes 65560
  3.1 0.1 collective-permute-start.3
  3.2 0.5 collective-permute-start.4
  3.8 0.4 collective-permute-start.5
  4.2 1.3 %collective-permute-start.1 = (bf16[176,512]{1,0:T(8,128)(2,1)S(1)}, bf16[176,512]{1,0:T(8,128)(2,1)S(1)}, u32[]{:S(2)}, u32[]{:S(2)}) collective-permute-start(bf16[176,512]{1,0:T(8,128)(2,1)S(1)} %shard_map.209.packed_ref), channel_id=1, source_target_pairs={{2,0},{4,2},{6,4},{8,6},{10,8},{12,10},{14,12},{1,3},{3,5},{5,7},{... | collective-permute-start | bytes 540680 | tf_op jit(solution)/shard_map/ppermute | solution.py:416
  5.5 8.1 %all-to-all-start = ((bf16[8,16,512]{2,1,0:T(8,128)(2,1)}), bf16[8,16,512]{2,1,0:T(8,128)(2,1)S(1)}, u32[]{:S(2)}, u32[]{:S(2)}) async-start(bf16[8,16,512]{2,1,0:T(8,128)(2,1)} %bitcast.3), calls=%async_computation | async-start | bytes 262144 | tf_op jit(solution)/shard_map/all_to_all | solution.py:422
  13.6 0.5 collective-permute-start.10
  14.1 4.4 %shard_map.210.table_ref = bf16[512,2048]{1,0:T(8,128)(2,1)S(1)} custom-call(bf16[227,2048]{1,0:T(8,128)(2,1)} %bitcast.15, bf16[227,256]{1,0:T(8,128)(2,1)} %f_hbm.1, bf16[256,512]{1,0:T(8,128)(2,1)} %s_hbm.1, bf16[512,256]{1,0:T(8,128)(2,1)} %l_hbm.1, bf16[227,256]{1,0:T(8,128)(2,1)S(1)} %collective-permute-done.2.f_oth, ...), custom_call_target="tpu_custom_call" | custom-call | flops 1610612736 | bytes 4194304 | tf_op jit(solution)/shard_map/pallas_call | solution.py:45
  18.7 5.0 %shard_map.211 = bf16[512,128]{1,0:T(8,128)(2,1)S(1)} custom-call(bf16[176,512]{1,0:T(8,128)(2,1)S(1)} %collective-permute-done.1.packed_ref, bf16[512,2048]{1,0:T(8,128)(2,1)S(1)} %shard_map.210.table_ref, bf16[512,256]{1,0:T(8,128)(2,1)S(1)} %copy-done.13, bf16[512,256]{1,0:T(8,128)(2,1)S(1)} %collective-permute-done.5.lr_oth, ...), custom_call_target="tpu_custom_call" | custom-call | flops 4000000000 | bytes 4194304 | tf_op jit(solution)/shard_map/pallas_call | solution.py:45
  23.7 4.0 %collective-permute-start.7 = (bf16[512,128]{1,0:T(8,128)(2,1)S(1)}, bf16[512,128]{1,0:T(8,128)(2,1)S(1)}, u32[]{:S(2)}, u32[]{:S(2)}) collective-permute-start(bf16[512,128]{1,0:T(8,128)(2,1)S(1)} %shard_map.211), channel_id=1, source_target_pairs={{0,2},{2,4},{4,6},{6,8},{8,10},{10,12},{12,14},{3,1},{5,3},{7,5},{... | collective-permute-start | bytes 393224 | tf_op jit(solution)/shard_map/ppermute | solution.py:467
  27.8 0.9 %copy-done.15 = bf16[512,256]{1,0:T(8,128)(2,1)S(1)} copy-done((bf16[512,256]{1,0:T(8,128)(2,1)S(1)}, bf16[512,256]{1,0:T(8,128)(2,1)}, u32[]{:S(2)}) %copy-start.15) | copy-done | bytes 262168
  28.7 3.8 %shard_map.212.own_ref = f32[512,64]{1,0:T(8,128)S(1)} custom-call(bf16[176,512]{1,0:T(8,128)(2,1)S(1)} %shard_map.209.packed_ref, bf16[512,2048]{1,0:T(8,128)(2,1)S(1)} %shard_map.210.table_ref, bf16[512,256]{1,0:T(8,128)(2,1)S(1)} %copy-done.13, bf16[512,256]{1,0:T(8,128)(2,1)S(1)} %copy-done.15, bf16[4,256]{1,0:T(4,128)(2,1)S(1)} %copy-done.16, ...), custom_call_target="tpu_custom_call" | custom-call | flops 4000000000 | bytes 4194304 | tf_op jit(solution)/shard_map/pallas_call | solution.py:45
  32.6 0.5 collective-permute-start.8
  33.1 1.0 %collective-permute-done.9.own_oth_ref = f32[512,64]{1,0:T(8,128)S(1)} collective-permute-done((f32[512,64]{1,0:T(8,128)S(1)}, f32[512,64]{1,0:T(8,128)S(1)}, u32[]{:S(2)}, u32[]{:S(2)}) %collective-permute-start.9) | collective-permute-done | bytes 131104 | tf_op jit(solution)/shard_map/ppermute | solution.py:390
  34.1 0.2 collective-permute-done.8.near_oth_ref
  34.3 1.2 %shard_map.213 = (bf16[128,512]{1,0:T(8,128)(2,1)S(1)}, bf16[128,512]{1,0:T(8,128)(2,1)}) custom-call(bf16[176,512]{1,0:T(8,128)(2,1)S(1)} %shard_map.209.packed_ref, bf16[512,128]{1,0:T(8,128)(2,1)S(1)} %collective-permute-done.7.near_ref, bf16[512,128]{1,0:T(8,128)(2,1)S(1)} %collective-permute-done.8.near_oth_ref, f32[512,64]{1,0:T(8,128)S(1)} %shard_map.212.own_ref, ...), custom_call_target="tpu_custom_call" | custom-call | tf_op jit(solution)/shard_map/pallas_call | solution.py:45
  35.5 0.1 collective-permute-start.13
  35.6 0.4 collective-permute-start.12
  36.0 0.1 collective-permute-start.11
  36.2 0.4 collective-permute-start.14
  36.5 0.1 collective-permute-start.15
  36.7 0.7 %collective-permute-done.12.pe_oth = bf16[4,256]{1,0:T(4,128)(2,1)S(1)} collective-permute-done((bf16[4,256]{1,0:T(4,128)(2,1)S(1)}, bf16[4,256]{1,0:T(4,128)(2,1)S(1)}, u32[]{:S(2)}, u32[]{:S(2)}) %collective-permute-start.12) | collective-permute-done | bytes 2080 | tf_op jit(solution)/shard_map/ppermute | solution.py:390
  37.4 0.1 collective-permute-start.16
  37.6 4.5 %all-to-all-start.1 = ((bf16[8,16,512]{2,1,0:T(8,128)(2,1)}), bf16[8,16,512]{2,1,0:T(8,128)(2,1)S(1)}, u32[]{:S(2)}, u32[]{:S(2)}) async-start(bf16[8,16,512]{2,1,0:T(8,128)(2,1)} %bitcast.5), calls=%async_computation.1 | async-start | bytes 262144 | tf_op jit(solution)/shard_map/all_to_all | solution.py:476
  42.4 0.7 %copy-done.7 = bf16[512,256]{1,0:T(8,128)(2,1)} copy-done((bf16[512,256]{1,0:T(8,128)(2,1)}, bf16[512,256]{1,0:T(8,128)(2,1)S(1)}, u32[]{:S(2)}) %copy-start.7) | copy-done | bytes 262168
  43.1 0.9 %copy-done.6 = bf16[512,256]{1,0:T(8,128)(2,1)S(1)} copy-done((bf16[512,256]{1,0:T(8,128)(2,1)S(1)}, bf16[512,256]{1,0:T(8,128)(2,1)}, u32[]{:S(2)}) %copy-start.6) | copy-done | bytes 262168
  44.0 0.9 %copy-done.8 = bf16[512,256]{1,0:T(8,128)(2,1)S(1)} copy-done((bf16[512,256]{1,0:T(8,128)(2,1)S(1)}, bf16[512,256]{1,0:T(8,128)(2,1)}, u32[]{:S(2)}) %copy-start.8) | copy-done | bytes 262168
  45.0 0.7 %shard_map.214 = (f32[128,512]{1,0:T(8,128)S(1)}, f32[128,512]{1,0:T(8,128)S(1)}) custom-call(bf16[128,512]{1,0:T(8,128)(2,1)S(1)} %get-tuple-element.34.mid_ref, s32[1,128]{1,0:T(1,128)S(1)} %reshape.39.receivers_ref, bf16[4,128]{1,0:T(4,128)(2,1)S(1)} %copy-done.12, bf16[512,256]{1,0:T(8,128)(2,1)S(1)} %copy-done.6, bf16[512,256]{1,0:T(8,128)(2,1)S(1)} %copy-done.8, ...), custom_call_target="tpu_custom_call" | custom-call | tf_op jit(solution)/shard_map/pallas_call | solution.py:45
  45.7 3.9 %all-to-all-done.1 = bf16[8,16,512]{2,1,0:T(8,128)(2,1)S(1)} async-done(((bf16[8,16,512]{2,1,0:T(8,128)(2,1)}), bf16[8,16,512]{2,1,0:T(8,128)(2,1)S(1)}, u32[]{:S(2)}, u32[]{:S(2)}) %all-to-all-start.1) | async-done | bytes 131104 | tf_op jit(solution)/shard_map/all_to_all | solution.py:476
  49.6 1.9 %shard_map.215 = bf16[128,256]{1,0:T(8,128)(2,1)} custom-call(bf16[128,512]{1,0:T(8,128)(2,1)S(1)} %bitcast.10, f32[128,512]{1,0:T(8,128)S(1)} %get-tuple-element.38.base_ref, f32[128,512]{1,0:T(8,128)S(1)} %get-tuple-element.39.upper_ref, bf16[128,512]{1,0:T(8,128)(2,1)S(1)} %get-tuple-element.34.mid_ref, s32[1,128]{1,0:T(1,128)S(1)} %reshape.39.receivers_ref, ...), custom_call_target="tpu_custom_call" | custom-call | tf_op jit(solution)/shard_map/pallas_call | solution.py:45
  (55 shorter events, 0.6 us)
Async XLA Ops:
  0.0 2.2 %collective-permute-start = (bf16[128,256]{1,0:T(8,128)(2,1)}, bf16[128,256]{1,0:T(8,128)(2,1)S(1)}, u32[]{:S(2)}, u32[]{:S(2)}) collective-permute-start(bf16[128,256]{1,0:T(8,128)(2,1)} %own_ref.1), channel_id=1, source_target_pairs={{0,1},{1,0},{2,3},{3,2},{4,5},{5,4},{6,7},{7,6},{8,9},{9,8},{10,11... | collective-permute-start | bytes 196616 | tf_op jit(solution)/shard_map/ppermute | solution.py:390
  3.1 10.5 %collective-permute-start.3 = (bf16[256,512]{1,0:T(8,128)(2,1)}, bf16[256,512]{1,0:T(8,128)(2,1)S(1)}, u32[]{:S(2)}, u32[]{:S(2)}) collective-permute-start(bf16[256,512]{1,0:T(8,128)(2,1)} %s_hbm.1), channel_id=1, source_target_pairs={{0,1},{1,0},{2,3},{3,2},{4,5},{5,4},{6,7},{7,6},{8,9},{9,8},{10,11... | collective-permute-start | bytes 786440 | tf_op jit(solution)/shard_map/ppermute | solution.py:390
  3.2 10.9 %collective-permute-start.4 = (bf16[512,256]{1,0:T(8,128)(2,1)}, bf16[512,256]{1,0:T(8,128)(2,1)S(1)}, u32[]{:S(2)}, u32[]{:S(2)}) collective-permute-start(bf16[512,256]{1,0:T(8,128)(2,1)} %l_hbm.1), channel_id=1, source_target_pairs={{0,1},{1,0},{2,3},{3,2},{4,5},{5,4},{6,7},{7,6},{8,9},{9,8},{10,11... | collective-permute-start | bytes 786440 | tf_op jit(solution)/shard_map/ppermute | solution.py:390
  3.7 9.9 %collective-permute-start.2 = (bf16[227,256]{1,0:T(8,128)(2,1)}, bf16[227,256]{1,0:T(8,128)(2,1)S(1)}, u32[]{:S(2)}, u32[]{:S(2)}) collective-permute-start(bf16[227,256]{1,0:T(8,128)(2,1)} %f_hbm.1), channel_id=1, source_target_pairs={{0,1},{1,0},{2,3},{3,2},{4,5},{5,4},{6,7},{7,6},{8,9},{9,8},{10,11... | collective-permute-start | bytes 348680 | tf_op jit(solution)/shard_map/ppermute | solution.py:390
  3.8 14.8 %collective-permute-start.5 = (bf16[512,256]{1,0:T(8,128)(2,1)}, bf16[512,256]{1,0:T(8,128)(2,1)S(1)}, u32[]{:S(2)}, u32[]{:S(2)}) collective-permute-start(bf16[512,256]{1,0:T(8,128)(2,1)} %lr_own.1), channel_id=1, source_target_pairs={{0,1},{1,0},{2,3},{3,2},{4,5},{5,4},{6,7},{7,6},{8,9},{9,8},{10,11... | collective-permute-start | bytes 786440 | tf_op jit(solution)/shard_map/ppermute | solution.py:390
  4.2 14.4 %collective-permute-start.1 = (bf16[176,512]{1,0:T(8,128)(2,1)S(1)}, bf16[176,512]{1,0:T(8,128)(2,1)S(1)}, u32[]{:S(2)}, u32[]{:S(2)}) collective-permute-start(bf16[176,512]{1,0:T(8,128)(2,1)S(1)} %shard_map.209.packed_ref), channel_id=1, source_target_pairs={{2,0},{4,2},{6,4},{8,6},{10,8},{12,10},{14,12},{1,3},{3,5},{5,7},{... | collective-permute-start | bytes 540680 | tf_op jit(solution)/shard_map/ppermute | solution.py:416
  5.5 27.6 %all-to-all-start = ((bf16[8,16,512]{2,1,0:T(8,128)(2,1)}), bf16[8,16,512]{2,1,0:T(8,128)(2,1)S(1)}, u32[]{:S(2)}, u32[]{:S(2)}) async-start(bf16[8,16,512]{2,1,0:T(8,128)(2,1)} %bitcast.3), calls=%async_computation | async-start | bytes 262144 | tf_op jit(solution)/shard_map/all_to_all | solution.py:422
  13.6 5.0 %collective-permute-start.6 = (bf16[4,256]{1,0:T(4,128)(2,1)}, bf16[4,256]{1,0:T(4,128)(2,1)S(1)}, u32[]{:S(2)}, u32[]{:S(2)}) collective-permute-start(bf16[4,256]{1,0:T(4,128)(2,1)} %le_own.1), channel_id=1, source_target_pairs={{0,1},{1,0},{2,3},{3,2},{4,5},{5,4},{6,7},{7,6},{8,9},{9,8},{10,11... | collective-permute-start | bytes 6152 | tf_op jit(solution)/shard_map/ppermute | solution.py:390
  13.6 19.5 %collective-permute-start.10 = (bf16[256,512]{1,0:T(8,128)(2,1)}, bf16[256,512]{1,0:T(8,128)(2,1)S(1)}, u32[]{:S(2)}, u32[]{:S(2)}) collective-permute-start(bf16[256,512]{1,0:T(8,128)(2,1)} %lo_own), channel_id=1, source_target_pairs={{0,1},{1,0},{2,3},{3,2},{4,5},{5,4},{6,7},{7,6},{8,9},{9,8},{10,11... | collective-permute-start | bytes 786440 | tf_op jit(solution)/shard_map/ppermute | solution.py:390
  14.1 4.5 %copy-start.16 = (bf16[4,256]{1,0:T(4,128)(2,1)S(1)}, bf16[4,256]{1,0:T(4,128)(2,1)}, u32[]{:S(2)}) copy-start(bf16[4,256]{1,0:T(4,128)(2,1)} %le_own.1) | copy-start | bytes 6148
  18.6 5.0 %copy-start.14 = (bf16[512,256]{1,0:T(8,128)(2,1)}, bf16[512,256]{1,0:T(8,128)(2,1)S(1)}, u32[]{:S(2)}) copy-start(bf16[512,256]{1,0:T(8,128)(2,1)S(1)} %collective-permute-done.5.lr_oth) | copy-start | bytes 786436
  23.6 10.7 %copy-start.1 = (bf16[256,512]{1,0:T(8,128)(2,1)S(1)}, bf16[256,512]{1,0:T(8,128)(2,1)}, u32[]{:S(2)}) copy-start(bf16[256,512]{1,0:T(8,128)(2,1)} %lo_own) | copy-start | bytes 786436
  23.7 11.8 %copy-start = (bf16[1024,256]{1,0:T(8,128)(2,1)S(1)}, bf16[1024,256]{1,0:T(8,128)(2,1)}, u32[]{:S(2)}) copy-start(bf16[1024,256]{1,0:T(8,128)(2,1)} %nf_own.1) | copy-start | bytes 1572868
  23.7 12.0 %copy-start.10 = (bf16[4,256]{1,0:T(4,128)(2,1)S(1)}, bf16[4,256]{1,0:T(4,128)(2,1)}, u32[]{:S(2)}) copy-start(bf16[4,256]{1,0:T(4,128)(2,1)} %pe_own) | copy-start | bytes 6148
  23.7 12.3 %copy-start.5 = (bf16[512,256]{1,0:T(8,128)(2,1)S(1)}, bf16[512,256]{1,0:T(8,128)(2,1)}, u32[]{:S(2)}) copy-start(bf16[512,256]{1,0:T(8,128)(2,1)} %pr_own) | copy-start | bytes 786436
  23.7 12.5 %copy-start.2 = (bf16[512,256]{1,0:T(8,128)(2,1)S(1)}, bf16[512,256]{1,0:T(8,128)(2,1)}, u32[]{:S(2)}) copy-start(bf16[512,256]{1,0:T(8,128)(2,1)} %ps_own) | copy-start | bytes 786436
  23.7 12.8 %copy-start.3 = (bf16[256,512]{1,0:T(8,128)(2,1)S(1)}, bf16[256,512]{1,0:T(8,128)(2,1)}, u32[]{:S(2)}) copy-start(bf16[256,512]{1,0:T(8,128)(2,1)} %po_own) | copy-start | bytes 786436
  23.7 13.7 %copy-start.4 = (bf16[256,512]{1,0:T(8,128)(2,1)S(1)}, bf16[256,512]{1,0:T(8,128)(2,1)}, u32[]{:S(2)}) copy-start(bf16[256,512]{1,0:T(8,128)(2,1)} %ns_own) | copy-start | bytes 786436
  23.7 19.3 %copy-start.12 = (bf16[4,128]{1,0:T(4,128)(2,1)S(1)}, bf16[4,128]{1,0:T(4,128)(2,1)}, u32[]{:S(2)}) copy-start(bf16[4,128]{1,0:T(4,128)(2,1)} %feats_ref.1) | copy-start | bytes 3076
  23.7 8.9 %collective-permute-start.7 = (bf16[512,128]{1,0:T(8,128)(2,1)S(1)}, bf16[512,128]{1,0:T(8,128)(2,1)S(1)}, u32[]{:S(2)}, u32[]{:S(2)}) collective-permute-start(bf16[512,128]{1,0:T(8,128)(2,1)S(1)} %shard_map.211), channel_id=1, source_target_pairs={{0,2},{2,4},{4,6},{6,8},{8,10},{10,12},{12,14},{3,1},{5,3},{7,5},{... | collective-permute-start | bytes 393224 | tf_op jit(solution)/shard_map/ppermute | solution.py:467
  28.7 13.4 %copy-start.17 = (s32[8,16]{1,0:T(8,128)S(1)}, s32[8,16]{1,0:T(8,128)}, u32[]{:S(2)}) copy-start(s32[8,16]{1,0:T(8,128)} %param.28) | copy-start | bytes 1540
  28.7 13.5 %copy-start.18 = (s32[1,8]{1,0:T(1,128)S(1)}, s32[1,8]{1,0:T(1,128)}, u32[]{:S(2)}) copy-start(s32[1,8]{1,0:T(1,128)} %param.29) | copy-start | bytes 100
  32.5 17.1 %copy-start.11 = (f32[256]{0:T(256)S(1)}, f32[256]{0:T(256)}, u32[]{:S(2)}) copy-start(f32[256]{0:T(256)} %param.43) | copy-start | bytes 3076
  32.5 1.6 %collective-permute-start.9 = (f32[512,64]{1,0:T(8,128)S(1)}, f32[512,64]{1,0:T(8,128)S(1)}, u32[]{:S(2)}, u32[]{:S(2)}) collective-permute-start(f32[512,64]{1,0:T(8,128)S(1)} %shard_map.212.own_ref), channel_id=1, source_target_pairs={{0,1},{1,0},{2,3},{3,2},{4,5},{5,4},{6,7},{7,6},{8,9},{9,8},{10,11... | collective-permute-start | bytes 393224 | tf_op jit(solution)/shard_map/ppermute | solution.py:390
  32.6 1.7 %collective-permute-start.8 = (bf16[512,128]{1,0:T(8,128)(2,1)S(1)}, bf16[512,128]{1,0:T(8,128)(2,1)S(1)}, u32[]{:S(2)}, u32[]{:S(2)}) collective-permute-start(bf16[512,128]{1,0:T(8,128)(2,1)S(1)} %collective-permute-done.7.near_ref), channel_id=1, source_target_pairs={{0,1},{1,0},{2,3},{3,2},{4,5},{5,4},{6,7},{7,6},{8,9},{9,8},{10,11... | collective-permute-start | bytes 393224 | tf_op jit(solution)/shard_map/ppermute | solution.py:390
  35.5 7.5 %collective-permute-start.13 = (bf16[1024,256]{1,0:T(8,128)(2,1)S(1)}, bf16[1024,256]{1,0:T(8,128)(2,1)S(1)}, u32[]{:S(2)}, u32[]{:S(2)}) collective-permute-start(bf16[1024,256]{1,0:T(8,128)(2,1)S(1)} %copy-done), channel_id=1, source_target_pairs={{0,1},{1,0},{2,3},{3,2},{4,5},{5,4},{6,7},{7,6},{8,9},{9,8},{10,11... | collective-permute-start | bytes 1572872 | tf_op jit(solution)/shard_map/ppermute | solution.py:390
  35.6 1.8 %collective-permute-start.12 = (bf16[4,256]{1,0:T(4,128)(2,1)S(1)}, bf16[4,256]{1,0:T(4,128)(2,1)S(1)}, u32[]{:S(2)}, u32[]{:S(2)}) collective-permute-start(bf16[4,256]{1,0:T(4,128)(2,1)S(1)} %copy-done.10), channel_id=1, source_target_pairs={{0,1},{1,0},{2,3},{3,2},{4,5},{5,4},{6,7},{7,6},{8,9},{9,8},{10,11... | collective-permute-start | bytes 6152 | tf_op jit(solution)/shard_map/ppermute | solution.py:390
  36.0 6.3 %collective-permute-start.11 = (bf16[512,256]{1,0:T(8,128)(2,1)S(1)}, bf16[512,256]{1,0:T(8,128)(2,1)S(1)}, u32[]{:S(2)}, u32[]{:S(2)}) collective-permute-start(bf16[512,256]{1,0:T(8,128)(2,1)S(1)} %copy-done.5), channel_id=1, source_target_pairs={{0,1},{1,0},{2,3},{3,2},{4,5},{5,4},{6,7},{7,6},{8,9},{9,8},{10,11... | collective-permute-start | bytes 786440 | tf_op jit(solution)/shard_map/ppermute | solution.py:390
  36.2 13.4 %collective-permute-start.14 = (bf16[512,256]{1,0:T(8,128)(2,1)S(1)}, bf16[512,256]{1,0:T(8,128)(2,1)S(1)}, u32[]{:S(2)}, u32[]{:S(2)}) collective-permute-start(bf16[512,256]{1,0:T(8,128)(2,1)S(1)} %copy-done.2), channel_id=1, source_target_pairs={{0,1},{1,0},{2,3},{3,2},{4,5},{5,4},{6,7},{7,6},{8,9},{9,8},{10,11... | collective-permute-start | bytes 786440 | tf_op jit(solution)/shard_map/ppermute | solution.py:390
  36.5 13.1 %collective-permute-start.15 = (bf16[256,512]{1,0:T(8,128)(2,1)S(1)}, bf16[256,512]{1,0:T(8,128)(2,1)S(1)}, u32[]{:S(2)}, u32[]{:S(2)}) collective-permute-start(bf16[256,512]{1,0:T(8,128)(2,1)S(1)} %copy-done.3), channel_id=1, source_target_pairs={{0,1},{1,0},{2,3},{3,2},{4,5},{5,4},{6,7},{7,6},{8,9},{9,8},{10,11... | collective-permute-start | bytes 786440 | tf_op jit(solution)/shard_map/ppermute | solution.py:390
  37.4 12.2 %collective-permute-start.16 = (bf16[256,512]{1,0:T(8,128)(2,1)S(1)}, bf16[256,512]{1,0:T(8,128)(2,1)S(1)}, u32[]{:S(2)}, u32[]{:S(2)}) collective-permute-start(bf16[256,512]{1,0:T(8,128)(2,1)S(1)} %copy-done.4), channel_id=1, source_target_pairs={{0,1},{1,0},{2,3},{3,2},{4,5},{5,4},{6,7},{7,6},{8,9},{9,8},{10,11... | collective-permute-start | bytes 786440 | tf_op jit(solution)/shard_map/ppermute | solution.py:390
  37.6 12.1 %all-to-all-start.1 = ((bf16[8,16,512]{2,1,0:T(8,128)(2,1)}), bf16[8,16,512]{2,1,0:T(8,128)(2,1)S(1)}, u32[]{:S(2)}, u32[]{:S(2)}) async-start(bf16[8,16,512]{2,1,0:T(8,128)(2,1)} %bitcast.5), calls=%async_computation.1 | async-start | bytes 262144 | tf_op jit(solution)/shard_map/all_to_all | solution.py:476
  (6 other events, 8.9 us)

commit v5 on v4

--- a/solution.py
+++ b/solution.py
@@ -52,12 +52,14 @@
     )(*args)
 
 
-def tail_body(slab_rows, width, senders_hbm, lengths_hbm, feats_hbm, mesh_hbm, out_ref, request_ref, senders_ref, lengths_ref, feats_ref, mesh_ref, turned, sems):
+def tail_body(slab_rows, width, senders_hbm, lengths_hbm, feats_hbm, mesh_hbm, le_hbm, pe_hbm, f_hbm, latent_hbm, s_hbm, l_hbm, out_ref, request_ref, edge_ref, latent_ref, early_ref, senders_ref, lengths_ref, feats_ref, mesh_ref, le_ref, pe_ref, f_ref, turned, sems):
     band = lax.axis_index("band")
     copies = fetch(
-        [(senders_hbm, senders_ref), (lengths_hbm, lengths_ref), (feats_hbm, feats_ref), (mesh_hbm, mesh_ref)], sems
-    )
-    for c in copies:
+        [(senders_hbm, senders_ref), (lengths_hbm, lengths_ref), (feats_hbm, feats_ref), (mesh_hbm, mesh_ref), (le_hbm, le_ref), (pe_hbm, pe_ref), (f_hbm, f_ref), (latent_hbm, latent_ref)]
+        + pack_copies((s_hbm, l_hbm), early_ref),
+        sems,
+    )
+    for c in copies[:6]:
         c.wait()
     slots, nodes = senders_ref.shape
     turned[...] = (senders_ref[...] - (band - 1) * slab_rows).astype(F32).T
@@ -87,7 +89,18 @@
     lists = dot(peer, mesh_ref[...].astype(F32).astype(BF16))
     own_slot = iota((edges, capacity), 0) % capacity == iota((edges, capacity), 1)
     single = jnp.where(own_slot, lists, 0.0).astype(BF16)
-    request_ref[...] = dot(single, jnp.ones((capacity, width), BF16)).astype(BF16)
+    request_ref[:, :LANES] = dot(single, jnp.ones((capacity, LANES), BF16)).astype(BF16)
+    request_ref[:, LANES:] = jnp.zeros((edges, width - LANES), BF16)
+    eight = lambda ref: jnp.concatenate(
+        [ref[...].astype(F32), jnp.zeros((8 - ref.shape[0], ref.shape[1]), F32)], axis=0
+    )
+    edge_ref[...] = jnp.concatenate([eight(le_ref), eight(pe_ref)], axis=0).astype(BF16)
+    for c in copies[6:]:
+        c.wait()
+    rows_f, half_width = f_ref.shape
+    early_ref[early_ref.shape[0] - (rows_f + 15) // 16 * 16 :, :] = jnp.concatenate(
+        [f_ref[...], jnp.zeros((-rows_f % 16, half_width), BF16)], axis=0
+    )
 
 
 def pack_body(own_ref, other_ref, tail_ref, out_ref):
@@ -107,31 +120,21 @@
     return copies
 
 
-def embed_body(tile, x_hbm, f_hbm, s_hbm, l_hbm, f_oth, s_oth, l_oth, out_ref, x_ref, f_own, s_own, l_own, first_t, joint_t, sems):
-    half = f_oth.shape[1]
-    tiles = x_ref.shape[1] // tile
-    moves = [(s_hbm, s_own), (l_hbm, l_own), (f_hbm, f_own)]
-    moves += [
-        (x_hbm.at[:, pl.ds(k * tile, tile)], x_ref.at[:, pl.ds(k * tile, tile)]) for k in range(tiles)
-    ]
-    copies = fetch(moves, sems)
-    first_t[half:, :] = f_oth[...].T
+def embed_body(x_hbm, own_ref, oth_ref, out_ref, x_ref, first_t, joint_t, sems):
+    copies = fetch([(x_hbm, x_ref)], sems)
+    half = own_ref.shape[1]
+    inputs = x_ref.shape[0]
+    width = 2 * half
+    for k, side in enumerate((own_ref, oth_ref)):
+        at = slice(k * half, (k + 1) * half)
+        first_t[at, :] = side[2 * width : 2 * width + inputs, :].T
+        for j, l in enumerate((own_ref, oth_ref)):
+            joint = dot(side[0:half, :], l[width : width + half, :])
+            joint = joint + dot(side[half:width, :], l[width + half : 2 * width, :])
+            joint_t[j * half : (j + 1) * half, at] = joint.astype(BF16).T
     copies[0].wait()
-    copies[1].wait()
-    for k, s in ((0, s_own), (1, s_oth)):
-        for j, l in ((0, l_own), (1, l_oth)):
-            joint = dot(s[...], l[...]).astype(BF16)
-            joint_t[j * half : (j + 1) * half, k * half : (k + 1) * half] = joint.T
-    copies[2].wait()
-    first_t[:half, :] = f_own[...].T
-    for c in copies[3:]:
-        c.wait()
-
-    @pl.loop(0, tiles)
-    def _(k):
-        at = pl.ds(pl.multiple_of(k * tile, tile), tile)
-        hidden = silu(dot(first_t[...], x_ref[:, at])).astype(BF16)
-        out_ref[:, at] = dot(joint_t[...], hidden).astype(BF16)
+    hidden = silu(dot(first_t[...], x_ref[...])).astype(BF16)
+    out_ref[...] = dot(joint_t[...], hidden).astype(BF16)
 
 
 def running(flag16, together):
@@ -143,7 +146,7 @@
     return inclusive + jnp.sum(dot(ones_where(earlier), flag16), axis=1, keepdims=True)
 
 
-def pool_part(high, low, feats, latent, kind, slots, room, spare, table_ref, weights, payload, late, right, out_ref):
+def pool_part(high, low, feats, latent, kind, slots, room, spare, step_size, table_ref, weights, payload, late, right, out_ref, midway=lambda: None):
     lr_own, lr_oth, le_own, le_oth = weights
     blocks = high.shape[0]
     nodes = latent.shape[0]
@@ -153,10 +156,10 @@
     width, table_rows = table_ref.shape
     per_slab = table_rows // LANES
     recv = jnp.concatenate([dot(latent, lr_own[...]), dot(latent, lr_oth[...])], axis=1)
-    edge = jnp.concatenate([le_own[...], le_oth[...]], axis=1).astype(F32)
+    edge = jnp.concatenate([le_own[...], le_oth[...]], axis=1).astype(F32)[0:8]
     right[0:nodes, :] = recv.astype(BF16)
     right[nodes:, :] = jnp.concatenate(
-        [edge, jnp.zeros((PAYLOAD_ROWS - edge.shape[0], width), F32)], axis=0
+        [edge, jnp.zeros((PAYLOAD_ROWS - 8, width), F32)], axis=0
     ).astype(BF16)
     base = (kind * per_slab + 1).astype(F32)
     local = high - base
@@ -216,12 +219,13 @@
         parts.append(picked(rows, 0.0, room, columns))
     if spare:
         parts.append(picked_late(0.0, spare))
+    midway()
     out_ref[...] = pooled(jnp.concatenate(parts, axis=1))
     count = jnp.sum(over_flag).astype(jnp.int32)
 
-    @pl.loop(0, jnp.maximum(count - spare + CHUNK - 1, 0) // CHUNK)
+    @pl.loop(0, jnp.maximum(count - spare + step_size - 1, 0) // step_size)
     def _(step):
-        out_ref[...] += pooled(picked_late((step * CHUNK + spare).astype(F32), CHUNK))
+        out_ref[...] += pooled(picked_late((step * step_size + spare).astype(F32), step_size))
 
 
 def unpack(packed_ref, nodes, slots):
@@ -240,7 +244,15 @@
     return high, low, feats
 
 
-def own_pool_body(nodes, slots, packed_ref, table_ref, lr_own, lr_oth, le_own, le_oth, out_ref, payload, late, right):
+def own_pool_body(nodes, slots, packed_ref, table_ref, lr_own, lr_oth, le_own, le_oth, pr_hbm, nf_hbm, ps_hbm, po_hbm, ns_hbm, out_ref, pack_hbm, payload, late, right, pack_ref, sems, pack_sem):
+    copies = fetch(pack_copies((pr_hbm, nf_hbm, ps_hbm, po_hbm, ns_hbm), pack_ref), sems)
+    leave = pltpu.make_async_copy(pack_ref, pack_hbm, pack_sem.at[0])
+
+    def midway():
+        for c in copies:
+            c.wait()
+        leave.start()
+
     first = lax.axis_index("ch") == 0
     high, low, feats = unpack(packed_ref, nodes, slots)
     half_blocks = high.shape[0] // 2
@@ -254,15 +266,18 @@
         latent,
         jnp.int32(1),
         slots,
+        CHUNK,
+        0,
         2 * CHUNK,
-        0,
         table_ref,
         (lr_own, lr_oth, le_own, le_oth),
         payload,
         late,
         right,
         out_ref,
-    )
+        midway,
+    )
+    leave.wait()
 
 
 def near_pool_body(nodes, slots, packed_ref, table_ref, lr_own, lr_oth, le_own, le_oth, out_ref, payload, late, right, total):
@@ -277,6 +292,7 @@
         slots,
         CHUNK,
         SPARE,
+        CHUNK,
         table_ref,
         (lr_own, lr_oth, le_own, le_oth),
         payload,
@@ -285,6 +301,17 @@
         total,
     )
     out_ref[...] = total[...].astype(BF16)
+
+
+def pack_copies(refs, packed_ref):
+    half = packed_ref.shape[1]
+    moves, top = [], 0
+    for ref in refs:
+        for c in range(0, ref.shape[1], half):
+            target = packed_ref.at[pl.ds(top, ref.shape[0]), :]
+            moves.append((ref.at[:, pl.ds(c, half)], target))
+            top += ref.shape[0]
+    return moves
 
 
 def middle_body(packed_ref, near_ref, near_oth_ref, own_ref, own_oth_ref, lo_own, lo_oth, request_ref, mid_ref, rows_ref):
@@ -307,45 +334,66 @@
     rows_ref[...] = dot(wanted, mid).astype(BF16)
 
 
-def base_body(mid_ref, receivers_ref, feats_ref, pr_own, pr_oth, pe_own, pe_oth, nf_own, nf_oth, base_ref, upper_ref):
+def base_body(mid_ref, receivers_ref, feats_ref, edge_own, edge_oth, late_own_hbm, late_oth_hbm, base_ref, upper_ref, last_own, last_oth, late_own, late_oth, sems):
     nodes, width = mid_ref.shape
+    copies = []
+    top = late_own.shape[0]
+    for k, (source, near_by, last) in enumerate(
+        ((late_own_hbm, late_own, last_own), (late_oth_hbm, late_oth, last_oth))
+    ):
+        copies += [
+            pltpu.make_async_copy(source.at[pl.ds(0, top), :], near_by, sems.at[2 * k]),
+            pltpu.make_async_copy(
+                source.at[pl.ds(top, last.shape[0]), :], last, sems.at[2 * k + 1]
+            ),
+        ]
+    for c in copies:
+        c.start()
+    copies[0].wait()
+    copies[2].wait()
     mid = mid_ref[...]
     edges = receivers_ref.shape[1]
     into = ones_where(iota((nodes, edges), 0) == receivers_ref[...])
     half = width // 2
-    for k, (pr, pe, nf) in enumerate(((pr_own, pe_own, nf_own), (pr_oth, pe_oth, nf_oth))):
+    for k, (edge, late) in enumerate(((edge_own, late_own), (edge_oth, late_oth))):
         at = slice(k * half, (k + 1) * half)
-        recv = dot(mid, pr[...])
-        high = recv.astype(BF16)
-        low = (recv - high.astype(F32)).astype(BF16)
+        recv = dot(mid, late[0:width, :])
+        top = recv.astype(BF16)
+        rest_of = (recv - top.astype(F32)).astype(BF16)
+        pe = edge[...].astype(F32)[8 : 8 + feats_ref.shape[0]].astype(BF16)
         base_ref[:, at] = (
-            dot_on(into, high, 0, 0) + dot_on(into, low, 0, 0) + dot_on(feats_ref[...], pe[...], 0, 0)
+            dot_on(into, top, 0, 0) + dot_on(into, rest_of, 0, 0) + dot_on(feats_ref[...], pe, 0, 0)
         )
-        upper_ref[:, at] = dot(mid, nf[0:width, :])
-
-
-def node_body(rows_ref, base_ref, upper_ref, mid_ref, receivers_ref, limit_ref, gain_ref, ps_own, ps_oth, po_own, po_oth, nf_own, nf_oth, ns_own, ns_oth, out_ref):
+        upper_ref[:, at] = dot(mid, late[width : 2 * width, :])
+    copies[1].wait()
+    copies[3].wait()
+
+
+def node_body(rows_ref, base_ref, upper_ref, mid_ref, receivers_ref, limit_ref, gain_ref, late_own, late_oth, out_ref):
     first = lax.axis_index("ch") == 0
     nodes, width = mid_ref.shape
     half = width // 2
+    wide = lambda late, top: jnp.concatenate(
+        [late[top : top + half, :], late[top + half : top + width, :]], axis=1
+    )
     rows = rows_ref[...]
     edges = rows.shape[0]
     into = ones_where(
         (iota((nodes, edges), 0) == receivers_ref[...]) & (limit_ref[...] > 0)
     )
     agg = None
-    for k, (ps, po) in enumerate(((ps_own, po_own), (ps_oth, po_oth))):
+    for k, late in enumerate((late_own, late_oth)):
         at = slice(k * half, (k + 1) * half)
-        sent = dot(rows, ps[...]).astype(BF16).astype(F32)
+        sent = dot(rows, late[width : 2 * width, :]).astype(BF16).astype(F32)
         act = silu(sent + base_ref[:, at]).astype(BF16)
-        term = dot(dot(into, act).astype(BF16), po[...])
+        term = dot(dot(into, act).astype(BF16), wide(late, 2 * width))
         agg = term if agg is None else agg + term
     agg = agg.astype(BF16)
     update = None
-    for k, (nf, ns) in enumerate(((nf_own, ns_own), (nf_oth, ns_oth))):
+    for k, late in enumerate((late_own, late_oth)):
         at = slice(k * half, (k + 1) * half)
-        hidden = silu(upper_ref[:, at] + dot(agg, nf[width:, :])).astype(BF16)
-        term = dot(hidden, ns[...])
+        hidden = silu(upper_ref[:, at] + dot(agg, late[0:width, :])).astype(BF16)
+        term = dot(hidden, wide(late, 3 * width))
         update = term if update is None else update + term
     mean = jnp.sum(update, axis=1, keepdims=True) / width
     square = jnp.sum(update * update, axis=1, keepdims=True) / width
@@ -400,62 +448,50 @@
     latent_other = other(mesh_latent)
     blocks = nodes * slots // LANES
     tail_rows = 4 * (nodes * slots // width) + blocks // 2
-    tail_inputs = [pin(a) for a in (grid_senders.T, grid_lengths.reshape(1, nodes), grid_feats, mesh_senders)]
-    tail, request = call(
+    tail_inputs = [pin(a) for a in (grid_senders.T, grid_lengths.reshape(1, nodes), grid_feats, mesh_senders, link_edge, proc_edge, embed_first, mesh_latent, embed_second, link_sender)]
+    inputs = grid_input.shape[1]
+    early_rows = 2 * width + (inputs + 15) // 16 * 16
+    tail, request, edge_own, latent_own, early_own = call(
         functools.partial(tail_body, slab_rows, width),
-        (shape((tail_rows, width), BF16), shape((edges, width), BF16)),
+        (shape((tail_rows, width), BF16), shape((edges, width), BF16), shape((16, half), BF16), shape(mesh_latent.shape, BF16), shape((early_rows, half), BF16)),
         tail_inputs,
-        in_specs=[hbm] * 4,
-        out_specs=(vmem, vmem),
-        scratch=[pltpu.VMEM(a.shape, a.dtype) for a in tail_inputs]
-        + [pltpu.VMEM((nodes, slots), F32), pltpu.SemaphoreType.DMA((4,))],
+        in_specs=[hbm] * 10,
+        out_specs=(vmem,) * 5,
+        scratch=[pltpu.VMEM(a.shape, a.dtype) for a in tail_inputs[:7]]
+        + [pltpu.VMEM((nodes, slots), F32), pltpu.SemaphoreType.DMA((11,))],
     )
     packed = call(
-        pack_body, shape((nodes + tail_rows, width), BF16), (mesh_latent, latent_other, tail)
+        pack_body, shape((nodes + tail_rows, width), BF16), (latent_own, latent_other, tail)
     )
     near_packed = lax.ppermute(packed, ("band", "ch"), to_owner)
     after = lambda token, *arrays: lax.optimization_barrier((token, *arrays))[1:]
-    embed_weights = after(packed, embed_first, embed_second, link_sender)
-    link_receiver, link_edge, link_out, request = after(
-        packed, link_receiver, link_edge, link_out, request
+    (early_out,) = after(packed, early_own)
+    link_receiver, edge_own, link_out, request = after(
+        packed, link_receiver, edge_own, link_out, request
     )
     request = lax.all_to_all(request, "band", 0, 0, tiled=True)
 
-    tile = slab_rows // 4
-    inputs = grid_input.shape[1]
     table = call(
-        functools.partial(embed_body, tile),
+        embed_body,
         shape((width, slab_rows), BF16),
-        (
-            *[pin(a) for a in (grid_input.T, embed_first, embed_second, link_sender)],
-            *[other(w) for w in embed_weights],
-        ),
-        in_specs=[hbm] * 4 + [vmem] * 3,
+        (pin(grid_input.T), early_own, other(early_out)),
+        in_specs=[hbm, vmem, vmem],
         out_specs=vmem,
         scratch=[pltpu.VMEM((inputs, slab_rows), BF16)]
-        + [pltpu.VMEM(w.shape, BF16) for w in embed_weights]
         + [pltpu.VMEM((width, n), BF16) for n in (inputs, width)]
-        + [pltpu.SemaphoreType.DMA((3 + slab_rows // tile,))],
+        + [pltpu.SemaphoreType.DMA((1,))],
         flops=2 * slab_rows * width * (256 + width),
         moved=4 * 1024 * 1024,
     )
 
-    link_weights = (link_receiver, other(link_receiver), link_edge, other(link_edge))
+    edge_other = other(edge_own)
+    link_weights = (link_receiver, other(link_receiver), edge_own, edge_other)
     group_slots = BLOCKS_PER_GROUP * LANES
     scratch = lambda count: [
         pltpu.VMEM((count // BLOCKS_PER_GROUP, PAYLOAD_ROWS, group_slots), BF16),
         pltpu.VMEM((count, LANES), F32),
         pltpu.VMEM((PAYLOAD_ROWS + count * LANES // slots, width), BF16),
     ]
-    own = call(
-        functools.partial(own_pool_body, nodes, slots),
-        shape((width, nodes // 2), F32),
-        (packed, table, *link_weights),
-        scratch=scratch(blocks // 2),
-        flops=4 * 10**9,
-        moved=4 * 1024 * 1024,
-    )
-    own_other = other(own)
     near = call(
         functools.partial(near_pool_body, nodes, slots),
         shape((width, nodes), BF16),
@@ -465,32 +501,59 @@
         moved=4 * 1024 * 1024,
     )
     near_back = lax.ppermute(near, ("band", "ch"), to_patch)
+    weights = (proc_receiver, node_first, proc_sender, proc_out, node_second)
+    own, late_own = call(
+        functools.partial(own_pool_body, nodes, slots),
+        (shape((width, nodes // 2), F32), pltpu.HBM((6 * width, half), BF16)),
+        (*after(near, packed), table, *link_weights, *[pin(w) for w in weights]),
+        in_specs=[vmem] * 6 + [hbm] * 5,
+        out_specs=(vmem, hbm),
+        scratch=scratch(blocks // 2)
+        + [pltpu.VMEM((6 * width, half), BF16)]
+        + [pltpu.SemaphoreType.DMA((7,)), pltpu.SemaphoreType.DMA((1,))],
+        flops=4 * 10**9,
+        moved=4 * 1024 * 1024,
+    )
+    own_other = other(own)
     near_back_other = other(near_back)
 
     lanes = lambda a: a.reshape(1, edges)
     mid, rows = call(
         middle_body,
-        (shape((nodes, width), BF16), shape((edges, width), BF16)),
-        (packed, near_back, near_back_other, own, own_other, link_out, other(link_out), request),
-    )
+        (
+            shape((nodes, width), BF16),
+            shape((edges, width), BF16),
+        ),
+        (
+            *(packed, near_back, near_back_other, own, own_other),
+            *(link_out, other(link_out), request),
+        ),
+    )
+    late_other = pin(other(*after(mid, late_own)))
     rows = lax.all_to_all(rows, "band", 0, 0, tiled=True)
-    pairs = []
-    for w in after(mid, proc_receiver, proc_edge, node_first, proc_sender, proc_out, node_second):
-        pairs.append((w, other(w)))
-    pr, pe, nf, ps, po, ns = pairs
     receivers = lanes(mesh_receivers)
     limit = lanes(
         mesh_counts.reshape(bands, 1) - jnp.arange(capacity, dtype=jnp.int32)[None, :]
     )
-    base, upper = call(
+    base, upper, last_own, last_other = call(
         base_body,
-        (shape((edges, width), F32), shape((nodes, width), F32)),
-        (mid, receivers, mesh_feats, *pr, *pe, *nf),
+        (
+            shape((edges, width), F32),
+            shape((nodes, width), F32),
+            *[shape((4 * width, half), BF16)] * 2,
+        ),
+        (mid, receivers, mesh_feats, edge_own, edge_other, pin(late_own), late_other),
+        in_specs=[vmem] * 5 + [hbm] * 2,
+        out_specs=(vmem,) * 4,
+        scratch=[pltpu.VMEM((2 * width, half), BF16)] * 2 + [pltpu.SemaphoreType.DMA((4,))],
     )
     return call(
         node_body,
         shape((nodes, half), BF16),
-        (rows, base, upper, mid, receivers, limit, norm_gain.reshape(1, half), *ps, *po, *nf, *ns),
+        (
+            *(rows, base, upper, mid, receivers, limit, norm_gain.reshape(1, half)),
+            *(last_own, last_other),
+        ),
     )
 
 

time: 52.1 us -> 47.9 us (0.919)
  local copies, waits for them, and re-layouts: 4.6 us -> 0.2 us
  Pallas kernels: 18.8 us -> 21.5 us
  starting transfers between devices: 21.8 us -> 19.4 us
    unnamed x38 -> x12, local copies, waits for them, and re-layouts: 4.44 us -> 0.04 us
    all_to_all x1, starting transfers between devices: 8.05 us -> 5.13 us  [per_device(): request = lax.all_to_all(request, 'band', 0, 0, tiled=True)]
    pallas_call x8, Pallas kernels: 18.8 us -> 21.5 us  [call(): pl.pallas_call(body, out_shape=out_shape, scratch_shapes=list(scratch), c...]
    ppermute x15 -> x8, starting transfers between devices: 3.96 us -> 5.21 us  [per_device(): other = lambda a: lax.ppermute(a, 'ch', [(0, 1), (1, 0)])]
    all_to_all x1, waiting for transfers between devices: 3.92 us -> 4.83 us  [per_device(): rows = lax.all_to_all(rows, 'band', 0, 0, tiled=True)]
    all_to_all x1, starting transfers between devices: 4.55 us -> 3.73 us  [per_device(): rows = lax.all_to_all(rows, 'band', 0, 0, tiled=True)]
    ppermute x15 -> x8, waiting for transfers between devices: 1.97 us -> 1.22 us  [per_device(): other = lambda a: lax.ppermute(a, 'ch', [(0, 1), (1, 0)])]
  transfers between devices with their start and end apart: 19 -> 12, of which waited for: 4 -> 3; matrix products, arithmetic and copies ran while one was open for 0% -> 0% of each run, Pallas kernels for 31% -> 39%
where the time goes in v5:
time: 47.9 us; the launch traced here: 47.4 us
  Pallas kernels  21.5 us (45%)
  starting transfers between devices  19.4 us (41%)
  waiting for transfers between devices  6.05 us (13%)
    pallas_call x8, Pallas kernels, call(): pl.pallas_call(body, out_shape=out_shape, scratch_shapes=list(scratch), c...  21.5 us
    ppermute x8, starting transfers between devices, per_device(): other = lambda a: lax.ppermute(a, 'ch', [(0, 1), (1, 0)])  5.21 us
    all_to_all x1, starting transfers between devices, per_device(): request = lax.all_to_all(request, 'band', 0, 0, tiled=True)  5.13 us
    all_to_all x1, waiting for transfers between devices, per_device(): rows = lax.all_to_all(rows, 'band', 0, 0, tiled=True)  4.83 us
    ppermute x1, starting transfers between devices, per_device(): near_back = lax.ppermute(near, ('band', 'ch'), to_patch)  4.05 us
    all_to_all x1, starting transfers between devices, per_device(): rows = lax.all_to_all(rows, 'band', 0, 0, tiled=True)  3.73 us
    ppermute x1, starting transfers between devices, per_device(): near_packed = lax.ppermute(packed, ('band', 'ch'), to_owner)  1.28 us
    ppermute x8, waiting for transfers between devices, per_device(): other = lambda a: lax.ppermute(a, 'ch', [(0, 1), (1, 0)])  1.22 us
  transfers between devices with their start and end apart: 12, of which 3 were waited for; matrix products, arithmetic and copies ran while one was open for 0% of the time, Pallas kernels for 39%

profile of v5, /device:TPU:0, one launch (start us, length us, event | category | flops | bytes accessed | tf_op | source)
XLA Modules:
  0.0 47.4 jit_solution(5977174583638639521)
XLA Ops:
  0.0 0.5 collective-permute-start
  0.5 2.0 %shard_map.208 = (bf16[48,512]{1,0:T(8,128)(2,1)S(1)}, bf16[128,512]{1,0:T(8,128)(2,1)}, bf16[16,256]{1,0:T(8,128)(2,1)S(1)}, bf16[128,256]{1,0:T(8,128)(2,1)S(1)}, bf16[1264,256]{1,0:T(8,128)(2,1)S(1)}) custom-call(s32[32,128]{1,0:T(8,128)} %bitcast.12, s32[1,128]{1,0:T(1,128)} %bitcast.14, bf16[4,4096]{1,0:T(4,128)(2,1)} %feats_hbm.1, s32[8,16]{1,0:T(8,128)} %mesh_hbm.1, ...), custom_call_target="tpu_custom_call" | custom-call | tf_op jit(solution)/shard_map/pallas_call | solution.py:45
  2.5 0.0 collective-permute-done.other_ref
  2.5 0.1 collective-permute-start.2
  2.6 0.5 collective-permute-start.3
  3.1 1.3 %collective-permute-start.1 = (bf16[176,512]{1,0:T(8,128)(2,1)S(1)}, bf16[176,512]{1,0:T(8,128)(2,1)S(1)}, u32[]{:S(2)}, u32[]{:S(2)}) collective-permute-start(bf16[176,512]{1,0:T(8,128)(2,1)S(1)} %shard_map.209.packed_ref), channel_id=1, source_target_pairs={{2,0},{4,2},{6,4},{8,6},{10,8},{12,10},{14,12},{1,3},{3,5},{5,7},{... | collective-permute-start | bytes 540680 | tf_op jit(solution)/shard_map/ppermute | solution.py:466
  4.4 3.4 %collective-permute-start.4 = (bf16[16,256]{1,0:T(8,128)(2,1)S(1)}, bf16[16,256]{1,0:T(8,128)(2,1)S(1)}, u32[]{:S(2)}, u32[]{:S(2)}) collective-permute-start(bf16[16,256]{1,0:T(8,128)(2,1)S(1)} %get-tuple-element.32.le_own.edge_own), channel_id=1, source_target_pairs={{0,1},{1,0},{2,3},{3,2},{4,5},{5,4},{6,7},{7,6},{8,9},{9,8},{10,11... | collective-permute-start | bytes 24584 | tf_op jit(solution)/shard_map/ppermute | solution.py:438
  7.8 0.1 collective-permute-start.8
  7.9 5.1 %all-to-all-start = ((bf16[8,16,512]{2,1,0:T(8,128)(2,1)}), bf16[8,16,512]{2,1,0:T(8,128)(2,1)S(1)}, u32[]{:S(2)}, u32[]{:S(2)}) async-start(bf16[8,16,512]{2,1,0:T(8,128)(2,1)} %bitcast.3), calls=%async_computation | async-start | bytes 262144 | tf_op jit(solution)/shard_map/all_to_all | solution.py:472
  13.0 0.0 copy-start.3
  13.0 3.5 %shard_map.210.table_ref = bf16[512,2048]{1,0:T(8,128)(2,1)S(1)} custom-call(bf16[227,2048]{1,0:T(8,128)(2,1)} %bitcast.15, bf16[1264,256]{1,0:T(8,128)(2,1)S(1)} %get-tuple-element.28.own_ref, bf16[1264,256]{1,0:T(8,128)(2,1)S(1)} %collective-permute-done.2.oth_ref), custom_call_target="tpu_custom_call" | custom-call | flops 1610612736 | bytes 4194304 | tf_op jit(solution)/shard_map/pallas_call | solution.py:45
  16.6 0.0 collective-permute-done.4.le_oth.edge_oth
  16.6 5.0 %shard_map.211 = bf16[512,128]{1,0:T(8,128)(2,1)S(1)} custom-call(bf16[176,512]{1,0:T(8,128)(2,1)S(1)} %collective-permute-done.1.packed_ref, bf16[512,2048]{1,0:T(8,128)(2,1)S(1)} %shard_map.210.table_ref, bf16[512,256]{1,0:T(8,128)(2,1)S(1)} %copy-done.3, bf16[512,256]{1,0:T(8,128)(2,1)S(1)} %collective-permute-done.3.lr_oth, ...), custom_call_target="tpu_custom_call" | custom-call | flops 4000000000 | bytes 4194304 | tf_op jit(solution)/shard_map/pallas_call | solution.py:45
  21.6 0.0 copy-start
  21.6 4.1 %collective-permute-start.5 = (bf16[512,128]{1,0:T(8,128)(2,1)S(1)}, bf16[512,128]{1,0:T(8,128)(2,1)S(1)}, u32[]{:S(2)}, u32[]{:S(2)}) collective-permute-start(bf16[512,128]{1,0:T(8,128)(2,1)S(1)} %shard_map.211), channel_id=1, source_target_pairs={{0,2},{2,4},{4,6},{6,8},{8,10},{10,12},{12,14},{3,1},{5,3},{7,5},{... | collective-permute-start | bytes 393224 | tf_op jit(solution)/shard_map/ppermute | solution.py:503
  25.7 5.6 %shard_map.212 = (f32[512,64]{1,0:T(8,128)S(1)}, bf16[3072,256]{1,0:T(8,128)(2,1)}) custom-call(bf16[176,512]{1,0:T(8,128)(2,1)S(1)} %shard_map.209.packed_ref, bf16[512,2048]{1,0:T(8,128)(2,1)S(1)} %shard_map.210.table_ref, bf16[512,256]{1,0:T(8,128)(2,1)S(1)} %copy-done.3, bf16[512,256]{1,0:T(8,128)(2,1)S(1)} %collective-permute-done.3.lr_oth, ...), custom_call_target="tpu_custom_call" | custom-call | flops 4000000000 | bytes 4194304 | tf_op jit(solution)/shard_map/pallas_call | solution.py:45
  31.3 0.0 copy-start.4
  31.3 0.0 copy-start.5
  31.3 0.0 copy-start.1
  31.3 0.1 collective-permute-start.7
  31.4 0.5 %collective-permute-start.6 = (bf16[512,128]{1,0:T(8,128)(2,1)S(1)}, bf16[512,128]{1,0:T(8,128)(2,1)S(1)}, u32[]{:S(2)}, u32[]{:S(2)}) collective-permute-start(bf16[512,128]{1,0:T(8,128)(2,1)S(1)} %collective-permute-done.5.near_ref), channel_id=1, source_target_pairs={{0,1},{1,0},{2,3},{3,2},{4,5},{5,4},{6,7},{7,6},{8,9},{9,8},{10,11... | collective-permute-start | bytes 393224 | tf_op jit(solution)/shard_map/ppermute | solution.py:438
  31.9 1.0 %collective-permute-done.7.own_oth_ref = f32[512,64]{1,0:T(8,128)S(1)} collective-permute-done((f32[512,64]{1,0:T(8,128)S(1)}, f32[512,64]{1,0:T(8,128)S(1)}, u32[]{:S(2)}, u32[]{:S(2)}) %collective-permute-start.7) | collective-permute-done | bytes 131104 | tf_op jit(solution)/shard_map/ppermute | solution.py:438
  33.0 0.2 collective-permute-done.6.near_oth_ref
  33.1 1.2 %shard_map.213 = (bf16[128,512]{1,0:T(8,128)(2,1)S(1)}, bf16[128,512]{1,0:T(8,128)(2,1)}) custom-call(bf16[176,512]{1,0:T(8,128)(2,1)S(1)} %shard_map.209.packed_ref, bf16[512,128]{1,0:T(8,128)(2,1)S(1)} %collective-permute-done.5.near_ref, bf16[512,128]{1,0:T(8,128)(2,1)S(1)} %collective-permute-done.6.near_oth_ref, ...), custom_call_target="tpu_custom_call" | custom-call | tf_op jit(solution)/shard_map/pallas_call | solution.py:45
  34.3 0.1 collective-permute-start.9
  34.4 3.7 %all-to-all-start.1 = ((bf16[8,16,512]{2,1,0:T(8,128)(2,1)}), bf16[8,16,512]{2,1,0:T(8,128)(2,1)S(1)}, u32[]{:S(2)}, u32[]{:S(2)}) async-start(bf16[8,16,512]{2,1,0:T(8,128)(2,1)} %bitcast.5), calls=%async_computation.1 | async-start | bytes 262144 | tf_op jit(solution)/shard_map/all_to_all | solution.py:533
  38.2 0.1 reshape.39.receivers_ref
  38.3 0.1 iota_subtract_fusion
  38.3 0.1 sub.29.limit_ref
  38.4 2.3 %shard_map.214 = (f32[128,512]{1,0:T(8,128)S(1)}, f32[128,512]{1,0:T(8,128)S(1)}, bf16[2048,256]{1,0:T(8,128)(2,1)S(1)}, bf16[2048,256]{1,0:T(8,128)(2,1)S(1)}) custom-call(bf16[128,512]{1,0:T(8,128)(2,1)S(1)} %get-tuple-element.38.mid_ref, s32[1,128]{1,0:T(1,128)S(1)} %reshape.39.receivers_ref, bf16[4,128]{1,0:T(4,128)(2,1)S(1)} %copy-done.1, ...), custom_call_target="tpu_custom_call" | custom-call | tf_op jit(solution)/shard_map/pallas_call | solution.py:45
  40.7 4.8 %all-to-all-done.1 = bf16[8,16,512]{2,1,0:T(8,128)(2,1)S(1)} async-done(((bf16[8,16,512]{2,1,0:T(8,128)(2,1)}), bf16[8,16,512]{2,1,0:T(8,128)(2,1)S(1)}, u32[]{:S(2)}, u32[]{:S(2)}) %all-to-all-start.1) | async-done | bytes 131104 | tf_op jit(solution)/shard_map/all_to_all | solution.py:533
  45.6 1.9 %shard_map.215 = bf16[128,256]{1,0:T(8,128)(2,1)} custom-call(bf16[128,512]{1,0:T(8,128)(2,1)S(1)} %bitcast.10, f32[128,512]{1,0:T(8,128)S(1)} %get-tuple-element.41.base_ref, f32[128,512]{1,0:T(8,128)S(1)} %get-tuple-element.42.upper_ref, bf16[128,512]{1,0:T(8,128)(2,1)S(1)} %get-tuple-element.38.mid_ref, s32[1,128]{1,0:T(1,128)S(1)} %reshape.39.receivers_ref, ...), custom_call_target="tpu_custom_call" | custom-call | tf_op jit(solution)/shard_map/pallas_call | solution.py:45
  (15 shorter events, 0.1 us)
Async XLA Ops:
  0.0 2.5 %collective-permute-start = (bf16[128,256]{1,0:T(8,128)(2,1)}, bf16[128,256]{1,0:T(8,128)(2,1)S(1)}, u32[]{:S(2)}, u32[]{:S(2)}) collective-permute-start(bf16[128,256]{1,0:T(8,128)(2,1)} %latent_hbm.1), channel_id=1, source_target_pairs={{0,1},{1,0},{2,3},{3,2},{4,5},{5,4},{6,7},{7,6},{8,9},{9,8},{10,11... | collective-permute-start | bytes 196616 | tf_op jit(solution)/shard_map/ppermute | solution.py:438
  2.5 10.5 %collective-permute-start.2 = (bf16[1264,256]{1,0:T(8,128)(2,1)S(1)}, bf16[1264,256]{1,0:T(8,128)(2,1)S(1)}, u32[]{:S(2)}, u32[]{:S(2)}) collective-permute-start(bf16[1264,256]{1,0:T(8,128)(2,1)S(1)} %get-tuple-element.28.own_ref), channel_id=1, source_target_pairs={{0,1},{1,0},{2,3},{3,2},{4,5},{5,4},{6,7},{7,6},{8,9},{9,8},{10,11... | collective-permute-start | bytes 1941512 | tf_op jit(solution)/shard_map/ppermute | solution.py:438
  2.6 14.0 %collective-permute-start.3 = (bf16[512,256]{1,0:T(8,128)(2,1)}, bf16[512,256]{1,0:T(8,128)(2,1)S(1)}, u32[]{:S(2)}, u32[]{:S(2)}) collective-permute-start(bf16[512,256]{1,0:T(8,128)(2,1)} %lr_own.1), channel_id=1, source_target_pairs={{0,1},{1,0},{2,3},{3,2},{4,5},{5,4},{6,7},{7,6},{8,9},{9,8},{10,11... | collective-permute-start | bytes 786440 | tf_op jit(solution)/shard_map/ppermute | solution.py:438
  3.1 13.5 %collective-permute-start.1 = (bf16[176,512]{1,0:T(8,128)(2,1)S(1)}, bf16[176,512]{1,0:T(8,128)(2,1)S(1)}, u32[]{:S(2)}, u32[]{:S(2)}) collective-permute-start(bf16[176,512]{1,0:T(8,128)(2,1)S(1)} %shard_map.209.packed_ref), channel_id=1, source_target_pairs={{2,0},{4,2},{6,4},{8,6},{10,8},{12,10},{14,12},{1,3},{3,5},{5,7},{... | collective-permute-start | bytes 540680 | tf_op jit(solution)/shard_map/ppermute | solution.py:466
  4.4 12.2 %collective-permute-start.4 = (bf16[16,256]{1,0:T(8,128)(2,1)S(1)}, bf16[16,256]{1,0:T(8,128)(2,1)S(1)}, u32[]{:S(2)}, u32[]{:S(2)}) collective-permute-start(bf16[16,256]{1,0:T(8,128)(2,1)S(1)} %get-tuple-element.32.le_own.edge_own), channel_id=1, source_target_pairs={{0,1},{1,0},{2,3},{3,2},{4,5},{5,4},{6,7},{7,6},{8,9},{9,8},{10,11... | collective-permute-start | bytes 24584 | tf_op jit(solution)/shard_map/ppermute | solution.py:438
  7.8 24.1 %collective-permute-start.8 = (bf16[256,512]{1,0:T(8,128)(2,1)}, bf16[256,512]{1,0:T(8,128)(2,1)S(1)}, u32[]{:S(2)}, u32[]{:S(2)}) collective-permute-start(bf16[256,512]{1,0:T(8,128)(2,1)} %lo_own), channel_id=1, source_target_pairs={{0,1},{1,0},{2,3},{3,2},{4,5},{5,4},{6,7},{7,6},{8,9},{9,8},{10,11... | collective-permute-start | bytes 786440 | tf_op jit(solution)/shard_map/ppermute | solution.py:438
  7.9 24.1 %all-to-all-start = ((bf16[8,16,512]{2,1,0:T(8,128)(2,1)}), bf16[8,16,512]{2,1,0:T(8,128)(2,1)S(1)}, u32[]{:S(2)}, u32[]{:S(2)}) async-start(bf16[8,16,512]{2,1,0:T(8,128)(2,1)} %bitcast.3), calls=%async_computation | async-start | bytes 262144 | tf_op jit(solution)/shard_map/all_to_all | solution.py:472
  13.0 3.6 %copy-start.3 = (bf16[512,256]{1,0:T(8,128)(2,1)S(1)}, bf16[512,256]{1,0:T(8,128)(2,1)}, u32[]{:S(2)}) copy-start(bf16[512,256]{1,0:T(8,128)(2,1)} %lr_own.1) | copy-start | bytes 786436
  21.6 11.5 %copy-start = (bf16[256,512]{1,0:T(8,128)(2,1)S(1)}, bf16[256,512]{1,0:T(8,128)(2,1)}, u32[]{:S(2)}) copy-start(bf16[256,512]{1,0:T(8,128)(2,1)} %lo_own) | copy-start | bytes 786436
  21.6 9.8 %collective-permute-start.5 = (bf16[512,128]{1,0:T(8,128)(2,1)S(1)}, bf16[512,128]{1,0:T(8,128)(2,1)S(1)}, u32[]{:S(2)}, u32[]{:S(2)}) collective-permute-start(bf16[512,128]{1,0:T(8,128)(2,1)S(1)} %shard_map.211), channel_id=1, source_target_pairs={{0,2},{2,4},{4,6},{6,8},{8,10},{10,12},{12,14},{3,1},{5,3},{7,5},{... | collective-permute-start | bytes 393224 | tf_op jit(solution)/shard_map/ppermute | solution.py:503
  31.3 6.9 %copy-start.4 = (s32[8,16]{1,0:T(8,128)S(1)}, s32[8,16]{1,0:T(8,128)}, u32[]{:S(2)}) copy-start(s32[8,16]{1,0:T(8,128)} %param.28) | copy-start | bytes 1540
  31.3 6.9 %copy-start.5 = (s32[1,8]{1,0:T(1,128)S(1)}, s32[1,8]{1,0:T(1,128)}, u32[]{:S(2)}) copy-start(s32[1,8]{1,0:T(1,128)} %param.29) | copy-start | bytes 100
  31.3 7.1 %copy-start.1 = (bf16[4,128]{1,0:T(4,128)(2,1)S(1)}, bf16[4,128]{1,0:T(4,128)(2,1)}, u32[]{:S(2)}) copy-start(bf16[4,128]{1,0:T(4,128)(2,1)} %feats_ref.1) | copy-start | bytes 3076
  31.3 1.6 %collective-permute-start.7 = (f32[512,64]{1,0:T(8,128)S(1)}, f32[512,64]{1,0:T(8,128)S(1)}, u32[]{:S(2)}, u32[]{:S(2)}) collective-permute-start(f32[512,64]{1,0:T(8,128)S(1)} %get-tuple-element.34.own_ref), channel_id=1, source_target_pairs={{0,1},{1,0},{2,3},{3,2},{4,5},{5,4},{6,7},{7,6},{8,9},{9,8},{10,11... | collective-permute-start | bytes 393224 | tf_op jit(solution)/shard_map/ppermute | solution.py:438
  31.4 1.7 %collective-permute-start.6 = (bf16[512,128]{1,0:T(8,128)(2,1)S(1)}, bf16[512,128]{1,0:T(8,128)(2,1)S(1)}, u32[]{:S(2)}, u32[]{:S(2)}) collective-permute-start(bf16[512,128]{1,0:T(8,128)(2,1)S(1)} %collective-permute-done.5.near_ref), channel_id=1, source_target_pairs={{0,1},{1,0},{2,3},{3,2},{4,5},{5,4},{6,7},{7,6},{8,9},{9,8},{10,11... | collective-permute-start | bytes 393224 | tf_op jit(solution)/shard_map/ppermute | solution.py:438
  34.3 4.1 %collective-permute-start.9 = (bf16[3072,256]{1,0:T(8,128)(2,1)}, bf16[3072,256]{1,0:T(8,128)(2,1)}, u32[]{:S(2)}, u32[]{:S(2)}) collective-permute-start(bf16[3072,256]{1,0:T(8,128)(2,1)} %get-tuple-element.40.late_own_hbm), channel_id=1, source_target_pairs={{0,1},{1,0},{2,3},{3,2},{4,5},{5,4},{6,7},{7,6},{8,9},{9,8},{10,11... | collective-permute-start | bytes 4718600 | tf_op jit(solution)/shard_map/ppermute | solution.py:438
  34.4 11.1 %all-to-all-start.1 = ((bf16[8,16,512]{2,1,0:T(8,128)(2,1)}), bf16[8,16,512]{2,1,0:T(8,128)(2,1)S(1)}, u32[]{:S(2)}, u32[]{:S(2)}) async-start(bf16[8,16,512]{2,1,0:T(8,128)(2,1)} %bitcast.5), calls=%async_computation.1 | async-start | bytes 262144 | tf_op jit(solution)/shard_map/all_to_all | solution.py:533
  38.4 7.1 %copy-start.2 = (f32[256]{0:T(256)S(1)}, f32[256]{0:T(256)}, u32[]{:S(2)}) copy-start(f32[256]{0:T(256)} %param.43) | copy-start | bytes 3076

commit v6 on v5

--- a/solution.py
+++ b/solution.py
@@ -12,6 +12,7 @@
 LANES = 128
 CHUNK = 256
 SPARE = 128
+ROOM = CHUNK - SPARE // 4
 PAYLOAD_ROWS = 16
 BLOCKS_PER_GROUP = 8
 VMEM_LIMIT = 48 * 1024 * 1024
@@ -120,8 +121,9 @@
     return copies
 
 
-def embed_body(x_hbm, own_ref, oth_ref, out_ref, x_ref, first_t, joint_t, sems):
-    copies = fetch([(x_hbm, x_ref)], sems)
+def embed_body(x_hbm, own_ref, oth_ref, pr_hbm, nf_hbm, ps_hbm, po_hbm, ns_hbm, out_ref, pack_hbm, x_ref, first_t, joint_t, pack_ref, sems, pack_sem):
+    copies = fetch([(x_hbm, x_ref)] + pack_copies((pr_hbm, nf_hbm, ps_hbm, po_hbm, ns_hbm), pack_ref), sems)
+    leave = pltpu.make_async_copy(pack_ref, pack_hbm, pack_sem.at[0])
     half = own_ref.shape[1]
     inputs = x_ref.shape[0]
     width = 2 * half
@@ -134,7 +136,11 @@
             joint_t[j * half : (j + 1) * half, at] = joint.astype(BF16).T
     copies[0].wait()
     hidden = silu(dot(first_t[...], x_ref[...])).astype(BF16)
+    for c in copies[1:]:
+        c.wait()
+    leave.start()
     out_ref[...] = dot(joint_t[...], hidden).astype(BF16)
+    leave.wait()
 
 
 def running(flag16, together):
@@ -146,7 +152,7 @@
     return inclusive + jnp.sum(dot(ones_where(earlier), flag16), axis=1, keepdims=True)
 
 
-def pool_part(high, low, feats, latent, kind, slots, room, spare, step_size, table_ref, weights, payload, late, right, out_ref, midway=lambda: None):
+def pool_part(high, low, feats, latent, kind, slots, room, spare, step_size, table_ref, weights, payload, late, right, out_ref):
     lr_own, lr_oth, le_own, le_oth = weights
     blocks = high.shape[0]
     nodes = latent.shape[0]
@@ -219,7 +225,6 @@
         parts.append(picked(rows, 0.0, room, columns))
     if spare:
         parts.append(picked_late(0.0, spare))
-    midway()
     out_ref[...] = pooled(jnp.concatenate(parts, axis=1))
     count = jnp.sum(over_flag).astype(jnp.int32)
 
@@ -244,17 +249,23 @@
     return high, low, feats
 
 
-def own_pool_body(nodes, slots, packed_ref, table_ref, lr_own, lr_oth, le_own, le_oth, pr_hbm, nf_hbm, ps_hbm, po_hbm, ns_hbm, out_ref, pack_hbm, payload, late, right, pack_ref, sems, pack_sem):
-    copies = fetch(pack_copies((pr_hbm, nf_hbm, ps_hbm, po_hbm, ns_hbm), pack_ref), sems)
-    leave = pltpu.make_async_copy(pack_ref, pack_hbm, pack_sem.at[0])
-
-    def midway():
-        for c in copies:
-            c.wait()
-        leave.start()
-
-    first = lax.axis_index("ch") == 0
+def place_of():
+    band, core = lax.axis_index("band"), lax.axis_index("ch")
+    last = lax.axis_size("band") - 1
+    idle = ((core == 1) & (band == 0)) | ((core == 0) & (band == last))
+    return core, idle, (band == 0) | (band == last)
+
+
+def keep_nodes(high, slots, masked, parity):
+    odd = iota(high.shape, 1) // slots % 2
+    return jnp.where(masked & (odd != parity), 0.0, high)
+
+
+def own_pool_body(nodes, slots, near_ref, packed_ref, table_ref, lr_own, lr_oth, le_own, le_oth, out_ref, payload, late, right, total):
+    core, idle, edge = place_of()
+    first = core == 0
     high, low, feats = unpack(packed_ref, nodes, slots)
+    high = keep_nodes(high, slots, edge, 1)
     half_blocks = high.shape[0] // 2
     half_groups = len(feats) // 2
     pick = lambda a, b: jnp.where(first, a, b)
@@ -268,29 +279,38 @@
         slots,
         CHUNK,
         0,
-        2 * CHUNK,
+        CHUNK,
         table_ref,
         (lr_own, lr_oth, le_own, le_oth),
         payload,
         late,
         right,
-        out_ref,
-        midway,
-    )
-    leave.wait()
-
-
-def near_pool_body(nodes, slots, packed_ref, table_ref, lr_own, lr_oth, le_own, le_oth, out_ref, payload, late, right, total):
-    high, low, feats = unpack(packed_ref, nodes, slots)
-    kind = 2 * lax.axis_index("ch")
+        total,
+    )
+    mine = total[...]
+    none = jnp.zeros(mine.shape, F32)
+    both = jnp.concatenate([pick(mine, none), pick(none, mine)], axis=1)
+    out_ref[...] = (both + jnp.where(idle, near_ref[...].astype(F32), 0.0)).astype(BF16)
+
+
+def near_pool_body(nodes, slots, packed_ref, own_ref, table_ref, lr_own, lr_oth, le_own, le_oth, out_ref, payload, late, right, total):
+    core, idle, _ = place_of()
+    own = unpack(own_ref, nodes, slots)
+    near = unpack(packed_ref, nodes, slots)
+    pick = lambda a, b: jnp.where(idle, a, b)
+    high = pick(keep_nodes(own[0], slots, True, 0), near[0])
+    low = pick(own[1], near[1])
+    feats = [pick(a, b) for a, b in zip(own[2], near[2])]
+    latent = pick(own_ref[0:nodes, :], packed_ref[0:nodes, :])
+    kind = pick(1, 2 * core)
     pool_part(
         high,
         low,
         feats,
-        packed_ref[0:nodes, :],
+        latent,
         kind,
         slots,
-        CHUNK,
+        ROOM,
         SPARE,
         CHUNK,
         table_ref,
@@ -315,18 +335,13 @@
 
 
 def middle_body(packed_ref, near_ref, near_oth_ref, own_ref, own_oth_ref, lo_own, lo_oth, request_ref, mid_ref, rows_ref):
-    first = lax.axis_index("ch") == 0
     half = lo_own.shape[0]
     nodes = near_ref.shape[1]
-    mine, theirs = own_ref[...], own_oth_ref[...]
     flip = lambda a: jnp.concatenate([a[half:, :], a[:half, :]], axis=0)
-    theirs = flip(theirs)
-    total = near_ref[...].astype(F32) + flip(near_oth_ref[...]).astype(F32)
-    total = total + jnp.concatenate(
-        [jnp.where(first, mine, theirs), jnp.where(first, theirs, mine)], axis=1
-    )
-    pool = total.astype(BF16).T
-    agg = dot(pool[:, :half], lo_own[...]) + dot(pool[:, half:], lo_oth[...])
+    wide = lambda a, b: a[...].astype(F32) + b[...].astype(F32)
+    total = wide(near_ref, own_ref) + flip(wide(near_oth_ref, own_oth_ref))
+    pool = total.astype(BF16)
+    agg = dot_on(pool[:half], lo_own[...], 0, 0) + dot_on(pool[half:], lo_oth[...], 0, 0)
     mid = (packed_ref[0:nodes, :].astype(F32) + agg).astype(BF16)
     mid_ref[...] = mid
     request = request_ref[...].astype(F32)
@@ -334,23 +349,15 @@
     rows_ref[...] = dot(wanted, mid).astype(BF16)
 
 
-def base_body(mid_ref, receivers_ref, feats_ref, edge_own, edge_oth, late_own_hbm, late_oth_hbm, base_ref, upper_ref, last_own, last_oth, late_own, late_oth, sems):
+def base_body(mid_ref, receivers_ref, feats_ref, edge_own, edge_oth, own_hbm, oth_hbm, base_ref, upper_ref, last_own, last_oth, late_own, late_oth, sems):
     nodes, width = mid_ref.shape
-    copies = []
     top = late_own.shape[0]
-    for k, (source, near_by, last) in enumerate(
-        ((late_own_hbm, late_own, last_own), (late_oth_hbm, late_oth, last_oth))
-    ):
-        copies += [
-            pltpu.make_async_copy(source.at[pl.ds(0, top), :], near_by, sems.at[2 * k]),
-            pltpu.make_async_copy(
-                source.at[pl.ds(top, last.shape[0]), :], last, sems.at[2 * k + 1]
-            ),
-        ]
-    for c in copies:
-        c.start()
+    rest = last_own.shape[0]
+    moves = [(own_hbm.at[pl.ds(0, top), :], late_own), (oth_hbm.at[pl.ds(0, top), :], late_oth)]
+    moves += [(own_hbm.at[pl.ds(top, rest), :], last_own), (oth_hbm.at[pl.ds(top, rest), :], last_oth)]
+    copies = fetch(moves, sems)
     copies[0].wait()
-    copies[2].wait()
+    copies[1].wait()
     mid = mid_ref[...]
     edges = receivers_ref.shape[1]
     into = ones_where(iota((nodes, edges), 0) == receivers_ref[...])
@@ -365,8 +372,8 @@
             dot_on(into, top, 0, 0) + dot_on(into, rest_of, 0, 0) + dot_on(feats_ref[...], pe, 0, 0)
         )
         upper_ref[:, at] = dot(mid, late[width : 2 * width, :])
-    copies[1].wait()
-    copies[3].wait()
+    for c in copies[2:]:
+        c.wait()
 
 
 def node_body(rows_ref, base_ref, upper_ref, mid_ref, receivers_ref, limit_ref, gain_ref, late_own, late_oth, out_ref):
@@ -471,15 +478,19 @@
     )
     request = lax.all_to_all(request, "band", 0, 0, tiled=True)
 
-    table = call(
+    table, late = call(
         embed_body,
-        shape((width, slab_rows), BF16),
-        (pin(grid_input.T), early_own, other(early_out)),
-        in_specs=[hbm, vmem, vmem],
-        out_specs=vmem,
+        (shape((width, slab_rows), BF16), pltpu.HBM((6 * width, half), BF16)),
+        (
+            *(pin(grid_input.T), early_own, other(early_out)),
+            *[pin(w) for w in (proc_receiver, node_first, proc_sender, proc_out, node_second)],
+        ),
+        in_specs=[hbm, vmem, vmem] + [hbm] * 5,
+        out_specs=(vmem, hbm),
         scratch=[pltpu.VMEM((inputs, slab_rows), BF16)]
         + [pltpu.VMEM((width, n), BF16) for n in (inputs, width)]
-        + [pltpu.SemaphoreType.DMA((1,))],
+        + [pltpu.VMEM((6 * width, half), BF16)]
+        + [pltpu.SemaphoreType.DMA((8,)), pltpu.SemaphoreType.DMA((1,))],
         flops=2 * slab_rows * width * (256 + width),
         moved=4 * 1024 * 1024,
     )
@@ -495,22 +506,17 @@
     near = call(
         functools.partial(near_pool_body, nodes, slots),
         shape((width, nodes), BF16),
-        (near_packed, table, *link_weights),
+        (near_packed, packed, table, *link_weights),
         scratch=scratch(blocks) + [pltpu.VMEM((width, nodes), F32)],
         flops=4 * 10**9,
         moved=4 * 1024 * 1024,
     )
     near_back = lax.ppermute(near, ("band", "ch"), to_patch)
-    weights = (proc_receiver, node_first, proc_sender, proc_out, node_second)
-    own, late_own = call(
+    own = call(
         functools.partial(own_pool_body, nodes, slots),
-        (shape((width, nodes // 2), F32), pltpu.HBM((6 * width, half), BF16)),
-        (*after(near, packed), table, *link_weights, *[pin(w) for w in weights]),
-        in_specs=[vmem] * 6 + [hbm] * 5,
-        out_specs=(vmem, hbm),
-        scratch=scratch(blocks // 2)
-        + [pltpu.VMEM((6 * width, half), BF16)]
-        + [pltpu.SemaphoreType.DMA((7,)), pltpu.SemaphoreType.DMA((1,))],
+        shape((width, nodes), BF16),
+        (near, packed, table, *link_weights),
+        scratch=scratch(blocks // 2) + [pltpu.VMEM((width, nodes // 2), F32)],
         flops=4 * 10**9,
         moved=4 * 1024 * 1024,
     )
@@ -529,7 +535,7 @@
             *(link_out, other(link_out), request),
         ),
     )
-    late_other = pin(other(*after(mid, late_own)))
+    late_other = pin(other(*after(mid, late)))
     rows = lax.all_to_all(rows, "band", 0, 0, tiled=True)
     receivers = lanes(mesh_receivers)
     limit = lanes(
@@ -542,7 +548,7 @@
             shape((nodes, width), F32),
             *[shape((4 * width, half), BF16)] * 2,
         ),
-        (mid, receivers, mesh_feats, edge_own, edge_other, pin(late_own), late_other),
+        (mid, receivers, mesh_feats, edge_own, edge_other, pin(late), late_other),
         in_specs=[vmem] * 5 + [hbm] * 2,
         out_specs=(vmem,) * 4,
         scratch=[pltpu.VMEM((2 * width, half), BF16)] * 2 + [pltpu.SemaphoreType.DMA((4,))],

time: 47.9 us -> 47.2 us (0.985)
  Pallas kernels: 21.5 us -> 19.8 us
  starting transfers between devices: 19.4 us -> 20.1 us
    pallas_call x8, Pallas kernels: 21.5 us -> 19.8 us  [call(): pl.pallas_call(body, out_shape=out_shape, scratch_shapes=list(scratch), c...]
    all_to_all x1, starting transfers between devices: 3.73 us -> 4.22 us  [per_device(): rows = lax.all_to_all(rows, 'band', 0, 0, tiled=True)]
  transfers between devices with their start and end apart: 12 -> 12, of which waited for: 3 -> 3; matrix products, arithmetic and copies ran while one was open for 0% -> 0% of each run, Pallas kernels for 39% -> 36%
where the time goes in v6:
time: 47.2 us; the launch traced here: 46.7 us
  starting transfers between devices  20.1 us (43%)
  Pallas kernels  19.8 us (42%)
  waiting for transfers between devices  6.29 us (13%)
    pallas_call x8, Pallas kernels, call(): pl.pallas_call(body, out_shape=out_shape, scratch_shapes=list(scratch), c...  19.8 us
    ppermute x8, starting transfers between devices, per_device(): other = lambda a: lax.ppermute(a, 'ch', [(0, 1), (1, 0)])  5.39 us
    all_to_all x1, waiting for transfers between devices, per_device(): rows = lax.all_to_all(rows, 'band', 0, 0, tiled=True)  5.26 us
    all_to_all x1, starting transfers between devices, per_device(): request = lax.all_to_all(request, 'band', 0, 0, tiled=True)  5.13 us
    all_to_all x1, starting transfers between devices, per_device(): rows = lax.all_to_all(rows, 'band', 0, 0, tiled=True)  4.22 us
    ppermute x1, starting transfers between devices, per_device(): near_back = lax.ppermute(near, ('band', 'ch'), to_patch)  4.05 us
    ppermute x1, starting transfers between devices, per_device(): near_packed = lax.ppermute(packed, ('band', 'ch'), to_owner)  1.28 us
    ppermute x8, waiting for transfers between devices, per_device(): other = lambda a: lax.ppermute(a, 'ch', [(0, 1), (1, 0)])  1.03 us
  transfers between devices with their start and end apart: 12, of which 3 were waited for; matrix products, arithmetic and copies ran while one was open for 0% of the time, Pallas kernels for 36%

profile of v6, /device:TPU:0, one launch (start us, length us, event | category | flops | bytes accessed | tf_op | source)
XLA Modules:
  0.0 46.7 jit_solution(12626184834989246758)
XLA Ops:
  0.0 0.5 collective-permute-start
  0.5 2.0 %shard_map.208 = (bf16[48,512]{1,0:T(8,128)(2,1)S(1)}, bf16[128,512]{1,0:T(8,128)(2,1)}, bf16[16,256]{1,0:T(8,128)(2,1)S(1)}, bf16[128,256]{1,0:T(8,128)(2,1)S(1)}, bf16[1264,256]{1,0:T(8,128)(2,1)S(1)}) custom-call(s32[32,128]{1,0:T(8,128)} %bitcast.12, s32[1,128]{1,0:T(1,128)} %bitcast.14, bf16[4,4096]{1,0:T(4,128)(2,1)} %feats_hbm.1, s32[8,16]{1,0:T(8,128)} %mesh_hbm.1, ...), custom_call_target="tpu_custom_call" | custom-call | tf_op jit(solution)/shard_map/pallas_call | solution.py:46
  2.5 0.1 collective-permute-start.2
  2.6 0.5 collective-permute-start.3
  3.1 1.3 %collective-permute-start.1 = (bf16[176,512]{1,0:T(8,128)(2,1)S(1)}, bf16[176,512]{1,0:T(8,128)(2,1)S(1)}, u32[]{:S(2)}, u32[]{:S(2)}) collective-permute-start(bf16[176,512]{1,0:T(8,128)(2,1)S(1)} %shard_map.209.own_ref.packed_ref), channel_id=1, source_target_pairs={{2,0},{4,2},{6,4},{8,6},{10,8},{12,10},{14,12},{1,3},{3,5},{5,7},{... | collective-permute-start | bytes 540680 | tf_op jit(solution)/shard_map/ppermute | solution.py:473
  4.4 3.4 %collective-permute-start.4 = (bf16[16,256]{1,0:T(8,128)(2,1)S(1)}, bf16[16,256]{1,0:T(8,128)(2,1)S(1)}, u32[]{:S(2)}, u32[]{:S(2)}) collective-permute-start(bf16[16,256]{1,0:T(8,128)(2,1)S(1)} %get-tuple-element.32.le_own.edge_own), channel_id=1, source_target_pairs={{0,1},{1,0},{2,3},{3,2},{4,5},{5,4},{6,7},{7,6},{8,9},{9,8},{10,11... | collective-permute-start | bytes 24584 | tf_op jit(solution)/shard_map/ppermute | solution.py:445
  7.8 0.1 collective-permute-start.8
  7.9 5.1 %all-to-all-start = ((bf16[8,16,512]{2,1,0:T(8,128)(2,1)}), bf16[8,16,512]{2,1,0:T(8,128)(2,1)S(1)}, u32[]{:S(2)}, u32[]{:S(2)}) async-start(bf16[8,16,512]{2,1,0:T(8,128)(2,1)} %bitcast.3), calls=%async_computation | async-start | bytes 262144 | tf_op jit(solution)/shard_map/all_to_all | solution.py:479
  13.0 0.0 collective-permute-done.2.oth_ref
  13.0 0.0 copy-start.3
  13.0 3.8 %shard_map.210 = (bf16[512,2048]{1,0:T(8,128)(2,1)S(1)}, bf16[3072,256]{1,0:T(8,128)(2,1)}) custom-call(bf16[227,2048]{1,0:T(8,128)(2,1)} %bitcast.15, bf16[1264,256]{1,0:T(8,128)(2,1)S(1)} %get-tuple-element.27.own_ref, bf16[1264,256]{1,0:T(8,128)(2,1)S(1)} %collective-permute-done.2.oth_ref, bf16[512,256]{1,0:T(8,128)(2,1)} %pr_hbm.1, ...), custom_call_target="tpu_custom_call" | custom-call | flops 1610612736 | bytes 4194304 | tf_op jit(solution)/shard_map/pallas_call | solution.py:46
  16.8 0.0 collective-permute-done.1.packed_ref
  16.9 4.8 %shard_map.211.near_ref = bf16[512,128]{1,0:T(8,128)(2,1)S(1)} custom-call(bf16[176,512]{1,0:T(8,128)(2,1)S(1)} %collective-permute-done.1.packed_ref, bf16[176,512]{1,0:T(8,128)(2,1)S(1)} %shard_map.209.own_ref.packed_ref, bf16[512,2048]{1,0:T(8,128)(2,1)S(1)} %get-tuple-element.28.table_ref, bf16[512,256]{1,0:T(8,128)(2,1)S(1)} %copy-done.3, ...), custom_call_target="tpu_custom_call" | custom-call | flops 4000000000 | bytes 4194304 | tf_op jit(solution)/shard_map/pallas_call | solution.py:46
  21.6 0.0 copy-start
  21.7 4.1 %collective-permute-start.5 = (bf16[512,128]{1,0:T(8,128)(2,1)S(1)}, bf16[512,128]{1,0:T(8,128)(2,1)S(1)}, u32[]{:S(2)}, u32[]{:S(2)}) collective-permute-start(bf16[512,128]{1,0:T(8,128)(2,1)S(1)} %shard_map.211.near_ref), channel_id=1, source_target_pairs={{0,2},{2,4},{4,6},{6,8},{8,10},{10,12},{12,14},{3,1},{5,3},{7,5},{... | collective-permute-start | bytes 393224 | tf_op jit(solution)/shard_map/ppermute | solution.py:514
  25.7 4.3 %shard_map.212.own_ref = bf16[512,128]{1,0:T(8,128)(2,1)S(1)} custom-call(bf16[512,128]{1,0:T(8,128)(2,1)S(1)} %shard_map.211.near_ref, bf16[176,512]{1,0:T(8,128)(2,1)S(1)} %shard_map.209.own_ref.packed_ref, bf16[512,2048]{1,0:T(8,128)(2,1)S(1)} %get-tuple-element.28.table_ref, bf16[512,256]{1,0:T(8,128)(2,1)S(1)} %copy-done.3, ...), custom_call_target="tpu_custom_call" | custom-call | flops 4000000000 | bytes 4194304 | tf_op jit(solution)/shard_map/pallas_call | solution.py:46
  30.0 0.0 copy-start.5
  30.0 0.0 copy-start.6
  30.0 0.0 copy-start.1
  30.0 0.1 collective-permute-start.7
  30.1 0.5 %collective-permute-start.6 = (bf16[512,128]{1,0:T(8,128)(2,1)S(1)}, bf16[512,128]{1,0:T(8,128)(2,1)S(1)}, u32[]{:S(2)}, u32[]{:S(2)}) collective-permute-start(bf16[512,128]{1,0:T(8,128)(2,1)S(1)} %collective-permute-done.5.near_ref), channel_id=1, source_target_pairs={{0,1},{1,0},{2,3},{3,2},{4,5},{5,4},{6,7},{7,6},{8,9},{9,8},{10,11... | collective-permute-start | bytes 393224 | tf_op jit(solution)/shard_map/ppermute | solution.py:445
  30.6 0.8 %collective-permute-done.7.own_oth_ref = bf16[512,128]{1,0:T(8,128)(2,1)S(1)} collective-permute-done((bf16[512,128]{1,0:T(8,128)(2,1)S(1)}, bf16[512,128]{1,0:T(8,128)(2,1)S(1)}, u32[]{:S(2)}, u32[]{:S(2)}) %collective-permute-start.7) | collective-permute-done | bytes 131104 | tf_op jit(solution)/shard_map/ppermute | solution.py:445
  31.5 0.2 collective-permute-done.6.near_oth_ref
  31.6 1.1 %shard_map.213 = (bf16[128,512]{1,0:T(8,128)(2,1)S(1)}, bf16[128,512]{1,0:T(8,128)(2,1)}) custom-call(bf16[176,512]{1,0:T(8,128)(2,1)S(1)} %shard_map.209.own_ref.packed_ref, bf16[512,128]{1,0:T(8,128)(2,1)S(1)} %collective-permute-done.5.near_ref, bf16[512,128]{1,0:T(8,128)(2,1)S(1)} %collective-permute-done.6.near_oth_ref, ...), custom_call_target="tpu_custom_call" | custom-call | tf_op jit(solution)/shard_map/pallas_call | solution.py:46
  32.8 0.3 collective-permute-start.9
  33.1 4.2 %all-to-all-start.1 = ((bf16[8,16,512]{2,1,0:T(8,128)(2,1)}), bf16[8,16,512]{2,1,0:T(8,128)(2,1)S(1)}, u32[]{:S(2)}, u32[]{:S(2)}) async-start(bf16[8,16,512]{2,1,0:T(8,128)(2,1)} %bitcast.5), calls=%async_computation.1 | async-start | bytes 262144 | tf_op jit(solution)/shard_map/all_to_all | solution.py:539
  37.3 0.1 reshape.39.receivers_ref
  37.4 0.1 iota_subtract_fusion
  37.5 0.1 sub.29.limit_ref
  37.6 2.0 %shard_map.214 = (f32[128,512]{1,0:T(8,128)S(1)}, f32[128,512]{1,0:T(8,128)S(1)}, bf16[2048,256]{1,0:T(8,128)(2,1)S(1)}, bf16[2048,256]{1,0:T(8,128)(2,1)S(1)}) custom-call(bf16[128,512]{1,0:T(8,128)(2,1)S(1)} %get-tuple-element.36.mid_ref, s32[1,128]{1,0:T(1,128)S(1)} %reshape.39.receivers_ref, bf16[4,128]{1,0:T(4,128)(2,1)S(1)} %copy-done.1, ...), custom_call_target="tpu_custom_call" | custom-call | tf_op jit(solution)/shard_map/pallas_call | solution.py:46
  39.5 5.3 %all-to-all-done.1 = bf16[8,16,512]{2,1,0:T(8,128)(2,1)S(1)} async-done(((bf16[8,16,512]{2,1,0:T(8,128)(2,1)}), bf16[8,16,512]{2,1,0:T(8,128)(2,1)S(1)}, u32[]{:S(2)}, u32[]{:S(2)}) %all-to-all-start.1) | async-done | bytes 131104 | tf_op jit(solution)/shard_map/all_to_all | solution.py:539
  44.8 1.9 %shard_map.215 = bf16[128,256]{1,0:T(8,128)(2,1)} custom-call(bf16[128,512]{1,0:T(8,128)(2,1)S(1)} %bitcast.9, f32[128,512]{1,0:T(8,128)S(1)} %get-tuple-element.39.base_ref, f32[128,512]{1,0:T(8,128)S(1)} %get-tuple-element.40.upper_ref, bf16[128,512]{1,0:T(8,128)(2,1)S(1)} %get-tuple-element.36.mid_ref, s32[1,128]{1,0:T(1,128)S(1)} %reshape.39.receivers_ref, ...), custom_call_target="tpu_custom_call" | custom-call | tf_op jit(solution)/shard_map/pallas_call | solution.py:46
  (17 shorter events, 0.1 us)
Async XLA Ops:
  0.0 2.5 %collective-permute-start = (bf16[128,256]{1,0:T(8,128)(2,1)}, bf16[128,256]{1,0:T(8,128)(2,1)S(1)}, u32[]{:S(2)}, u32[]{:S(2)}) collective-permute-start(bf16[128,256]{1,0:T(8,128)(2,1)} %latent_hbm.1), channel_id=1, source_target_pairs={{0,1},{1,0},{2,3},{3,2},{4,5},{5,4},{6,7},{7,6},{8,9},{9,8},{10,11... | collective-permute-start | bytes 196616 | tf_op jit(solution)/shard_map/ppermute | solution.py:445
  2.5 10.5 %collective-permute-start.2 = (bf16[1264,256]{1,0:T(8,128)(2,1)S(1)}, bf16[1264,256]{1,0:T(8,128)(2,1)S(1)}, u32[]{:S(2)}, u32[]{:S(2)}) collective-permute-start(bf16[1264,256]{1,0:T(8,128)(2,1)S(1)} %get-tuple-element.27.own_ref), channel_id=1, source_target_pairs={{0,1},{1,0},{2,3},{3,2},{4,5},{5,4},{6,7},{7,6},{8,9},{9,8},{10,11... | collective-permute-start | bytes 1941512 | tf_op jit(solution)/shard_map/ppermute | solution.py:445
  2.6 14.2 %collective-permute-start.3 = (bf16[512,256]{1,0:T(8,128)(2,1)}, bf16[512,256]{1,0:T(8,128)(2,1)S(1)}, u32[]{:S(2)}, u32[]{:S(2)}) collective-permute-start(bf16[512,256]{1,0:T(8,128)(2,1)} %lr_own.1), channel_id=1, source_target_pairs={{0,1},{1,0},{2,3},{3,2},{4,5},{5,4},{6,7},{7,6},{8,9},{9,8},{10,11... | collective-permute-start | bytes 786440 | tf_op jit(solution)/shard_map/ppermute | solution.py:445
  3.1 13.8 %collective-permute-start.1 = (bf16[176,512]{1,0:T(8,128)(2,1)S(1)}, bf16[176,512]{1,0:T(8,128)(2,1)S(1)}, u32[]{:S(2)}, u32[]{:S(2)}) collective-permute-start(bf16[176,512]{1,0:T(8,128)(2,1)S(1)} %shard_map.209.own_ref.packed_ref), channel_id=1, source_target_pairs={{2,0},{4,2},{6,4},{8,6},{10,8},{12,10},{14,12},{1,3},{3,5},{5,7},{... | collective-permute-start | bytes 540680 | tf_op jit(solution)/shard_map/ppermute | solution.py:473
  4.4 12.5 %collective-permute-start.4 = (bf16[16,256]{1,0:T(8,128)(2,1)S(1)}, bf16[16,256]{1,0:T(8,128)(2,1)S(1)}, u32[]{:S(2)}, u32[]{:S(2)}) collective-permute-start(bf16[16,256]{1,0:T(8,128)(2,1)S(1)} %get-tuple-element.32.le_own.edge_own), channel_id=1, source_target_pairs={{0,1},{1,0},{2,3},{3,2},{4,5},{5,4},{6,7},{7,6},{8,9},{9,8},{10,11... | collective-permute-start | bytes 24584 | tf_op jit(solution)/shard_map/ppermute | solution.py:445
  7.8 22.8 %collective-permute-start.8 = (bf16[256,512]{1,0:T(8,128)(2,1)}, bf16[256,512]{1,0:T(8,128)(2,1)S(1)}, u32[]{:S(2)}, u32[]{:S(2)}) collective-permute-start(bf16[256,512]{1,0:T(8,128)(2,1)} %lo_own), channel_id=1, source_target_pairs={{0,1},{1,0},{2,3},{3,2},{4,5},{5,4},{6,7},{7,6},{8,9},{9,8},{10,11... | collective-permute-start | bytes 786440 | tf_op jit(solution)/shard_map/ppermute | solution.py:445
  7.9 22.8 %all-to-all-start = ((bf16[8,16,512]{2,1,0:T(8,128)(2,1)}), bf16[8,16,512]{2,1,0:T(8,128)(2,1)S(1)}, u32[]{:S(2)}, u32[]{:S(2)}) async-start(bf16[8,16,512]{2,1,0:T(8,128)(2,1)} %bitcast.3), calls=%async_computation | async-start | bytes 262144 | tf_op jit(solution)/shard_map/all_to_all | solution.py:479
  13.0 3.9 %copy-start.3 = (bf16[512,256]{1,0:T(8,128)(2,1)S(1)}, bf16[512,256]{1,0:T(8,128)(2,1)}, u32[]{:S(2)}) copy-start(bf16[512,256]{1,0:T(8,128)(2,1)} %lr_own.1) | copy-start | bytes 786436
  21.6 10.0 %copy-start = (bf16[256,512]{1,0:T(8,128)(2,1)S(1)}, bf16[256,512]{1,0:T(8,128)(2,1)}, u32[]{:S(2)}) copy-start(bf16[256,512]{1,0:T(8,128)(2,1)} %lo_own) | copy-start | bytes 786436
  21.6 11.1 %copy-start.4 = (bf16[3072,256]{1,0:T(8,128)(2,1)S(1)}, bf16[3072,256]{1,0:T(8,128)(2,1)}, u32[]{:S(2)}) copy-start(bf16[3072,256]{1,0:T(8,128)(2,1)} %get-tuple-element.38.own_hbm) | copy-start | bytes 4718596
  21.7 8.5 %collective-permute-start.5 = (bf16[512,128]{1,0:T(8,128)(2,1)S(1)}, bf16[512,128]{1,0:T(8,128)(2,1)S(1)}, u32[]{:S(2)}, u32[]{:S(2)}) collective-permute-start(bf16[512,128]{1,0:T(8,128)(2,1)S(1)} %shard_map.211.near_ref), channel_id=1, source_target_pairs={{0,2},{2,4},{4,6},{6,8},{8,10},{10,12},{12,14},{3,1},{5,3},{7,5},{... | collective-permute-start | bytes 393224 | tf_op jit(solution)/shard_map/ppermute | solution.py:514
  30.0 7.3 %copy-start.5 = (s32[8,16]{1,0:T(8,128)S(1)}, s32[8,16]{1,0:T(8,128)}, u32[]{:S(2)}) copy-start(s32[8,16]{1,0:T(8,128)} %param.28) | copy-start | bytes 1540
  30.0 7.4 %copy-start.6 = (s32[1,8]{1,0:T(1,128)S(1)}, s32[1,8]{1,0:T(1,128)}, u32[]{:S(2)}) copy-start(s32[1,8]{1,0:T(1,128)} %param.29) | copy-start | bytes 100
  30.0 7.5 %copy-start.1 = (bf16[4,128]{1,0:T(4,128)(2,1)S(1)}, bf16[4,128]{1,0:T(4,128)(2,1)}, u32[]{:S(2)}) copy-start(bf16[4,128]{1,0:T(4,128)(2,1)} %feats_ref.1) | copy-start | bytes 3076
  30.0 1.4 %collective-permute-start.7 = (bf16[512,128]{1,0:T(8,128)(2,1)S(1)}, bf16[512,128]{1,0:T(8,128)(2,1)S(1)}, u32[]{:S(2)}, u32[]{:S(2)}) collective-permute-start(bf16[512,128]{1,0:T(8,128)(2,1)S(1)} %shard_map.212.own_ref), channel_id=1, source_target_pairs={{0,1},{1,0},{2,3},{3,2},{4,5},{5,4},{6,7},{7,6},{8,9},{9,8},{10,11... | collective-permute-start | bytes 393224 | tf_op jit(solution)/shard_map/ppermute | solution.py:445
  30.1 1.5 %collective-permute-start.6 = (bf16[512,128]{1,0:T(8,128)(2,1)S(1)}, bf16[512,128]{1,0:T(8,128)(2,1)S(1)}, u32[]{:S(2)}, u32[]{:S(2)}) collective-permute-start(bf16[512,128]{1,0:T(8,128)(2,1)S(1)} %collective-permute-done.5.near_ref), channel_id=1, source_target_pairs={{0,1},{1,0},{2,3},{3,2},{4,5},{5,4},{6,7},{7,6},{8,9},{9,8},{10,11... | collective-permute-start | bytes 393224 | tf_op jit(solution)/shard_map/ppermute | solution.py:445
  32.8 4.8 %collective-permute-start.9 = (bf16[3072,256]{1,0:T(8,128)(2,1)S(1)}, bf16[3072,256]{1,0:T(8,128)(2,1)}, u32[]{:S(2)}, u32[]{:S(2)}) collective-permute-start(bf16[3072,256]{1,0:T(8,128)(2,1)S(1)} %copy-done.4), channel_id=1, source_target_pairs={{0,1},{1,0},{2,3},{3,2},{4,5},{5,4},{6,7},{7,6},{8,9},{9,8},{10,11... | collective-permute-start | bytes 4718600 | tf_op jit(solution)/shard_map/ppermute | solution.py:445
  33.1 11.7 %all-to-all-start.1 = ((bf16[8,16,512]{2,1,0:T(8,128)(2,1)}), bf16[8,16,512]{2,1,0:T(8,128)(2,1)S(1)}, u32[]{:S(2)}, u32[]{:S(2)}) async-start(bf16[8,16,512]{2,1,0:T(8,128)(2,1)} %bitcast.5), calls=%async_computation.1 | async-start | bytes 262144 | tf_op jit(solution)/shard_map/all_to_all | solution.py:539
  37.5 7.3 %copy-start.2 = (f32[256]{0:T(256)S(1)}, f32[256]{0:T(256)}, u32[]{:S(2)}) copy-start(f32[256]{0:T(256)} %param.43) | copy-start | bytes 3076

commit v7 on v6

--- a/solution.py
+++ b/solution.py
@@ -53,7 +53,7 @@
     )(*args)
 
 
-def tail_body(slab_rows, width, senders_hbm, lengths_hbm, feats_hbm, mesh_hbm, le_hbm, pe_hbm, f_hbm, latent_hbm, s_hbm, l_hbm, out_ref, request_ref, edge_ref, latent_ref, early_ref, senders_ref, lengths_ref, feats_ref, mesh_ref, le_ref, pe_ref, f_ref, turned, sems):
+def tail_body(slab_rows, width, senders_hbm, lengths_hbm, feats_hbm, mesh_hbm, le_hbm, pe_hbm, f_hbm, latent_hbm, s_hbm, l_hbm, out_ref, request_hbm, edge_ref, latent_ref, early_ref, senders_ref, lengths_ref, feats_ref, mesh_ref, le_ref, pe_ref, f_ref, turned, request_ref, sems, request_sem):
     band = lax.axis_index("band")
     copies = fetch(
         [(senders_hbm, senders_ref), (lengths_hbm, lengths_ref), (feats_hbm, feats_ref), (mesh_hbm, mesh_ref), (le_hbm, le_ref), (pe_hbm, pe_ref), (f_hbm, f_ref), (latent_hbm, latent_ref)]
@@ -62,6 +62,16 @@
     )
     for c in copies[:6]:
         c.wait()
+    peers, capacity = mesh_ref.shape
+    edges = peers * capacity
+    peer = ones_where(iota((edges, peers), 0) // capacity == iota((edges, peers), 1))
+    lists = dot(peer, mesh_ref[...].astype(F32).astype(BF16))
+    own_slot = iota((edges, capacity), 0) % capacity == iota((edges, capacity), 1)
+    single = jnp.where(own_slot, lists, 0.0).astype(BF16)
+    request_ref[:, :LANES] = dot(single, jnp.ones((capacity, LANES), BF16)).astype(BF16)
+    request_ref[:, LANES:] = jnp.zeros((edges, width - LANES), BF16)
+    leave = pltpu.make_async_copy(request_ref, request_hbm, request_sem.at[0])
+    leave.start()
     slots, nodes = senders_ref.shape
     turned[...] = (senders_ref[...] - (band - 1) * slab_rows).astype(F32).T
     per_row = LANES // slots
@@ -84,14 +94,6 @@
     places = [high[:half], low[:half], high[half:], low[half:]]
     tail = jnp.concatenate(parts + [jnp.concatenate(places, axis=1)], axis=0)
     out_ref[...] = tail.astype(BF16)
-    peers, capacity = mesh_ref.shape
-    edges = peers * capacity
-    peer = ones_where(iota((edges, peers), 0) // capacity == iota((edges, peers), 1))
-    lists = dot(peer, mesh_ref[...].astype(F32).astype(BF16))
-    own_slot = iota((edges, capacity), 0) % capacity == iota((edges, capacity), 1)
-    single = jnp.where(own_slot, lists, 0.0).astype(BF16)
-    request_ref[:, :LANES] = dot(single, jnp.ones((capacity, LANES), BF16)).astype(BF16)
-    request_ref[:, LANES:] = jnp.zeros((edges, width - LANES), BF16)
     eight = lambda ref: jnp.concatenate(
         [ref[...].astype(F32), jnp.zeros((8 - ref.shape[0], ref.shape[1]), F32)], axis=0
     )
@@ -102,6 +104,7 @@
     early_ref[early_ref.shape[0] - (rows_f + 15) // 16 * 16 :, :] = jnp.concatenate(
         [f_ref[...], jnp.zeros((-rows_f % 16, half_width), BF16)], axis=0
     )
+    leave.wait()
 
 
 def pack_body(own_ref, other_ref, tail_ref, out_ref):
@@ -460,12 +463,13 @@
     early_rows = 2 * width + (inputs + 15) // 16 * 16
     tail, request, edge_own, latent_own, early_own = call(
         functools.partial(tail_body, slab_rows, width),
-        (shape((tail_rows, width), BF16), shape((edges, width), BF16), shape((16, half), BF16), shape(mesh_latent.shape, BF16), shape((early_rows, half), BF16)),
+        (shape((tail_rows, width), BF16), pltpu.HBM((edges, width), BF16), shape((16, half), BF16), shape(mesh_latent.shape, BF16), shape((early_rows, half), BF16)),
         tail_inputs,
         in_specs=[hbm] * 10,
-        out_specs=(vmem,) * 5,
+        out_specs=(vmem, hbm, vmem, vmem, vmem),
         scratch=[pltpu.VMEM(a.shape, a.dtype) for a in tail_inputs[:7]]
-        + [pltpu.VMEM((nodes, slots), F32), pltpu.SemaphoreType.DMA((11,))],
+        + [pltpu.VMEM((nodes, slots), F32), pltpu.VMEM((edges, width), BF16)]
+        + [pltpu.SemaphoreType.DMA((11,)), pltpu.SemaphoreType.DMA((1,))],
     )
     packed = call(
         pack_body, shape((nodes + tail_rows, width), BF16), (latent_own, latent_other, tail)
@@ -473,9 +477,7 @@
     near_packed = lax.ppermute(packed, ("band", "ch"), to_owner)
     after = lambda token, *arrays: lax.optimization_barrier((token, *arrays))[1:]
     (early_out,) = after(packed, early_own)
-    link_receiver, edge_own, link_out, request = after(
-        packed, link_receiver, edge_own, link_out, request
-    )
+    link_receiver, edge_own, request = after(packed, link_receiver, edge_own, request)
     request = lax.all_to_all(request, "band", 0, 0, tiled=True)
 
     table, late = call(
@@ -532,7 +534,7 @@
         ),
         (
             *(packed, near_back, near_back_other, own, own_other),
-            *(link_out, other(link_out), request),
+            *(link_out, other(*after(near, link_out)), request),
         ),
     )
     late_other = pin(other(*after(mid, late)))

time: 47.2 us -> 47 us (level)
  Pallas kernels: 19.8 us -> 17.7 us
  starting transfers between devices: 20.1 us -> 21.4 us
  waiting for transfers between devices: 6.29 us -> 7.09 us
    pallas_call x8, Pallas kernels: 19.8 us -> 17.7 us  [call(): pl.pallas_call(body, out_shape=out_shape, scratch_shapes=list(scratch), c...]
    all_to_all x1, starting transfers between devices: 4.22 us -> 5.97 us  [per_device(): rows = lax.all_to_all(rows, 'band', 0, 0, tiled=True)]
    ppermute x1, waiting for transfers between devices: 0.01 us -> 0.49 us  [per_device(): near_back = lax.ppermute(near, ('band', 'ch'), to_patch)]
  transfers between devices with their start and end apart: 12 -> 12, of which waited for: 3 -> 4; matrix products, arithmetic and copies ran while one was open for 0% -> 0% of each run, Pallas kernels for 36% -> 32%
where the time goes in v7:
time: 47 us; the launch traced here: 46.7 us
  starting transfers between devices  21.4 us (46%)
  Pallas kernels  17.7 us (38%)
  waiting for transfers between devices  7.09 us (15%)
    pallas_call x8, Pallas kernels, call(): pl.pallas_call(body, out_shape=out_shape, scratch_shapes=list(scratch), c...  17.7 us
    all_to_all x1, starting transfers between devices, per_device(): rows = lax.all_to_all(rows, 'band', 0, 0, tiled=True)  5.97 us
    all_to_all x1, waiting for transfers between devices, per_device(): rows = lax.all_to_all(rows, 'band', 0, 0, tiled=True)  5.24 us
    ppermute x8, starting transfers between devices, per_device(): other = lambda a: lax.ppermute(a, 'ch', [(0, 1), (1, 0)])  5.21 us
    all_to_all x1, starting transfers between devices, per_device(): request = lax.all_to_all(request, 'band', 0, 0, tiled=True)  4.87 us
    ppermute x1, starting transfers between devices, per_device(): near_back = lax.ppermute(near, ('band', 'ch'), to_patch)  4.05 us
    ppermute x8, waiting for transfers between devices, per_device(): other = lambda a: lax.ppermute(a, 'ch', [(0, 1), (1, 0)])  1.36 us
    ppermute x1, starting transfers between devices, per_device(): near_packed = lax.ppermute(packed, ('band', 'ch'), to_owner)  1.28 us
  transfers between devices with their start and end apart: 12, of which 4 were waited for; matrix products, arithmetic and copies ran while one was open for 0% of the time, Pallas kernels for 32%

profile of v7, /device:TPU:0, one launch (start us, length us, event | category | flops | bytes accessed | tf_op | source)
XLA Modules:
  0.0 46.7 jit_solution(18116748345302093675)
XLA Ops:
  0.0 0.5 collective-permute-start
  0.5 1.8 %shard_map.208 = (bf16[48,512]{1,0:T(8,128)(2,1)S(1)}, bf16[128,512]{1,0:T(8,128)(2,1)}, bf16[16,256]{1,0:T(8,128)(2,1)S(1)}, bf16[128,256]{1,0:T(8,128)(2,1)S(1)}, bf16[1264,256]{1,0:T(8,128)(2,1)S(1)}) custom-call(s32[32,128]{1,0:T(8,128)} %bitcast.13, s32[1,128]{1,0:T(1,128)} %bitcast.15, bf16[4,4096]{1,0:T(4,128)(2,1)} %feats_hbm.1, s32[8,16]{1,0:T(8,128)} %mesh_hbm.1, ...), custom_call_target="tpu_custom_call" | custom-call | tf_op jit(solution)/shard_map/pallas_call | solution.py:46
  2.3 0.1 collective-permute-start.2
  2.4 0.5 collective-permute-start.3
  2.9 1.3 %collective-permute-start.1 = (bf16[176,512]{1,0:T(8,128)(2,1)S(1)}, bf16[176,512]{1,0:T(8,128)(2,1)S(1)}, u32[]{:S(2)}, u32[]{:S(2)}) collective-permute-start(bf16[176,512]{1,0:T(8,128)(2,1)S(1)} %shard_map.209.own_ref.packed_ref), channel_id=1, source_target_pairs={{2,0},{4,2},{6,4},{8,6},{10,8},{12,10},{14,12},{1,3},{3,5},{5,7},{... | collective-permute-start | bytes 540680 | tf_op jit(solution)/shard_map/ppermute | solution.py:477
  4.2 3.4 %collective-permute-start.4 = (bf16[16,256]{1,0:T(8,128)(2,1)S(1)}, bf16[16,256]{1,0:T(8,128)(2,1)S(1)}, u32[]{:S(2)}, u32[]{:S(2)}) collective-permute-start(bf16[16,256]{1,0:T(8,128)(2,1)S(1)} %get-tuple-element.32.le_own.edge_own), channel_id=1, source_target_pairs={{0,1},{1,0},{2,3},{3,2},{4,5},{5,4},{6,7},{7,6},{8,9},{9,8},{10,11... | collective-permute-start | bytes 24584 | tf_op jit(solution)/shard_map/ppermute | solution.py:448
  7.6 4.9 %all-to-all-start = ((bf16[8,16,512]{2,1,0:T(8,128)(2,1)}), bf16[8,16,512]{2,1,0:T(8,128)(2,1)S(1)}, u32[]{:S(2)}, u32[]{:S(2)}) async-start(bf16[8,16,512]{2,1,0:T(8,128)(2,1)} %bitcast.12), calls=%async_computation | async-start | bytes 262144 | tf_op jit(solution)/shard_map/all_to_all | solution.py:481
  12.5 0.0 collective-permute-done.2.oth_ref
  12.5 0.0 copy-start.3
  12.5 3.8 %shard_map.210 = (bf16[512,2048]{1,0:T(8,128)(2,1)S(1)}, bf16[3072,256]{1,0:T(8,128)(2,1)}) custom-call(bf16[227,2048]{1,0:T(8,128)(2,1)} %bitcast.16, bf16[1264,256]{1,0:T(8,128)(2,1)S(1)} %get-tuple-element.27.own_ref, bf16[1264,256]{1,0:T(8,128)(2,1)S(1)} %collective-permute-done.2.oth_ref, bf16[512,256]{1,0:T(8,128)(2,1)} %pr_hbm.1, ...), custom_call_target="tpu_custom_call" | custom-call | flops 1610612736 | bytes 4194304 | tf_op jit(solution)/shard_map/pallas_call | solution.py:46
  16.3 0.0 collective-permute-done.4.le_oth.edge_oth
  16.3 0.0 copy-start
  16.4 4.8 %shard_map.211.near_ref = bf16[512,128]{1,0:T(8,128)(2,1)S(1)} custom-call(bf16[176,512]{1,0:T(8,128)(2,1)S(1)} %collective-permute-done.1.packed_ref, bf16[176,512]{1,0:T(8,128)(2,1)S(1)} %shard_map.209.own_ref.packed_ref, bf16[512,2048]{1,0:T(8,128)(2,1)S(1)} %get-tuple-element.28.table_ref, bf16[512,256]{1,0:T(8,128)(2,1)S(1)} %copy-done.3, ...), custom_call_target="tpu_custom_call" | custom-call | flops 4000000000 | bytes 4194304 | tf_op jit(solution)/shard_map/pallas_call | solution.py:46
  21.1 4.1 %collective-permute-start.5 = (bf16[512,128]{1,0:T(8,128)(2,1)S(1)}, bf16[512,128]{1,0:T(8,128)(2,1)S(1)}, u32[]{:S(2)}, u32[]{:S(2)}) collective-permute-start(bf16[512,128]{1,0:T(8,128)(2,1)S(1)} %shard_map.211.near_ref), channel_id=1, source_target_pairs={{0,2},{2,4},{4,6},{6,8},{8,10},{10,12},{12,14},{3,1},{5,3},{7,5},{... | collective-permute-start | bytes 393224 | tf_op jit(solution)/shard_map/ppermute | solution.py:516
  25.2 0.1 collective-permute-start.8
  25.3 2.4 %shard_map.212.own_ref = bf16[512,128]{1,0:T(8,128)(2,1)S(1)} custom-call(bf16[512,128]{1,0:T(8,128)(2,1)S(1)} %shard_map.211.near_ref, bf16[176,512]{1,0:T(8,128)(2,1)S(1)} %shard_map.209.own_ref.packed_ref, bf16[512,2048]{1,0:T(8,128)(2,1)S(1)} %get-tuple-element.28.table_ref, bf16[512,256]{1,0:T(8,128)(2,1)S(1)} %copy-done.3, ...), custom_call_target="tpu_custom_call" | custom-call | flops 4000000000 | bytes 4194304 | tf_op jit(solution)/shard_map/pallas_call | solution.py:46
  27.7 0.0 copy-start.5
  27.7 0.0 copy-start.6
  27.7 0.0 copy-start.1
  27.7 0.6 %collective-permute-start.7 = (bf16[512,128]{1,0:T(8,128)(2,1)S(1)}, bf16[512,128]{1,0:T(8,128)(2,1)S(1)}, u32[]{:S(2)}, u32[]{:S(2)}) collective-permute-start(bf16[512,128]{1,0:T(8,128)(2,1)S(1)} %shard_map.212.own_ref), channel_id=1, source_target_pairs={{0,1},{1,0},{2,3},{3,2},{4,5},{5,4},{6,7},{7,6},{8,9},{9,8},{10,11... | collective-permute-start | bytes 393224 | tf_op jit(solution)/shard_map/ppermute | solution.py:448
  28.3 0.5 %collective-permute-done.5.near_ref = bf16[512,128]{1,0:T(8,128)(2,1)S(1)} collective-permute-done((bf16[512,128]{1,0:T(8,128)(2,1)S(1)}, bf16[512,128]{1,0:T(8,128)(2,1)S(1)}, u32[]{:S(2)}, u32[]{:S(2)}) %collective-permute-start.5) | collective-permute-done | bytes 131104 | tf_op jit(solution)/shard_map/ppermute | solution.py:516
  28.8 0.5 %collective-permute-done.7.own_oth_ref = bf16[512,128]{1,0:T(8,128)(2,1)S(1)} collective-permute-done((bf16[512,128]{1,0:T(8,128)(2,1)S(1)}, bf16[512,128]{1,0:T(8,128)(2,1)S(1)}, u32[]{:S(2)}, u32[]{:S(2)}) %collective-permute-start.7) | collective-permute-done | bytes 131104 | tf_op jit(solution)/shard_map/ppermute | solution.py:448
  29.3 0.8 %collective-permute-done.6.near_oth_ref = bf16[512,128]{1,0:T(8,128)(2,1)S(1)} collective-permute-done((bf16[512,128]{1,0:T(8,128)(2,1)S(1)}, bf16[512,128]{1,0:T(8,128)(2,1)S(1)}, u32[]{:S(2)}, u32[]{:S(2)}) %collective-permute-start.6) | collective-permute-done | bytes 131104 | tf_op jit(solution)/shard_map/ppermute | solution.py:448
  30.1 1.1 %shard_map.213 = (bf16[128,512]{1,0:T(8,128)(2,1)S(1)}, bf16[128,512]{1,0:T(8,128)(2,1)}) custom-call(bf16[176,512]{1,0:T(8,128)(2,1)S(1)} %shard_map.209.own_ref.packed_ref, bf16[512,128]{1,0:T(8,128)(2,1)S(1)} %collective-permute-done.5.near_ref, bf16[512,128]{1,0:T(8,128)(2,1)S(1)} %collective-permute-done.6.near_oth_ref, ...), custom_call_target="tpu_custom_call" | custom-call | tf_op jit(solution)/shard_map/pallas_call | solution.py:46
  31.2 0.1 collective-permute-start.9
  31.4 6.0 %all-to-all-start.1 = ((bf16[8,16,512]{2,1,0:T(8,128)(2,1)}), bf16[8,16,512]{2,1,0:T(8,128)(2,1)S(1)}, u32[]{:S(2)}, u32[]{:S(2)}) async-start(bf16[8,16,512]{2,1,0:T(8,128)(2,1)} %bitcast.5), calls=%async_computation.1 | async-start | bytes 262144 | tf_op jit(solution)/shard_map/all_to_all | solution.py:541
  37.3 0.1 reshape.39.receivers_ref
  37.4 0.1 iota_subtract_fusion
  37.5 0.1 sub.29.limit_ref
  37.6 2.0 %shard_map.214 = (f32[128,512]{1,0:T(8,128)S(1)}, f32[128,512]{1,0:T(8,128)S(1)}, bf16[2048,256]{1,0:T(8,128)(2,1)S(1)}, bf16[2048,256]{1,0:T(8,128)(2,1)S(1)}) custom-call(bf16[128,512]{1,0:T(8,128)(2,1)S(1)} %get-tuple-element.36.mid_ref, s32[1,128]{1,0:T(1,128)S(1)} %reshape.39.receivers_ref, bf16[4,128]{1,0:T(4,128)(2,1)S(1)} %copy-done.1, ...), custom_call_target="tpu_custom_call" | custom-call | tf_op jit(solution)/shard_map/pallas_call | solution.py:46
  39.6 5.2 %all-to-all-done.1 = bf16[8,16,512]{2,1,0:T(8,128)(2,1)S(1)} async-done(((bf16[8,16,512]{2,1,0:T(8,128)(2,1)}), bf16[8,16,512]{2,1,0:T(8,128)(2,1)S(1)}, u32[]{:S(2)}, u32[]{:S(2)}) %all-to-all-start.1) | async-done | bytes 131104 | tf_op jit(solution)/shard_map/all_to_all | solution.py:541
  44.8 1.9 %shard_map.215 = bf16[128,256]{1,0:T(8,128)(2,1)} custom-call(bf16[128,512]{1,0:T(8,128)(2,1)S(1)} %bitcast.9, f32[128,512]{1,0:T(8,128)S(1)} %get-tuple-element.39.base_ref, f32[128,512]{1,0:T(8,128)S(1)} %get-tuple-element.40.upper_ref, bf16[128,512]{1,0:T(8,128)(2,1)S(1)} %get-tuple-element.36.mid_ref, s32[1,128]{1,0:T(1,128)S(1)} %reshape.39.receivers_ref, ...), custom_call_target="tpu_custom_call" | custom-call | tf_op jit(solution)/shard_map/pallas_call | solution.py:46
  (17 shorter events, 0.1 us)
Async XLA Ops:
  0.0 2.3 %collective-permute-start = (bf16[128,256]{1,0:T(8,128)(2,1)}, bf16[128,256]{1,0:T(8,128)(2,1)S(1)}, u32[]{:S(2)}, u32[]{:S(2)}) collective-permute-start(bf16[128,256]{1,0:T(8,128)(2,1)} %latent_hbm.1), channel_id=1, source_target_pairs={{0,1},{1,0},{2,3},{3,2},{4,5},{5,4},{6,7},{7,6},{8,9},{9,8},{10,11... | collective-permute-start | bytes 196616 | tf_op jit(solution)/shard_map/ppermute | solution.py:448
  2.3 10.1 %collective-permute-start.2 = (bf16[1264,256]{1,0:T(8,128)(2,1)S(1)}, bf16[1264,256]{1,0:T(8,128)(2,1)S(1)}, u32[]{:S(2)}, u32[]{:S(2)}) collective-permute-start(bf16[1264,256]{1,0:T(8,128)(2,1)S(1)} %get-tuple-element.27.own_ref), channel_id=1, source_target_pairs={{0,1},{1,0},{2,3},{3,2},{4,5},{5,4},{6,7},{7,6},{8,9},{9,8},{10,11... | collective-permute-start | bytes 1941512 | tf_op jit(solution)/shard_map/ppermute | solution.py:448
  2.4 13.9 %collective-permute-start.3 = (bf16[512,256]{1,0:T(8,128)(2,1)}, bf16[512,256]{1,0:T(8,128)(2,1)S(1)}, u32[]{:S(2)}, u32[]{:S(2)}) collective-permute-start(bf16[512,256]{1,0:T(8,128)(2,1)} %lr_own.1), channel_id=1, source_target_pairs={{0,1},{1,0},{2,3},{3,2},{4,5},{5,4},{6,7},{7,6},{8,9},{9,8},{10,11... | collective-permute-start | bytes 786440 | tf_op jit(solution)/shard_map/ppermute | solution.py:448
  2.9 13.4 %collective-permute-start.1 = (bf16[176,512]{1,0:T(8,128)(2,1)S(1)}, bf16[176,512]{1,0:T(8,128)(2,1)S(1)}, u32[]{:S(2)}, u32[]{:S(2)}) collective-permute-start(bf16[176,512]{1,0:T(8,128)(2,1)S(1)} %shard_map.209.own_ref.packed_ref), channel_id=1, source_target_pairs={{2,0},{4,2},{6,4},{8,6},{10,8},{12,10},{14,12},{1,3},{3,5},{5,7},{... | collective-permute-start | bytes 540680 | tf_op jit(solution)/shard_map/ppermute | solution.py:477
  4.2 12.1 %collective-permute-start.4 = (bf16[16,256]{1,0:T(8,128)(2,1)S(1)}, bf16[16,256]{1,0:T(8,128)(2,1)S(1)}, u32[]{:S(2)}, u32[]{:S(2)}) collective-permute-start(bf16[16,256]{1,0:T(8,128)(2,1)S(1)} %get-tuple-element.32.le_own.edge_own), channel_id=1, source_target_pairs={{0,1},{1,0},{2,3},{3,2},{4,5},{5,4},{6,7},{7,6},{8,9},{9,8},{10,11... | collective-permute-start | bytes 24584 | tf_op jit(solution)/shard_map/ppermute | solution.py:448
  7.6 21.2 %all-to-all-start = ((bf16[8,16,512]{2,1,0:T(8,128)(2,1)}), bf16[8,16,512]{2,1,0:T(8,128)(2,1)S(1)}, u32[]{:S(2)}, u32[]{:S(2)}) async-start(bf16[8,16,512]{2,1,0:T(8,128)(2,1)} %bitcast.12), calls=%async_computation | async-start | bytes 262144 | tf_op jit(solution)/shard_map/all_to_all | solution.py:481
  12.5 3.9 %copy-start.3 = (bf16[512,256]{1,0:T(8,128)(2,1)S(1)}, bf16[512,256]{1,0:T(8,128)(2,1)}, u32[]{:S(2)}) copy-start(bf16[512,256]{1,0:T(8,128)(2,1)} %lr_own.1) | copy-start | bytes 786436
  16.3 8.9 %copy-start = (bf16[256,512]{1,0:T(8,128)(2,1)S(1)}, bf16[256,512]{1,0:T(8,128)(2,1)}, u32[]{:S(2)}) copy-start(bf16[256,512]{1,0:T(8,128)(2,1)} %lo_own.1) | copy-start | bytes 786436
  21.1 10.1 %copy-start.4 = (bf16[3072,256]{1,0:T(8,128)(2,1)S(1)}, bf16[3072,256]{1,0:T(8,128)(2,1)}, u32[]{:S(2)}) copy-start(bf16[3072,256]{1,0:T(8,128)(2,1)} %get-tuple-element.38.own_hbm) | copy-start | bytes 4718596
  21.1 7.6 %collective-permute-start.5 = (bf16[512,128]{1,0:T(8,128)(2,1)S(1)}, bf16[512,128]{1,0:T(8,128)(2,1)S(1)}, u32[]{:S(2)}, u32[]{:S(2)}) collective-permute-start(bf16[512,128]{1,0:T(8,128)(2,1)S(1)} %shard_map.211.near_ref), channel_id=1, source_target_pairs={{0,2},{2,4},{4,6},{6,8},{8,10},{10,12},{12,14},{3,1},{5,3},{7,5},{... | collective-permute-start | bytes 393224 | tf_op jit(solution)/shard_map/ppermute | solution.py:516
  25.2 4.9 %collective-permute-start.8 = (bf16[256,512]{1,0:T(8,128)(2,1)S(1)}, bf16[256,512]{1,0:T(8,128)(2,1)S(1)}, u32[]{:S(2)}, u32[]{:S(2)}) collective-permute-start(bf16[256,512]{1,0:T(8,128)(2,1)S(1)} %copy-done), channel_id=1, source_target_pairs={{0,1},{1,0},{2,3},{3,2},{4,5},{5,4},{6,7},{7,6},{8,9},{9,8},{10,11... | collective-permute-start | bytes 786440 | tf_op jit(solution)/shard_map/ppermute | solution.py:448
  27.7 9.7 %copy-start.5 = (s32[8,16]{1,0:T(8,128)S(1)}, s32[8,16]{1,0:T(8,128)}, u32[]{:S(2)}) copy-start(s32[8,16]{1,0:T(8,128)} %param.28) | copy-start | bytes 1540
  27.7 9.7 %copy-start.6 = (s32[1,8]{1,0:T(1,128)S(1)}, s32[1,8]{1,0:T(1,128)}, u32[]{:S(2)}) copy-start(s32[1,8]{1,0:T(1,128)} %param.29) | copy-start | bytes 100
  27.7 9.9 %copy-start.1 = (bf16[4,128]{1,0:T(4,128)(2,1)S(1)}, bf16[4,128]{1,0:T(4,128)(2,1)}, u32[]{:S(2)}) copy-start(bf16[4,128]{1,0:T(4,128)(2,1)} %feats_ref.1) | copy-start | bytes 3076
  27.7 1.5 %collective-permute-start.7 = (bf16[512,128]{1,0:T(8,128)(2,1)S(1)}, bf16[512,128]{1,0:T(8,128)(2,1)S(1)}, u32[]{:S(2)}, u32[]{:S(2)}) collective-permute-start(bf16[512,128]{1,0:T(8,128)(2,1)S(1)} %shard_map.212.own_ref), channel_id=1, source_target_pairs={{0,1},{1,0},{2,3},{3,2},{4,5},{5,4},{6,7},{7,6},{8,9},{9,8},{10,11... | collective-permute-start | bytes 393224 | tf_op jit(solution)/shard_map/ppermute | solution.py:448
  28.8 1.3 %collective-permute-start.6 = (bf16[512,128]{1,0:T(8,128)(2,1)S(1)}, bf16[512,128]{1,0:T(8,128)(2,1)S(1)}, u32[]{:S(2)}, u32[]{:S(2)}) collective-permute-start(bf16[512,128]{1,0:T(8,128)(2,1)S(1)} %collective-permute-done.5.near_ref), channel_id=1, source_target_pairs={{0,1},{1,0},{2,3},{3,2},{4,5},{5,4},{6,7},{7,6},{8,9},{9,8},{10,11... | collective-permute-start | bytes 393224 | tf_op jit(solution)/shard_map/ppermute | solution.py:448
  31.2 6.4 %collective-permute-start.9 = (bf16[3072,256]{1,0:T(8,128)(2,1)S(1)}, bf16[3072,256]{1,0:T(8,128)(2,1)}, u32[]{:S(2)}, u32[]{:S(2)}) collective-permute-start(bf16[3072,256]{1,0:T(8,128)(2,1)S(1)} %copy-done.4), channel_id=1, source_target_pairs={{0,1},{1,0},{2,3},{3,2},{4,5},{5,4},{6,7},{7,6},{8,9},{9,8},{10,11... | collective-permute-start | bytes 4718600 | tf_op jit(solution)/shard_map/ppermute | solution.py:448
  31.4 13.4 %all-to-all-start.1 = ((bf16[8,16,512]{2,1,0:T(8,128)(2,1)}), bf16[8,16,512]{2,1,0:T(8,128)(2,1)S(1)}, u32[]{:S(2)}, u32[]{:S(2)}) async-start(bf16[8,16,512]{2,1,0:T(8,128)(2,1)} %bitcast.5), calls=%async_computation.1 | async-start | bytes 262144 | tf_op jit(solution)/shard_map/all_to_all | solution.py:541
  37.6 7.2 %copy-start.2 = (f32[256]{0:T(256)S(1)}, f32[256]{0:T(256)}, u32[]{:S(2)}) copy-start(f32[256]{0:T(256)} %param.43) | copy-start | bytes 3076
